TPU v7x, 32 devices: a whole 2x2x4 slice. The times are simulated.
32 devices in a mesh: hx: 4 (over y, core), hy: 8 (over z, x).
Axes of the slice: x: 2, y: 2, z: 4, core: 2. Of those that a mesh axis runs over, the one named last changes fastest.
Arguments:
- embeddings: bfloat16 [16384, 768], P(('hx', 'hy')), may hold values from -60 to 60
- bucket: int32 [16384], P(('hx', 'hy')), may hold values from 0 to 63, as said below
Outputs:
- smoothed: bfloat16 [16384, 768], P(('hx', 'hy'))
Inputs may be any that keep to these rules, and one draw needn't show every extreme that they name: Every bucket holds at most 512 files and some bucket holds exactly 512; buckets may be empty. The files of each bucket, and of each owner's 2 buckets taken together, lie on the devices as evenly as can be (counts on two devices differ by at most one), so that no device holds more than 32 files of one owner's buckets, and some owner's buckets give exactly 32 to every device.
All inputs are finite; a program needn't handle non-finite values.
Results may differ from a plain program's by a relative error of at most 0.0042.
Values may be sent and summed in bfloat16 or wider, within the bound.
No kernel may reach another device: no remote copies, remote signals or barrier semaphores. Data moves between devices by JAX's collectives and lax.ppermute only.
A program may use at most 64 MiB of HBM per device.

v0:
```python
import jax
import jax.numpy as jnp
from jax import lax
from jax.sharding import PartitionSpec as P

BPD = 2
CAP = 512


sharpness = 32.0
epsilon = 1e-06


def swapped(value, axis, apart):
    return lax.ppermute(value, axis, [(i, i ^ 1 << apart) for i in range(lax.axis_size(axis))])


def inverse_norm(rows):
    return 1.0 / jnp.sqrt(jnp.mean(jnp.square(rows.astype(jnp.float32)), axis=-1) + epsilon)


def rank_within(labels, groups):
    total_rows = labels.shape[0]
    block_rows = min(128, total_rows)
    block_count = total_rows // block_rows
    onehot = (labels[:, None] == jnp.arange(groups, dtype=jnp.int32)[None, :]).astype(jnp.bfloat16)
    stacked = onehot.reshape(block_count, block_rows, groups)
    lower = (jnp.arange(block_rows)[:, None] > jnp.arange(block_rows)[None, :]).astype(jnp.bfloat16)
    within = jnp.einsum("ij,bjn->bin", lower, stacked, preferred_element_type=jnp.float32)
    stacked_wide = stacked.astype(jnp.float32)
    totals = jnp.sum(stacked_wide, axis=1)
    offsets = jnp.cumsum(totals, axis=0) - totals
    before = within + offsets[:, None, :]
    rank_rows = jnp.sum(before * stacked_wide, axis=2).reshape(total_rows)
    return (rank_rows.astype(jnp.int32), jnp.sum(totals, axis=0).astype(jnp.int32))


def place_matrix(target, total):
    return (jnp.arange(total, dtype=jnp.int32)[:, None] == target[None, :]).astype(jnp.bfloat16)


def pick_back(matrix, values):
    return lax.dot_general(
        matrix, values, (((0,), (0,)), ((), ())), preferred_element_type=jnp.float32
    ).astype(jnp.bfloat16)


def body(embeddings, bucket):
    count_hx = lax.axis_size("hx")
    count_hy = lax.axis_size("hy")
    device_count = count_hx * count_hy
    feature_width = embeddings.shape[1]
    slot_size = BPD * CAP // device_count
    send_total = device_count * slot_size
    owner_dev = bucket // BPD
    local_slot = bucket % BPD
    slot_of, unused_counts = rank_within(owner_dev, device_count)
    send_match = place_matrix(owner_dev * slot_size + slot_of, send_total)
    send_flat = jnp.dot(send_match, embeddings, preferred_element_type=jnp.float32).astype(
        jnp.bfloat16
    )
    slot_tag = (local_slot + 1).astype(jnp.bfloat16)[:, None]
    send_tag = jnp.dot(send_match, slot_tag, preferred_element_type=jnp.float32)[:, 0]
    send_ids = send_tag.astype(jnp.int32) - 1
    got_rows, got_ids = (
        lax.all_to_all(
            send_flat.reshape(device_count, slot_size, feature_width),
            ("hx", "hy"),
            split_axis=0,
            concat_axis=0,
            tiled=True,
        ),
        lax.all_to_all(
            send_ids.reshape(device_count, slot_size),
            ("hx", "hy"),
            split_axis=0,
            concat_axis=0,
            tiled=True,
        ),
    )
    recv_total = device_count * slot_size
    recv_rows = got_rows.reshape(recv_total, feature_width)
    recv_ids = got_ids.reshape(recv_total)
    valid_row = recv_ids >= 0
    target_bucket = jnp.where(valid_row, recv_ids, BPD)
    rank_in, group_counts = rank_within(target_bucket, BPD + 1)
    own_counts = group_counts[:BPD]
    own_match = place_matrix(target_bucket * CAP + rank_in, BPD * CAP)
    own_blocks = (
        jnp.dot(own_match, recv_rows, preferred_element_type=jnp.float32)
        .astype(jnp.bfloat16)
        .reshape(BPD, CAP, feature_width)
    )
    hx_blocks, hx_counts = swapped((own_blocks, own_counts), "hx", count_hx.bit_length() - 2)
    hy_blocks, hy_counts = swapped((own_blocks, own_counts), "hy", count_hy.bit_length() - 2)
    own_inv = inverse_norm(own_blocks)
    hx_inv = inverse_norm(hx_blocks)
    hy_inv = inverse_norm(hy_blocks)
    query_block = min(512, CAP)
    column_index = jnp.arange(CAP, dtype=jnp.int32)
    factor = sharpness / feature_width
    out_list = []
    for which in range(BPD):
        other = which ^ 1
        key_sets = [
            (own_blocks[which], own_inv[which], own_counts[which], True),
            (own_blocks[other], own_inv[other], own_counts[other], False),
            (hx_blocks[which], hx_inv[which], hx_counts[which], False),
            (hy_blocks[which], hy_inv[which], hy_counts[which], False),
        ]
        query_rows = own_blocks[which, 0:query_block]
        query_inv = own_inv[which, 0:query_block]
        row_index = 0 + jnp.arange(query_block, dtype=jnp.int32)
        numerator = jnp.zeros((query_block, feature_width), jnp.float32)
        denominator = jnp.ones((query_block,), jnp.float32)
        for key_rows, key_inv, key_count, is_own in key_sets:
            products = lax.dot_general(
                query_rows, key_rows, (((1,), (1,)), ((), ())), preferred_element_type=jnp.float32
            )
            score = products * query_inv[:, None] * key_inv[None, :] * factor
            live = jnp.broadcast_to((column_index < key_count)[None, :], score.shape)
            if is_own:
                live = live & (row_index[:, None] != column_index[None, :])
            kernel = jnp.where(live, jnp.exp(score), jnp.float32(0.0))
            denominator = denominator + jnp.sum(kernel, axis=1)
            numerator = numerator + jnp.dot(
                kernel.astype(jnp.bfloat16), key_rows, preferred_element_type=jnp.float32
            )
        pieces = (numerator / denominator[:, None]).astype(jnp.bfloat16)
        out_list.append(pieces)
    out_flat = jnp.concatenate(out_list, axis=0)
    back_rows = pick_back(own_match, out_flat)
    home_rows = lax.all_to_all(
        back_rows.reshape(device_count, slot_size, feature_width),
        ("hx", "hy"),
        split_axis=0,
        concat_axis=0,
        tiled=True,
    )
    home_flat = home_rows.reshape(send_total, feature_width)
    return pick_back(send_match, home_flat)


def solution(mesh):
    return jax.shard_map(
        body,
        mesh=mesh,
        in_specs=(P(("hx", "hy"), None), P(("hx", "hy"))),
        out_specs=P(("hx", "hy"), None),
        check_vma=False,
    )
```

profile of v0, /device:TPU:0, one launch (start us, length us, event | category | flops | bytes accessed | tf_op | source)
XLA Modules:
  0.0 187.6 jit_solution(2052902563297148260)
XLA Ops:
  0.0 0.8 fusion.104
  1.1 0.7 bitcast_add_fusion
  2.3 0.7 sub.29
  3.0 7.3 %all-to-all-start = ((s32[32,1,32]{2,1,0:T(1,128)}), s32[32,1,32]{2,1,0:T(1,128)S(1)}, u32[]{:S(2)}, u32[]{:S(2)}) async-start(s32[32,1,32]{2,1,0:T(1,128)} %sub.29), calls=%async_computation | async-start | bytes 32768 | tf_op jit(solution)/shard_map/all_to_all | solution.py:73
  10.3 2.2 %fusion.7 = bf16[1024,768]{1,0:T(8,128)(2,1)} fusion(bf16[512,768]{1,0:T(8,128)(2,1)S(1)} %copy-done, s32[512]{0:T(512)S(1)} %get-tuple-element.13), kind=kOutput, calls=%fused_computation.12 | convolution fusion | flops 806617088 | bytes 2361344 | tf_op jit(solution)/shard_map/dot_general | solution.py:59
  12.5 4.8 %all-to-all-done = s32[32,1,32]{2,1,0:T(1,128)S(1)} async-done(((s32[32,1,32]{2,1,0:T(1,128)}), s32[32,1,32]{2,1,0:T(1,128)S(1)}, u32[]{:S(2)}, u32[]{:S(2)}) %all-to-all-start) | async-done | bytes 4128 | tf_op jit(solution)/shard_map/all_to_all | solution.py:73
  17.3 2.7 %all-to-all-start.1 = ((bf16[32,32,768]{2,1,0:T(8,128)(2,1)}), bf16[32,32,768]{2,1,0:T(8,128)(2,1)S(1)}, u32[]{:S(2)}, u32[]{:S(2)}) async-start(bf16[32,32,768]{2,1,0:T(8,128)(2,1)} %bitcast.79), calls=%async_computation.1 | async-start | bytes 3145728 | tf_op jit(solution)/shard_map/all_to_all | solution.py:66
  20.2 2.7 %collective-permute-start.2 = (s32[2]{0:T(128)S(1)}, s32[2]{0:T(128)S(1)}, u32[]{:S(2)}, u32[]{:S(2)}) collective-permute-start(s32[2]{0:T(128)S(1)} %bitcast.84), channel_id=1, source_target_pairs={{0,4},{1,5},{2,6},{3,7},{4,0},{5,1},{6,2},{7,3},{8,12},{9,13},{10,... | collective-permute-start | bytes 32 | tf_op jit(solution)/shard_map/ppermute | solution.py:15
  22.9 1.5 collective-permute-start
  25.1 0.7 reduce.7
  27.1 0.7 iota_compare_fusion.26
  27.9 29.6 %collective-permute-done.2 = s32[2]{0:T(128)S(1)} collective-permute-done((s32[2]{0:T(128)S(1)}, s32[2]{0:T(128)S(1)}, u32[]{:S(2)}, u32[]{:S(2)}) %collective-permute-start.2) | collective-permute-done | bytes 40 | tf_op jit(solution)/shard_map/ppermute | solution.py:15
  57.5 0.7 fusion.108
  58.1 0.6 iota_compare_fusion.23
  61.3 2.0 %multiply_reduce_fusion.2 = (f32[1024]{0:T(1024)S(1)}, bf16[1024,768]{1,0:T(8,128)(2,1)S(1)}) fusion(bf16[1024,768]{1,0:T(8,128)(2,1)S(1)} %bitcast.78, s32[1024]{0:T(1024)S(1)} %fusion.95), kind=kOutput, calls=%fused_computation.5 | convolution fusion | flops 1614806016 | bytes 3153920 | tf_op jit(solution)/shard_map/dot_general | solution.py:90
  63.4 1.6 collective-permute-start.1
  65.0 0.8 fusion.113
  65.7 0.7 fusion.111
  66.5 0.8 fusion.114
  67.9 0.8 fusion.112
  70.5 62.1 %collective-permute-done.3 = bf16[2,512,768]{2,1,0:T(8,128)(2,1)S(1)} collective-permute-done((bf16[2,512,768]{2,1,0:T(8,128)(2,1)S(1)}, bf16[2,512,768]{2,1,0:T(8,128)(2,1)S(1)}, u32[]{:S(2)}, u32[]{:S(2)}) %collective-permute-start.3) | collective-permute-done | bytes 1572896 | tf_op jit(solution)/shard_map/ppermute | solution.py:15
  133.4 0.8 select_reduce_fusion.2
  134.2 0.7 select_reduce_fusion.3
  134.9 0.8 select_reduce_fusion
  135.7 0.8 select_reduce_fusion.1
  136.5 0.7 fusion.53
  137.2 0.7 fusion.55
  137.9 0.8 divide_convert_fusion.1
  138.7 1.1 divide_convert_fusion
  139.8 2.3 %fusion.9 = bf16[1024,768]{1,0:T(8,128)(2,1)S(1)} fusion(s32[1024]{0:T(1024)S(1)} %fusion.95, bf16[512,768]{1,0:T(8,128)(2,1)S(1)} %divide_convert_fusion, bf16[512,768]{1,0:T(8,128)(2,1)S(1)} %divide_convert_fusion.1), kind=kOutput, calls=%fused_computation.14 | convolution fusion | flops 1615593472 | bytes 3149824 | tf_op jit(solution)/shard_map/dot_general | solution.py:43
  142.1 43.4 %all_to_all.16 = bf16[32,32,768]{2,1,0:T(8,128)(2,1)S(1)} all-to-all(bf16[32,32,768]{2,1,0:T(8,128)(2,1)S(1)} %bitcast.80), channel_id=1, replica_groups=mesh['hx'=4,'hy'=8] {'hx','hy'}, dimensions={0} | all-to-all | bytes 3145728 | tf_op jit(solution)/shard_map/all_to_all | solution.py:133
  185.5 2.1 %fusion.13 = bf16[512,768]{1,0:T(8,128)(2,1)} fusion(bf16[1024,768]{1,0:T(8,128)(2,1)S(1)} %bitcast.81, s32[512]{0:T(512)S(1)} %get-tuple-element.13), kind=kOutput, calls=%fused_computation.20 | convolution fusion | flops 806223872 | bytes 2361344 | tf_op jit(solution)/shard_map/dot_general | solution.py:43
  (43 shorter events, 8.9 us)
Async XLA Ops:
  0.0 10.3 %copy-start = (bf16[512,768]{1,0:T(8,128)(2,1)S(1)}, bf16[512,768]{1,0:T(8,128)(2,1)}, u32[]{:S(2)}) copy-start(bf16[512,768]{1,0:T(8,128)(2,1)} %param.2) | copy-start | bytes 2359300
  3.0 14.3 %all-to-all-start = ((s32[32,1,32]{2,1,0:T(1,128)}), s32[32,1,32]{2,1,0:T(1,128)S(1)}, u32[]{:S(2)}, u32[]{:S(2)}) async-start(s32[32,1,32]{2,1,0:T(1,128)} %sub.29), calls=%async_computation | async-start | bytes 32768 | tf_op jit(solution)/shard_map/all_to_all | solution.py:73
  17.3 44.0 %all-to-all-start.1 = ((bf16[32,32,768]{2,1,0:T(8,128)(2,1)}), bf16[32,32,768]{2,1,0:T(8,128)(2,1)S(1)}, u32[]{:S(2)}, u32[]{:S(2)}) async-start(bf16[32,32,768]{2,1,0:T(8,128)(2,1)} %bitcast.79), calls=%async_computation.1 | async-start | bytes 3145728 | tf_op jit(solution)/shard_map/all_to_all | solution.py:66
  20.2 37.2 %collective-permute-start.2 = (s32[2]{0:T(128)S(1)}, s32[2]{0:T(128)S(1)}, u32[]{:S(2)}, u32[]{:S(2)}) collective-permute-start(s32[2]{0:T(128)S(1)} %bitcast.84), channel_id=1, source_target_pairs={{0,4},{1,5},{2,6},{3,7},{4,0},{5,1},{6,2},{7,3},{8,12},{9,13},{10,... | collective-permute-start | bytes 32 | tf_op jit(solution)/shard_map/ppermute | solution.py:15
  22.9 35.8 %collective-permute-start = (s32[2]{0:T(128)S(1)}, s32[2]{0:T(128)S(1)}, u32[]{:S(2)}, u32[]{:S(2)}) collective-permute-start(s32[2]{0:T(128)S(1)} %bitcast.85), channel_id=1, source_target_pairs={{0,16},{8,24},{16,0},{24,8},{1,17},{9,25},{17,1},{25,9},{2,18},{10... | collective-permute-start | bytes 32 | tf_op jit(solution)/shard_map/ppermute | solution.py:15
  63.3 69.3 %collective-permute-start.3 = (bf16[2,512,768]{2,1,0:T(8,128)(2,1)S(1)}, bf16[2,512,768]{2,1,0:T(8,128)(2,1)S(1)}, u32[]{:S(2)}, u32[]{:S(2)}) collective-permute-start(bf16[2,512,768]{2,1,0:T(8,128)(2,1)S(1)} %bitcast.76), channel_id=1, source_target_pairs={{0,4},{1,5},{2,6},{3,7},{4,0},{5,1},{6,2},{7,3},{8,12},{9,13},{10,... | collective-permute-start | bytes 4718600 | tf_op jit(solution)/shard_map/ppermute | solution.py:15
  63.4 69.6 %collective-permute-start.1 = (bf16[2,512,768]{2,1,0:T(8,128)(2,1)S(1)}, bf16[2,512,768]{2,1,0:T(8,128)(2,1)S(1)}, u32[]{:S(2)}, u32[]{:S(2)}) collective-permute-start(bf16[2,512,768]{2,1,0:T(8,128)(2,1)S(1)} %bitcast.77), channel_id=1, source_target_pairs={{0,16},{8,24},{16,0},{24,8},{1,17},{9,25},{17,1},{25,9},{2,18},{10... | collective-permute-start | bytes 4718600 | tf_op jit(solution)/shard_map/ppermute | solution.py:15
where the time goes:
time: 188 us
  waiting for transfers between devices  96.5 us (51%)
  blocking collectives  43.4 us (23%)
  matrix products  21.2 us (11%)
  starting transfers between devices  15.8 us (8%)
  other arithmetic  7.23 us (4%)
  local copies, waits for them, and re-layouts  3.25 us (2%)
    ppermute x4, waiting for transfers between devices, swapped(): lax.ppermute(value, axis, [(i, i ^ 1 << apart) for i in range(lax.axis_si...  91.7 us
    all_to_all x1, blocking collectives, body(): lax.all_to_all(back_rows.reshape(device_count, slot_size, feature_width),...  43.4 us
    all_to_all x1, starting transfers between devices, body(): lax.all_to_all(send_ids.reshape(device_count, slot_size), ('hx', 'hy'), s...  7.3 us
    dot_general x8, matrix products, body(): lax.dot_general(query_rows, key_rows, (((1,), (1,)), ((), ())), preferred...  6.11 us
    ppermute x4, starting transfers between devices, swapped(): lax.ppermute(value, axis, [(i, i ^ 1 << apart) for i in range(lax.axis_si...  5.84 us
    dot_general x8, matrix products, body(): jnp.dot(kernel.astype(jnp.bfloat16), key_rows, preferred_element_type=jnp...  5.71 us
    all_to_all x1, waiting for transfers between devices, body(): lax.all_to_all(send_ids.reshape(device_count, slot_size), ('hx', 'hy'), s...  4.84 us
    dot_general x2, matrix products, pick_back(): lax.dot_general(matrix, values, (((0,), (0,)), ((), ())), preferred_eleme...  4.39 us
  transfers between devices with their start and end apart: 6, of which 3 were waited for; matrix products, arithmetic and copies ran while one was open for 8% of the time, Pallas kernels for 0%

commit v1 on v0

v1 whole, which is shorter than its diff:
```python
import jax
import jax.numpy as jnp
from jax import lax
from jax.sharding import PartitionSpec as P

BPD = 2
CAP = 512
META = 16

sharpness = 32.0
epsilon = 1e-06

AXES = ("hx", "hy")


def swapped(value, bit, total):
    return lax.ppermute(value, AXES, [(i, i ^ bit) for i in range(total)])


def exchange(value, groups):
    return lax.all_to_all(
        value, AXES, split_axis=0, concat_axis=0, tiled=True, axis_index_groups=groups
    )


def match_of(target, total):
    return jnp.arange(total, dtype=jnp.int32)[:, None] == target[None, :]


def pick(match, rows):
    return jnp.dot(match, rows, preferred_element_type=jnp.float32).astype(jnp.bfloat16)


def attend(queries, query_inv, query_bits, keys, key_inv, key_bit, factor, exclude_self):
    products = lax.dot_general(
        queries, keys, (((1,), (1,)), ((), ())), preferred_element_type=jnp.float32
    )
    score = products * query_inv[:, None] * key_inv[None, :] * factor
    live = (query_bits[:, None] & key_bit[None, :]) != 0
    if exclude_self:
        row = jnp.arange(queries.shape[0], dtype=jnp.int32)
        live = live & (row[:, None] != row[None, :])
    kernel = jnp.where(live, jnp.exp(score), jnp.float32(0.0))
    numerator = jnp.dot(kernel.astype(jnp.bfloat16), keys, preferred_element_type=jnp.float32)
    return numerator, jnp.sum(kernel, axis=1)


def key_facts(meta):
    wide = meta.astype(jnp.float32)
    tag = wide[:, 0].astype(jnp.int32)
    inv = wide[:, 1] + wide[:, 2] + wide[:, 3]
    bit = jnp.where(tag > 0, jnp.left_shift(1, jnp.maximum(tag - 1, 0)), 0)
    return tag, inv, bit


def body(embeddings, bucket):
    nx, ny = lax.axis_size("hx"), lax.axis_size("hy")
    devices = nx * ny
    cells = devices // 4
    files, width = embeddings.shape
    slots = 4 * BPD * CAP // devices
    slots_a = max(16, slots * 3 // 4 // 16 * 16)
    slots_b = slots - slots_a
    stride = slots // slots_b
    files_a = files - files // stride
    core_bit, half_bit = ny, ny // 2
    groups = [
        [(2 * u + core) * ny + half * (ny // 2) + v for u in range(nx // 2) for v in range(ny // 2)]
        for core in range(2)
        for half in range(2)
    ]

    a, b, c = bucket // (BPD * ny), bucket // BPD % ny, bucket % BPD
    cell = a % (nx // 2) * (ny // 2) + b % (ny // 2)
    tag = a // (nx // 2) * 4 + b // (ny // 2) * 2 + c
    order = cell * files + jnp.arange(files, dtype=jnp.int32)
    rank = jnp.sum((order[:, None] < order[None, :]).astype(jnp.int32), axis=0)
    start = jnp.sum((cell[:, None] < cell[None, :]).astype(jnp.int32), axis=0)
    late = rank % stride == stride - 1
    late_rank, late_start = rank // stride, start // stride
    early_index = (rank - late_rank) - (start - late_start)
    slot = cell * slots + jnp.where(late, slots_a + late_rank - late_start, early_index)

    early_match = match_of(jnp.where(late, files, rank - late_rank), files_a)
    early_rows = pick(early_match.astype(jnp.bfloat16), embeddings)
    early_slot = jnp.sum(
        jnp.where(early_match, (cell * slots_a + early_index)[None, :], 0), axis=1
    )
    other_early = swapped(early_rows, half_bit, devices)
    other_slot = swapped(early_slot, half_bit, devices)

    squares = jnp.square(embeddings.astype(jnp.float32))
    inv = 1.0 / jnp.sqrt(jnp.mean(squares, axis=-1) + epsilon)
    high = lax.reduce_precision(inv, 8, 7)
    middle = lax.reduce_precision(inv - high, 8, 7)
    low = inv - high - middle
    facts = jnp.stack([(tag + 1).astype(jnp.float32), high, middle, low]).astype(jnp.bfloat16)
    facts = jnp.pad(facts, ((0, META - 4), (0, 0)))
    send_match = match_of(slot, cells * slots).astype(jnp.bfloat16)
    send_rows = pick(send_match, embeddings).reshape(cells, slots, width)
    send_meta = lax.dot_general(
        facts, send_match, (((1,), (1,)), ((), ())), preferred_element_type=jnp.float32
    ).astype(jnp.bfloat16)
    send_meta = send_meta.reshape(META, cells, slots).transpose(1, 0, 2)
    send_meta = jnp.pad(send_meta, ((0, 0), (0, 0), (0, width - slots)))
    got = exchange(jnp.concatenate([send_rows, send_meta], axis=1), groups)
    own_rows = got[:, :slots].reshape(cells * slots, width)
    own_meta = got[:, slots:, :slots]

    half_late = swapped(got[:, slots_a:slots], half_bit, devices).reshape(cells * slots_b, width)
    half_meta = swapped(own_meta, half_bit, devices)

    other_match = match_of(other_slot, cells * slots_a).astype(jnp.bfloat16)
    half_early = exchange(
        pick(other_match, other_early).reshape(cells, slots_a, width), groups
    ).reshape(cells * slots_a, width)

    mate_rows = swapped(own_rows, core_bit, devices)
    mate_meta, mate_half_meta = (
        swapped(own_meta, core_bit, devices),
        swapped(half_meta, core_bit, devices),
    )
    mate_late = swapped(half_late, core_bit, devices)
    mate_early = swapped(half_early, core_bit, devices)

    own_tag, own_inv, own_bit = key_facts(own_meta)
    query_tag = jnp.maximum(own_tag - 1, 0)
    query_bits = (
        jnp.left_shift(1, query_tag)
        | jnp.left_shift(1, query_tag ^ 1)
        | jnp.left_shift(1, query_tag ^ 2)
        | jnp.left_shift(1, query_tag ^ 4)
    )
    query_inv, query_bits = own_inv.reshape(-1), query_bits.reshape(-1)
    key_sets = [(own_rows, own_inv, own_bit, True)]
    _, mate_inv, mate_bit = key_facts(mate_meta)
    key_sets.append((mate_rows, mate_inv, mate_bit, False))
    for meta, early, late_rows in (
        (half_meta, half_early, half_late),
        (mate_half_meta, mate_early, mate_late),
    ):
        _, one_inv, one_bit = key_facts(meta)
        key_sets.append((late_rows, one_inv[:, slots_a:], one_bit[:, slots_a:], False))
        key_sets.append((early, one_inv[:, :slots_a], one_bit[:, :slots_a], False))
    factor = sharpness / width
    numerator = jnp.zeros((cells * slots, width), jnp.float32)
    denominator = jnp.ones((cells * slots,), jnp.float32)
    for keys, key_inv, key_bit, is_own in key_sets:
        one_numerator, one_denominator = attend(
            own_rows, query_inv, query_bits, keys, key_inv.reshape(-1), key_bit.reshape(-1), factor, is_own
        )
        numerator, denominator = numerator + one_numerator, denominator + one_denominator
    smoothed = (numerator / denominator[:, None]).astype(jnp.bfloat16)
    home = exchange(smoothed.reshape(cells, slots, width), groups).reshape(cells * slots, width)
    return lax.dot_general(
        send_match, home, (((0,), (0,)), ((), ())), preferred_element_type=jnp.float32
    ).astype(jnp.bfloat16)


def solution(mesh):
    return jax.shard_map(
        body,
        mesh=mesh,
        in_specs=(P(("hx", "hy"), None), P(("hx", "hy"))),
        out_specs=P(("hx", "hy"), None),
        check_vma=False,
    )
```

time: 188 us -> 154 us (0.82)
  waiting for transfers between devices: 96.5 us -> 68 us
  blocking collectives: 43.4 us -> 24.4 us
  matrix products: 21.2 us -> 39.3 us
  other arithmetic: 7.23 us -> 2.91 us
    ppermute x4 -> x9, waiting for transfers between devices: 91.7 us -> 30.9 us  [swapped(): return lax.ppermute(value, AXES, [(i, i ^ bit) for i in range(total)])]
    all_to_all x2, waiting for transfers between devices: 4.85 us -> 37.1 us  [exchange(): lax.all_to_all(value, AXES, split_axis=0, concat_axis=0, tiled=True, axis...]
    all_to_all x1, blocking collectives: 43.4 us -> 24.4 us  [exchange(): lax.all_to_all(value, AXES, split_axis=0, concat_axis=0, tiled=True, axis...]
    dot_general x23 -> x17, matrix products: 21.2 us -> 39.3 us  [the longest x6 17 us: attend(): jnp.dot(kernel.astype(jnp.bfloat16), keys, preferred_element_type=jnp.flo...]
    lt x6 -> x0, other arithmetic: 3.81 us -> none  [body(): live = jnp.broadcast_to((column_index < key_count)[None, :], score.shape)]
    ppermute x4 -> x9, starting transfers between devices: 5.84 us -> 9.06 us  [swapped(): return lax.ppermute(value, AXES, [(i, i ^ bit) for i in range(total)])]
    all_to_all x2, starting transfers between devices: 9.98 us -> 8.03 us  [exchange(): lax.all_to_all(value, AXES, split_axis=0, concat_axis=0, tiled=True, axis...]
  transfers between devices with their start and end apart: 6 -> 11, of which waited for: 3 -> 5; matrix products, arithmetic and copies ran while one was open for 8% -> 17% of each run, Pallas kernels for 0% -> 0%
where the time goes in v1:
time: 154 us
  waiting for transfers between devices  68 us (44%)
  matrix products  39.3 us (26%)
  blocking collectives  24.4 us (16%)
  starting transfers between devices  17.1 us (11%)
  other arithmetic  2.91 us (2%)
  local copies, waits for them, and re-layouts  1.79 us (1%)
    all_to_all x2, waiting for transfers between devices, exchange(): lax.all_to_all(value, AXES, split_axis=0, concat_axis=0, tiled=True, axis...  37.1 us
    ppermute x9, waiting for transfers between devices, swapped(): return lax.ppermute(value, AXES, [(i, i ^ bit) for i in range(total)])  30.9 us
    all_to_all x1, blocking collectives, exchange(): lax.all_to_all(value, AXES, split_axis=0, concat_axis=0, tiled=True, axis...  24.4 us
    dot_general x6, matrix products, attend(): jnp.dot(kernel.astype(jnp.bfloat16), keys, preferred_element_type=jnp.flo...  17 us
    dot_general x6, matrix products, attend(): lax.dot_general(queries, keys, (((1,), (1,)), ((), ())), preferred_elemen...  15.3 us
    ppermute x9, starting transfers between devices, swapped(): return lax.ppermute(value, AXES, [(i, i ^ bit) for i in range(total)])  9.06 us
    all_to_all x2, starting transfers between devices, exchange(): lax.all_to_all(value, AXES, split_axis=0, concat_axis=0, tiled=True, axis...  8.03 us
    dot_general x3, matrix products, pick(): jnp.dot(match, rows, preferred_element_type=jnp.float32)  4.5 us
  transfers between devices with their start and end apart: 11, of which 5 were waited for; matrix products, arithmetic and copies ran while one was open for 17% of the time, Pallas kernels for 0%

profile of v1, /device:TPU:0, one launch (start us, length us, event | category | flops | bytes accessed | tf_op | source)
XLA Modules:
  0.0 153.9 jit_solution(3115717657151105555)
XLA Ops:
  0.0 0.7 iota_add_fusion
  0.7 0.3 convert_reduce_fusion
  1.0 1.7 %convolution_convert_fusion.1 = bf16[384,768]{1,0:T(8,128)(2,1)S(1)} fusion(bf16[512,768]{1,0:T(8,128)(2,1)} %param.2, s32[512]{0:T(512)S(1)} %get-tuple-element.13), kind=kOutput, calls=%fused_computation.48 | convolution fusion | flops 302481408 | bytes 1378304 | tf_op jit(solution)/shard_map/dot_general | solution.py:31
  2.7 4.1 %collective-permute-start.5 = (bf16[384,768]{1,0:T(8,128)(2,1)S(1)}, bf16[384,768]{1,0:T(8,128)(2,1)S(1)}, u32[]{:S(2)}, u32[]{:S(2)}) collective-permute-start(bf16[384,768]{1,0:T(8,128)(2,1)S(1)} %convolution_convert_fusion.1), channel_id=1, source_target_pairs={{0,4},{1,5},{2,6},{3,7},{4,0},{5,1},{6,2},{7,3},{8,12},{9,13},{10,... | collective-permute-start | bytes 1769480 | tf_op jit(solution)/shard_map/ppermute | solution.py:17
  7.1 25.8 %collective-permute-done.4 = s32[384]{0:T(512)S(1)} collective-permute-done((s32[384]{0:T(512)S(1)}, s32[384]{0:T(512)S(1)}, u32[]{:S(2)}, u32[]{:S(2)}) %collective-permute-start.4) | collective-permute-done | bytes 1568 | tf_op jit(solution)/shard_map/ppermute | solution.py:17
  32.9 1.8 %convolution_convert_fusion = bf16[768,768]{1,0:T(8,128)(2,1)} fusion(bf16[384,768]{1,0:T(8,128)(2,1)S(1)} %collective-permute-done.5, s32[384]{0:T(512)S(1)} %collective-permute-done.4), kind=kOutput, calls=%fused_computation.36 | convolution fusion | flops 453869568 | bytes 1771008 | tf_op jit(solution)/shard_map/dot_general | solution.py:31
  34.7 4.3 %all-to-all-start.1 = ((bf16[8,96,768]{2,1,0:T(8,128)(2,1)}), bf16[8,96,768]{2,1,0:T(8,128)(2,1)}, u32[]{:S(2)}, u32[]{:S(2)}) async-start(bf16[8,96,768]{2,1,0:T(8,128)(2,1)} %bitcast.12), calls=%async_computation.1 | async-start | bytes 2359296 | tf_op jit(solution)/shard_map/all_to_all | solution.py:21
  39.2 0.5 fusion.36
  39.7 1.0 fusion.19
  40.7 1.3 fusion.18
  42.1 14.7 %all-to-all-done.1 = bf16[8,96,768]{2,1,0:T(8,128)(2,1)} async-done(((bf16[8,96,768]{2,1,0:T(8,128)(2,1)}), bf16[8,96,768]{2,1,0:T(8,128)(2,1)}, u32[]{:S(2)}, u32[]{:S(2)}) %all-to-all-start.1) | async-done | bytes 1179680 | tf_op jit(solution)/shard_map/all_to_all | solution.py:21
  56.8 3.8 %all-to-all-start = ((bf16[8,144,768]{2,1,0:T(8,128)(2,1)}), bf16[8,144,768]{2,1,0:T(8,128)(2,1)S(1)}, u32[]{:S(2)}, u32[]{:S(2)}) async-start(bf16[8,144,768]{2,1,0:T(8,128)(2,1)} %fusion.18), calls=%async_computation | async-start | bytes 3538944 | tf_op jit(solution)/shard_map/all_to_all | solution.py:21
  60.7 22.4 %all-to-all-done = bf16[8,144,768]{2,1,0:T(8,128)(2,1)S(1)} async-done(((bf16[8,144,768]{2,1,0:T(8,128)(2,1)}), bf16[8,144,768]{2,1,0:T(8,128)(2,1)S(1)}, u32[]{:S(2)}, u32[]{:S(2)}) %all-to-all-start) | async-done | bytes 1769504 | tf_op jit(solution)/shard_map/all_to_all | solution.py:21
  83.2 4.2 %collective-permute-start.2 = (bf16[8,16,128]{2,1,0:T(8,128)(2,1)S(1)}, bf16[8,16,128]{2,1,0:T(8,128)(2,1)S(1)}, u32[]{:S(2)}, u32[]{:S(2)}) collective-permute-start(bf16[8,16,128]{2,1,0:T(8,128)(2,1)S(1)} %get-tuple-element.8), channel_id=1, source_target_pairs={{0,4},{1,5},{2,6},{3,7},{4,0},{5,1},{6,2},{7,3},{8,12},{9,13},{10,... | collective-permute-start | bytes 98312 | tf_op jit(solution)/shard_map/ppermute | solution.py:17
  87.7 0.8 slice.119
  88.5 0.3 collective-permute-start.3
  88.8 3.3 %fusion.92 = (f32[1024]{0:T(1024)S(1)}, bf16[1024,1024]{0,1:T(8,128)(2,1)S(1)}) fusion(f32[1024]{0:T(1024)S(1)} %bitcast.90, bf16[1024,768]{1,0:T(8,128)(2,1)S(1)} %bitcast.57, s32[1024]{0:T(1024)S(1)} %bitcast.87, s32[1024]{0:T(1024)S(1)} %bitcast.80), kind=kOutput, calls=%fused_computation.179 | convolution fusion | flops 1621097472 | bytes 3686400 | tf_op jit(solution)/shard_map/dot_general | solution.py:35
  92.1 3.6 %fusion.8 = f32[1024,768]{1,0:T(8,128)} fusion(bf16[1024,768]{1,0:T(8,128)(2,1)S(1)} %bitcast.58, bf16[1024,1024]{0,1:T(8,128)(2,1)S(1)} %get-tuple-element.29), kind=kOutput, calls=%fused_computation.18 | convolution fusion | flops 1610612736 | bytes 6815744 | tf_op jit(solution)/shard_map/dot_general | solution.py:44
  95.9 3.2 %fusion.90 = (f32[1024]{0:T(1024)S(1)}, bf16[1024,768]{0,1:T(8,128)(2,1)S(1)}) fusion(f32[768]{0:T(1024)S(1)} %mul.166, f32[1024]{0:T(1024)S(1)} %bitcast.91, bf16[1024,768]{1,0:T(8,128)(2,1)S(1)} %bitcast.59, bf16[768,768]{1,0:T(8,128)(2,1)} %bitcast.13, s32[768]{0:T(1024)S(1)} %and.167, s32[1024]{0:T(1024)S(1)} %bitcast.81), kind=kOutput, calls=%fused_computation.177 | convolution fusion | flops 1214249984 | bytes 4343808 | tf_op jit(solution)/shard_map/dot_general | solution.py:35
  99.1 4.4 %fusion.22 = f32[1024,768]{1,0:T(8,128)} fusion(bf16[768,768]{1,0:T(8,128)(2,1)} %bitcast.13, bf16[1024,768]{0,1:T(8,128)(2,1)S(1)} %get-tuple-element.23), kind=kOutput, calls=%fused_computation.33 | convolution fusion | flops 1207959552 | bytes 5898240 | tf_op jit(solution)/shard_map/dot_general | solution.py:44
  103.9 0.8 collective-permute-done.6
  105.2 4.2 %collective-permute-done.3 = bf16[8,32,768]{2,1,0:T(8,128)(2,1)S(1)} collective-permute-done((bf16[8,32,768]{2,1,0:T(8,128)(2,1)}, bf16[8,32,768]{2,1,0:T(8,128)(2,1)S(1)}, u32[]{:S(2)}, u32[]{:S(2)}) %collective-permute-start.3) | collective-permute-done | bytes 393248 | tf_op jit(solution)/shard_map/ppermute | solution.py:17
  109.4 0.7 fusion.91
  110.2 0.6 fusion.43
  110.8 3.2 %fusion.88 = (f32[1024]{0:T(1024)S(1)}, bf16[1024,768]{0,1:T(8,128)(2,1)S(1)}) fusion(f32[768]{0:T(1024)S(1)} %mul.176, f32[1024]{0:T(1024)S(1)} %bitcast.93, bf16[1024,768]{1,0:T(8,128)(2,1)S(1)} %bitcast.61, bf16[768,768]{1,0:T(8,128)(2,1)} %collective-permute-done.8, s32[768]{0:T(1024)S(1)} %and.173, s32[1024]{0:T(1024)S(1)} %bitcast.83), kind=kOutput, calls=%fused_computation.175 | convolution fusion | flops 1214249984 | bytes 4343808 | tf_op jit(solution)/shard_map/dot_general | solution.py:35
  114.0 0.7 fusion.89
  114.7 0.6 fusion.41
  115.4 4.2 %fusion.2 = (f32[1024]{0:T(1024)S(1)}, f32[1024,1024]{0,1:T(8,128)S(1)}) fusion(f32[1024]{0:T(1024)S(1)} %bitcast.97, s32[1024]{0:T(1024)S(1)} %bitcast.88, f32[1024]{0:T(1024)S(1)} %bitcast.95, s32[1024]{0:T(1024)S(1)} %bitcast.85, bf16[1024,768]{1,0:T(8,128)(2,1)S(1)} %bitcast.63, bf16[1024,768]{1,0:T(8,128)(2,1)} %collective-permute-done.1), kind=kOutput, calls=%fused_computation.13 | convolution fusion | flops 1617951744 | bytes 7360512 | tf_op jit(solution)/shard_map/dot_general | solution.py:35
  119.6 4.2 %fusion.4 = f32[1024,768]{1,0:T(8,128)S(1)} fusion(bf16[1024,768]{1,0:T(8,128)(2,1)} %collective-permute-done.1, f32[1024,1024]{0,1:T(8,128)S(1)} %get-tuple-element.27, f32[1024]{0:T(1024)S(1)} %bitcast.98, s32[1024]{0:T(1024)S(1)} %bitcast.89, f32[1024]{0:T(1024)S(1)} %bitcast.96, s32[1024]{0:T(1024)S(1)} %bitcast.86), kind=kOutput, calls=%fused_computation.15 | convolution fusion | flops 1617952768 | bytes 8929280 | tf_op jit(solution)/shard_map/dot_general | solution.py:44
  123.8 3.6 %divide_convert_fusion = bf16[1024,768]{1,0:T(8,128)(2,1)S(1)} fusion(f32[1024,768]{1,0:T(8,128)S(1)} %fusion.41, f32[1024,768]{1,0:T(8,128)S(1)} %copy-done.2, f32[1024,768]{1,0:T(8,128)S(1)} %fusion.43, f32[1024,768]{1,0:T(8,128)S(1)} %copy-done.1, f32[1024,768]{1,0:T(8,128)S(1)} %fusion.4, f32[1024]{0:T(1024)S(1)} %add_add_fusion, ...), kind=kOutput, calls=%fused_computation.8 | convolution fusion | flops 1213464576 | bytes 20058112 | tf_op jit(solution)/shard_map/dot_general | solution.py:44
  127.4 24.4 %all_to_all.15 = bf16[8,128,768]{2,1,0:T(8,128)(2,1)S(1)} all-to-all(bf16[8,128,768]{2,1,0:T(8,128)(2,1)S(1)} %bitcast.64), channel_id=1, replica_groups={{0,1,2,3,16,17,18,19},{4,5,6,7,20,21,22,23},{8,9,10,11,24,25,26,27},{12..., dimensions={0} | all-to-all | bytes 3145728 | tf_op jit(solution)/shard_map/all_to_all | solution.py:21
  151.7 2.1 %fusion.26 = bf16[512,768]{1,0:T(8,128)(2,1)} fusion(bf16[1024,768]{1,0:T(8,128)(2,1)S(1)} %bitcast.65, s32[512]{0:T(512)S(1)} %get-tuple-element.12), kind=kOutput, calls=%fused_computation.37 | convolution fusion | flops 806223872 | bytes 2361344 | tf_op jit(solution)/shard_map/dot_general | solution.py:155
  (51 shorter events, 2.1 us)
Async XLA Ops:
  1.0 37.9 %copy-start = (bf16[512,768]{1,0:T(8,128)(2,1)S(1)}, bf16[512,768]{1,0:T(8,128)(2,1)}, u32[]{:S(2)}) copy-start(bf16[512,768]{1,0:T(8,128)(2,1)} %param.2) | copy-start | bytes 2359300
  2.7 30.2 %collective-permute-start.5 = (bf16[384,768]{1,0:T(8,128)(2,1)S(1)}, bf16[384,768]{1,0:T(8,128)(2,1)S(1)}, u32[]{:S(2)}, u32[]{:S(2)}) collective-permute-start(bf16[384,768]{1,0:T(8,128)(2,1)S(1)} %convolution_convert_fusion.1), channel_id=1, source_target_pairs={{0,4},{1,5},{2,6},{3,7},{4,0},{5,1},{6,2},{7,3},{8,12},{9,13},{10,... | collective-permute-start | bytes 1769480 | tf_op jit(solution)/shard_map/ppermute | solution.py:17
  7.0 25.9 %collective-permute-start.4 = (s32[384]{0:T(512)S(1)}, s32[384]{0:T(512)S(1)}, u32[]{:S(2)}, u32[]{:S(2)}) collective-permute-start(s32[384]{0:T(512)S(1)} %select_reduce_fusion), channel_id=1, source_target_pairs={{0,4},{1,5},{2,6},{3,7},{4,0},{5,1},{6,2},{7,3},{8,12},{9,13},{10,... | collective-permute-start | bytes 4616 | tf_op jit(solution)/shard_map/ppermute | solution.py:17
  34.7 22.1 %all-to-all-start.1 = ((bf16[8,96,768]{2,1,0:T(8,128)(2,1)}), bf16[8,96,768]{2,1,0:T(8,128)(2,1)}, u32[]{:S(2)}, u32[]{:S(2)}) async-start(bf16[8,96,768]{2,1,0:T(8,128)(2,1)} %bitcast.12), calls=%async_computation.1 | async-start | bytes 2359296 | tf_op jit(solution)/shard_map/all_to_all | solution.py:21
  56.8 26.3 %all-to-all-start = ((bf16[8,144,768]{2,1,0:T(8,128)(2,1)}), bf16[8,144,768]{2,1,0:T(8,128)(2,1)S(1)}, u32[]{:S(2)}, u32[]{:S(2)}) async-start(bf16[8,144,768]{2,1,0:T(8,128)(2,1)} %fusion.18), calls=%async_computation | async-start | bytes 3538944 | tf_op jit(solution)/shard_map/all_to_all | solution.py:21
  60.6 50.2 %collective-permute-start.8 = (bf16[768,768]{1,0:T(8,128)(2,1)}, bf16[768,768]{1,0:T(8,128)(2,1)}, u32[]{:S(2)}, u32[]{:S(2)}) collective-permute-start(bf16[768,768]{1,0:T(8,128)(2,1)} %bitcast.13), channel_id=1, source_target_pairs={{0,8},{1,9},{2,10},{3,11},{4,12},{5,13},{6,14},{7,15},{8,0},{9,1},... | collective-permute-start | bytes 3538952 | tf_op jit(solution)/shard_map/ppermute | solution.py:17
  83.2 12.6 %collective-permute-start = (bf16[8,16,128]{2,1,0:T(8,128)(2,1)S(1)}, bf16[8,16,128]{2,1,0:T(8,128)(2,1)S(1)}, u32[]{:S(2)}, u32[]{:S(2)}) collective-permute-start(bf16[8,16,128]{2,1,0:T(8,128)(2,1)S(1)} %get-tuple-element.8), channel_id=1, source_target_pairs={{0,8},{1,9},{2,10},{3,11},{4,12},{5,13},{6,14},{7,15},{8,0},{9,1},... | collective-permute-start | bytes 98312 | tf_op jit(solution)/shard_map/ppermute | solution.py:17
  83.2 12.4 %collective-permute-start.2 = (bf16[8,16,128]{2,1,0:T(8,128)(2,1)S(1)}, bf16[8,16,128]{2,1,0:T(8,128)(2,1)S(1)}, u32[]{:S(2)}, u32[]{:S(2)}) collective-permute-start(bf16[8,16,128]{2,1,0:T(8,128)(2,1)S(1)} %get-tuple-element.8), channel_id=1, source_target_pairs={{0,4},{1,5},{2,6},{3,7},{4,0},{5,1},{6,2},{7,3},{8,12},{9,13},{10,... | collective-permute-start | bytes 98312 | tf_op jit(solution)/shard_map/ppermute | solution.py:17
  87.5 27.8 %collective-permute-start.1 = (bf16[1024,768]{1,0:T(8,128)(2,1)S(1)}, bf16[1024,768]{1,0:T(8,128)(2,1)}, u32[]{:S(2)}, u32[]{:S(2)}) collective-permute-start(bf16[1024,768]{1,0:T(8,128)(2,1)S(1)} %bitcast.56), channel_id=1, source_target_pairs={{0,8},{1,9},{2,10},{3,11},{4,12},{5,13},{6,14},{7,15},{8,0},{9,1},... | collective-permute-start | bytes 4718600 | tf_op jit(solution)/shard_map/ppermute | solution.py:17
  88.5 20.9 %collective-permute-start.3 = (bf16[8,32,768]{2,1,0:T(8,128)(2,1)}, bf16[8,32,768]{2,1,0:T(8,128)(2,1)S(1)}, u32[]{:S(2)}, u32[]{:S(2)}) collective-permute-start(bf16[8,32,768]{2,1,0:T(8,128)(2,1)} %slice.119), channel_id=1, source_target_pairs={{0,4},{1,5},{2,6},{3,7},{4,0},{5,1},{6,2},{7,3},{8,12},{9,13},{10,... | collective-permute-start | bytes 1179656 | tf_op jit(solution)/shard_map/ppermute | solution.py:17
  103.5 1.2 collective-permute-start.6
  109.4 4.6 %collective-permute-start.7 = (bf16[256,768]{1,0:T(8,128)(2,1)S(1)}, bf16[256,768]{1,0:T(8,128)(2,1)S(1)}, u32[]{:S(2)}, u32[]{:S(2)}) collective-permute-start(bf16[256,768]{1,0:T(8,128)(2,1)S(1)} %bitcast.67), channel_id=1, source_target_pairs={{0,8},{1,9},{2,10},{3,11},{4,12},{5,13},{6,14},{7,15},{8,0},{9,1},... | collective-permute-start | bytes 1179656 | tf_op jit(solution)/shard_map/ppermute | solution.py:17
  119.5 4.2 %copy-start.1 = (f32[1024,768]{1,0:T(8,128)S(1)}, f32[1024,768]{1,0:T(8,128)}, u32[]{:S(2)}) copy-start(f32[1024,768]{1,0:T(8,128)} %fusion.8) | copy-start | bytes 9437188
  119.5 4.2 %copy-start.2 = (f32[1024,768]{1,0:T(8,128)S(1)}, f32[1024,768]{1,0:T(8,128)}, u32[]{:S(2)}) copy-start(f32[1024,768]{1,0:T(8,128)} %fusion.22) | copy-start | bytes 9437188

commit v2 on v1

v2 whole, which is shorter than its diff:
```python
import functools

import jax
import jax.numpy as jnp
from jax import lax
from jax.experimental import pallas as pl
from jax.experimental.pallas import tpu as pltpu
from jax.sharding import PartitionSpec as P

BPD = 2
CAP = 512
META = 16
FACTS = 4
LANES = 128

sharpness = 32.0
epsilon = 1e-06

AXES = ("hx", "hy")
VMEM = pl.BlockSpec(memory_space=pltpu.VMEM)
ANY = pl.BlockSpec(memory_space=pl.ANY)
F32, BF16, I32 = jnp.float32, jnp.bfloat16, jnp.int32


class Plan:
    def __init__(self, nx, ny, files, width):
        self.nx, self.ny, self.files, self.width = nx, ny, files, width
        self.devices = nx * ny
        self.cells = self.devices // 4
        self.slots = 4 * BPD * CAP // self.devices
        self.slots_a = max(16, self.slots * 3 // 4 // 16 * 16)
        self.slots_b = self.slots - self.slots_a
        self.stride = self.slots // self.slots_b
        self.files_a = files - files // self.stride
        self.total = self.cells * self.slots
        self.segments = width // LANES
        self.block = max(META, -(-(-(-FACTS * self.cells // self.segments)) // META) * META)
        self.core_bit, self.half_bit = ny, ny // 2
        self.groups = [
            [(2 * u + core) * ny + half * (ny // 2) + v for u in range(nx // 2) for v in range(ny // 2)]
            for core in range(2)
            for half in range(2)
        ]


def swapped(value, bit, plan):
    return lax.ppermute(value, AXES, [(i, i ^ bit) for i in range(plan.devices)])


def exchange(value, plan):
    return lax.all_to_all(
        value, AXES, split_axis=0, concat_axis=0, tiled=True, axis_index_groups=plan.groups
    )


def call(kernel, out_shape, in_specs, flops, moved, exps=0):
    return pl.pallas_call(
        kernel,
        out_shape=out_shape,
        in_specs=in_specs,
        out_specs=jax.tree.map(lambda _: VMEM, out_shape),
        compiler_params=pltpu.CompilerParams(vmem_limit_bytes=56 * 1024 * 1024),
        cost_estimate=pl.CostEstimate(flops=flops, bytes_accessed=moved, transcendentals=exps),
    )


def iota(shape, dim):
    return lax.broadcasted_iota(I32, shape, dim)


def column(row):
    return jnp.broadcast_to(row, (LANES, row.shape[1])).T


def rows_dot(left, right):
    return lax.dot_general(left, right, (((1,), (1,)), ((), ())), preferred_element_type=F32)


def sort_kernel(plan, bucket_ref, rows_ref, early_ref, place_ref):
    nx, ny, files = plan.nx, plan.ny, plan.files
    bucket = bucket_ref[...]
    low_b = ny.bit_length() - 1
    a = bucket >> (low_b + 1)
    b = (bucket >> 1) & (ny - 1)
    c = bucket & 1
    cell = (a & (nx // 2 - 1)) * (ny // 2) + (b & (ny // 2 - 1))
    tag = (a >> (nx.bit_length() - 2)) * 4 + (b >> (low_b - 1)) * 2 + c + 1
    order = cell * files + iota((1, files), 1)
    rank = jnp.sum((column(order)[:, :1] < order).astype(I32), axis=0, keepdims=True)
    start = jnp.sum((column(cell)[:, :1] < cell).astype(I32), axis=0, keepdims=True)
    shift = plan.stride.bit_length() - 1
    late = (rank & (plan.stride - 1)) == plan.stride - 1
    late_rank, late_start = rank >> shift, start >> shift
    early_index = (rank - late_rank) - (start - late_start)
    slot = cell * plan.slots + jnp.where(late, plan.slots_a + late_rank - late_start, early_index)
    place_ref[...] = jnp.zeros(place_ref.shape, I32)
    place_ref[0:1, :] = slot
    place_ref[1:2, :] = tag
    target = jnp.where(late, files, rank - late_rank)
    match = (iota((plan.files_a, files), 0) == target).astype(F32).astype(BF16)
    early_ref[0 : plan.files_a, :] = jnp.dot(
        match, rows_ref[...], preferred_element_type=F32
    ).astype(BF16)
    which = iota((META, files), 0)
    info = jnp.where(which == 0, cell, jnp.where(which == 1, early_index, 0))
    info = rows_dot(info.astype(F32).astype(BF16), match).astype(BF16)
    early_ref[plan.files_a :, :] = jnp.zeros((META, plan.width), BF16)
    early_ref[plan.files_a :, 0 : plan.files_a] = info


def send_kernel(plan, place_ref, rows_ref, after_ref, out_ref):
    del after_ref
    files, slots = plan.files, plan.slots
    slot, tag = place_ref[0:1, :], place_ref[1:2, :]
    rows = rows_ref[...]
    wide = rows.astype(F32)
    square = jnp.sum(wide * wide, axis=1, keepdims=True)
    square = jnp.broadcast_to(square, (files, LANES)).T[0:1, :]
    inv = 1.0 / jnp.sqrt(square * (1.0 / plan.width) + epsilon)
    high = inv.astype(BF16).astype(F32)
    middle = (inv - high).astype(BF16).astype(F32)
    low = inv - high - middle
    which = iota((META, files), 0)
    facts = jnp.where(
        which == 0,
        tag.astype(F32),
        jnp.where(which == 1, high, jnp.where(which == 2, middle, jnp.where(which == 3, low, 0.0))),
    ).astype(BF16)
    for cell in range(plan.cells):
        match = (iota((slots, files), 0) + cell * slots == slot).astype(F32).astype(BF16)
        out_ref[cell, 0:slots, :] = jnp.dot(match, rows, preferred_element_type=F32).astype(BF16)
        out_ref[cell, slots:, :] = jnp.zeros((META, plan.width), BF16)
        out_ref[cell, slots:, 0:slots] = rows_dot(facts, match).astype(BF16)


def split_kernel(plan, got_ref, rows_ref, late_ref):
    slots, slots_a, slots_b, cells = plan.slots, plan.slots_a, plan.slots_b, plan.cells
    for source in range(cells):
        rows_ref[source * slots : (source + 1) * slots, :] = got_ref[source, 0:slots, :]
        late_ref[source * slots_b : (source + 1) * slots_b, :] = got_ref[source, slots_a:slots, :]
    metas = [got_ref[source, slots:, 0:LANES].astype(F32) for source in range(cells)]
    for segment in range(plan.segments):
        lines = []
        for line in range(plan.block):
            fact, source = divmod(line * plan.segments + segment, cells)
            lines.append(
                metas[source][fact : fact + 1, :] if fact < FACTS else jnp.zeros((1, LANES), F32)
            )
        block = jnp.concatenate(lines, axis=0).astype(BF16)
        lanes = slice(segment * LANES, (segment + 1) * LANES)
        rows_ref[cells * slots :, lanes] = block
        late_ref[cells * slots_b :, lanes] = block


def relay_kernel(plan, early_ref, after_ref, out_ref):
    del after_ref
    files_a = plan.files_a
    info = early_ref[files_a:, 0:files_a].astype(F32)
    target = (info[0:1, :] * plan.slots_a + info[1:2, :]).astype(I32)
    rows = early_ref[0:files_a, :]
    for cell in range(plan.cells):
        match = iota((plan.slots_a, files_a), 0) + cell * plan.slots_a == target
        out_ref[cell] = jnp.dot(
            match.astype(F32).astype(BF16), rows, preferred_element_type=F32
        ).astype(BF16)


def attend_kernel(plan, sets, first, last, *refs):
    refs = list(refs)
    query_ref, fact_ref = refs.pop(0), refs.pop(0)
    keys = [(refs.pop(0), refs.pop(0), count, own) for count, own in sets]
    if not first:
        old_ref, old_sum_ref = refs.pop(0), refs.pop(0)
    if last:
        out_ref, column_ref = refs
    else:
        out_ref, sum_ref, column_ref = refs
    tag = fact_ref[0:1, :].astype(I32)
    place = jnp.maximum(tag - 1, 0)
    bits = (2 << place) | (2 << (place ^ 1)) | (2 << (place ^ 2)) | (2 << (place ^ 4))
    column_ref[0] = column(fact_ref[1:2, :] * (sharpness / plan.width))
    column_ref[1] = column(bits.astype(F32))
    chunk = 256

    @pl.loop(0, plan.total // chunk)
    def _(step):
        here = pl.ds(pl.multiple_of(step * chunk, chunk), chunk)
        query = query_ref[here, :]
        query_inv = column_ref[0, here, :][:, 0:1]
        query_bits = column_ref[1, here, :][:, 0:1].astype(I32)
        if first:
            numerator = jnp.zeros((chunk, plan.width), F32)
            denominator = jnp.ones((chunk, LANES), F32)
        else:
            numerator, denominator = old_ref[here, :], old_sum_ref[here, :]
        for key_ref, key_fact_ref, count, own in keys:
            for begin in range(0, count, 512):
                size = min(512, count - begin)
                lanes = slice(begin, begin + size)
                key = key_ref[lanes, :]
                key_bit = 1 << key_fact_ref[0:1, lanes].astype(I32)
                score = rows_dot(query, key) * query_inv * key_fact_ref[1:2, lanes]
                live = (query_bits & key_bit) != 0
                if own:
                    live = live & (
                        iota((chunk, size), 0) + (step * chunk - begin) != iota((chunk, size), 1)
                    )
                kernel = jnp.where(live, jnp.exp(score), 0.0)
                denominator = denominator + jnp.sum(kernel, axis=1, keepdims=True)
                numerator = numerator + jnp.dot(
                    kernel.astype(BF16), key, preferred_element_type=F32
                )
        if last:
            out_ref[here, :] = (numerator / denominator[:, 0:1]).astype(BF16)
        else:
            out_ref[here, :] = numerator
            sum_ref[here, :] = denominator


def attend(plan, query, facts, key_sets, old=None, last=False):
    sets = [(fact.shape[1], own) for _, fact, own in key_sets]
    total, width = plan.total, plan.width
    keys = sum(count for count, _ in sets)
    if last:
        out_shape = jax.ShapeDtypeStruct((total, width), BF16)
    else:
        out_shape = (
            jax.ShapeDtypeStruct((total, width), F32),
            jax.ShapeDtypeStruct((total, LANES), F32),
        )
    args = [query, facts]
    for rows, fact, _ in key_sets:
        args += [rows, fact]
    if old is not None:
        args += list(old)
    return pl.pallas_call(
        functools.partial(attend_kernel, plan, sets, old is None, last),
        out_shape=out_shape,
        in_specs=[VMEM] * len(args),
        out_specs=jax.tree.map(lambda _: VMEM, out_shape),
        scratch_shapes=[pltpu.VMEM((2, total, LANES), F32)],
        compiler_params=pltpu.CompilerParams(vmem_limit_bytes=56 * 1024 * 1024),
        cost_estimate=pl.CostEstimate(
            flops=4 * total * keys * width, bytes_accessed=12 * total * width, transcendentals=total * keys
        ),
    )(*args)


def unpack_kernel(plan, place_ref, home_ref, out_ref):
    slot = column(place_ref[0:1, :])[:, 0:1]
    match = (iota((plan.files, plan.total), 1) == slot).astype(F32).astype(BF16)
    out_ref[...] = jnp.dot(match, home_ref[...], preferred_element_type=F32).astype(BF16)


def key_facts(plan, block):
    wide = block.reshape(plan.block * plan.segments, LANES)[: FACTS * plan.cells]
    wide = wide.reshape(FACTS, plan.cells, LANES)[:, :, : plan.slots].astype(F32)
    return jnp.stack([wide[0], wide[1] + wide[2] + wide[3]])


def flat(facts):
    return facts.reshape(2, -1)


def body(embeddings, bucket):
    files, width = embeddings.shape
    plan = Plan(lax.axis_size("hx"), lax.axis_size("hy"), files, width)
    cells, slots, slots_a, total = plan.cells, plan.slots, plan.slots_a, plan.total
    row_bytes = width * 2

    early, place = call(
        functools.partial(sort_kernel, plan),
        (
            jax.ShapeDtypeStruct((plan.files_a + META, width), BF16),
            jax.ShapeDtypeStruct((8, files), I32),
        ),
        [VMEM, VMEM],
        2 * plan.files_a * files * width,
        2 * files * row_bytes,
    )(bucket.reshape(1, files), embeddings)
    other_early = swapped(early, plan.half_bit, plan)
    payload = call(
        functools.partial(send_kernel, plan),
        jax.ShapeDtypeStruct((cells, slots + META, width), BF16),
        [VMEM, VMEM, ANY],
        2 * total * files * width,
        3 * files * row_bytes,
    )(place, embeddings, early)
    got = exchange(payload, plan)
    own, late = call(
        functools.partial(split_kernel, plan),
        (
            jax.ShapeDtypeStruct((total + plan.block, width), BF16),
            jax.ShapeDtypeStruct((cells * plan.slots_b + plan.block, width), BF16),
        ),
        [VMEM],
        0,
        4 * total * row_bytes,
    )(got)
    half_late = swapped(late, plan.half_bit, plan)
    mate = swapped(own, plan.core_bit, plan)
    mate_late = swapped(half_late, plan.core_bit, plan)

    own_facts = flat(key_facts(plan, own[total:]))
    sums = attend(plan, own, own_facts, [(own, own_facts, True)])
    relayed = call(
        functools.partial(relay_kernel, plan),
        jax.ShapeDtypeStruct((cells, slots_a, width), BF16),
        [VMEM, ANY],
        2 * cells * slots_a * plan.files_a * width,
        2 * cells * slots_a * row_bytes,
    )(other_early, sums[1])
    half_early = exchange(relayed, plan).reshape(cells * slots_a, width)
    sums = attend(plan, own, own_facts, [(mate, flat(key_facts(plan, mate[total:])), False)], sums)
    mate_early = swapped(half_early, plan.core_bit, plan)

    late_rows = cells * plan.slots_b
    half_facts = key_facts(plan, half_late[late_rows:])
    mate_facts = key_facts(plan, mate_late[late_rows:])
    sums = attend(
        plan,
        own,
        own_facts,
        [
            (half_late, flat(half_facts[:, :, slots_a:]), False),
            (mate_late, flat(mate_facts[:, :, slots_a:]), False),
            (half_early, flat(half_facts[:, :, :slots_a]), False),
        ],
        sums,
    )
    smoothed = attend(
        plan, own, own_facts, [(mate_early, flat(mate_facts[:, :, :slots_a]), False)], sums, last=True
    )
    home = exchange(smoothed.reshape(cells, slots, width), plan).reshape(total, width)
    return call(
        functools.partial(unpack_kernel, plan),
        jax.ShapeDtypeStruct((files, width), BF16),
        [VMEM, VMEM],
        2 * total * files * width,
        3 * files * row_bytes,
    )(place, home)


def solution(mesh):
    return jax.shard_map(
        body,
        mesh=mesh,
        in_specs=(P(("hx", "hy"), None), P(("hx", "hy"))),
        out_specs=P(("hx", "hy"), None),
        check_vma=False,
    )
```

time: 154 us -> 166 us (1.078)
  Pallas kernels: 0 us -> 56.5 us
  matrix products: 39.3 us -> 0 us
  waiting for transfers between devices: 68 us -> 60.3 us
  local copies, waits for them, and re-layouts: 1.79 us -> 7.47 us
  starting transfers between devices: 17.1 us -> 12.9 us
  blocking collectives: 24.4 us -> 26.2 us
    pallas_call x0 -> x9, Pallas kernels: none -> 56.5 us  [the longest x4 40.2 us: attend(): pl.pallas_call(functools.partial(attend_kernel, plan, sets, old is None,...]
    dot_general x17 -> x0, matrix products: 39.3 us -> none  [the longest x6 17 us: attend(): jnp.dot(kernel.astype(jnp.bfloat16), keys, preferred_element_type=jnp.flo...]
    ppermute x9 -> x5, waiting for transfers between devices: 30.9 us -> 21.5 us  [swapped(): lax.ppermute(value, AXES, [(i, i ^ bit) for i in range(plan.devices)])]
    ppermute x9 -> x5, starting transfers between devices: 9.06 us -> 2.88 us  [swapped(): lax.ppermute(value, AXES, [(i, i ^ bit) for i in range(plan.devices)])]
    unnamed x6 -> x16, local copies, waits for them, and re-layouts: 0.01 us -> 3.12 us
    reshape x1 -> x8, local copies, waits for them, and re-layouts: 0.01 us -> 2.86 us  [the longest x4 2.69 us: flat(): return facts.reshape(2, -1)]
    all_to_all x2, starting transfers between devices: 8.03 us -> 10 us  [exchange(): lax.all_to_all(value, AXES, split_axis=0, concat_axis=0, tiled=True, axis...]
    all_to_all x1, blocking collectives: 24.4 us -> 26.2 us  [exchange(): lax.all_to_all(value, AXES, split_axis=0, concat_axis=0, tiled=True, axis...]
  transfers between devices with their start and end apart: 11 -> 7, of which waited for: 5 -> 4; matrix products, arithmetic and copies ran while one was open for 17% -> 4% of each run, Pallas kernels for 0% -> 21%
where the time goes in v2:
time: 166 us; the launch traced here: 165 us
  waiting for transfers between devices  60.3 us (36%)
  Pallas kernels  56.5 us (34%)
  blocking collectives  26.2 us (16%)
  starting transfers between devices  12.9 us (8%)
  local copies, waits for them, and re-layouts  7.47 us (4%)
    pallas_call x4, Pallas kernels, attend(): pl.pallas_call(functools.partial(attend_kernel, plan, sets, old is None,...  40.2 us
    all_to_all x2, waiting for transfers between devices, exchange(): lax.all_to_all(value, AXES, split_axis=0, concat_axis=0, tiled=True, axis...  38.8 us
    all_to_all x1, blocking collectives, exchange(): lax.all_to_all(value, AXES, split_axis=0, concat_axis=0, tiled=True, axis...  26.2 us
    ppermute x5, waiting for transfers between devices, swapped(): lax.ppermute(value, AXES, [(i, i ^ bit) for i in range(plan.devices)])  21.5 us
    all_to_all x2, starting transfers between devices, exchange(): lax.all_to_all(value, AXES, split_axis=0, concat_axis=0, tiled=True, axis...  10 us
    pallas_call x1, Pallas kernels, body(): call(functools.partial(send_kernel, plan), jax.ShapeDtypeStruct((cells, s...  3.85 us
    pallas_call x1, Pallas kernels, body(): call(functools.partial(unpack_kernel, plan), jax.ShapeDtypeStruct((files,...  3.58 us
  transfers between devices with their start and end apart: 7, of which 4 were waited for; matrix products, arithmetic and copies ran while one was open for 4% of the time, Pallas kernels for 21%

profile of v2, /device:TPU:0, one launch (start us, length us, event | category | flops | bytes accessed | tf_op | source)
XLA Modules:
  0.0 165.0 jit_solution(17347609207897400868)
XLA Ops:
  0.0 2.9 %shard_map.28 = (bf16[400,768]{1,0:T(8,128)(2,1)}, s32[8,512]{1,0:T(8,128)}) custom-call(s32[1,512]{1,0:T(1,128)} %bitcast.24, bf16[512,768]{1,0:T(8,128)(2,1)} %rows_ref.3), custom_call_target="tpu_custom_call" | custom-call | flops 301989888 | bytes 1572864 | tf_op jit(solution)/shard_map/pallas_call | solution.py:271
  2.9 3.9 %shard_map.29 = bf16[8,144,768]{2,1,0:T(8,128)(2,1)} custom-call(s32[8,512]{1,0:T(8,128)} %get-tuple-element.15.place_ref, bf16[512,768]{1,0:T(8,128)(2,1)} %rows_ref.3, bf16[400,768]{1,0:T(8,128)(2,1)} %get-tuple-element.16.after_ref), custom_call_target="tpu_custom_call" | custom-call | flops 805306368 | bytes 2359296 | tf_op jit(solution)/shard_map/pallas_call | solution.py:282
  6.7 6.3 %all-to-all-start = ((bf16[8,144,768]{2,1,0:T(8,128)(2,1)}), bf16[8,144,768]{2,1,0:T(8,128)(2,1)S(1)}, u32[]{:S(2)}, u32[]{:S(2)}) async-start(bf16[8,144,768]{2,1,0:T(8,128)(2,1)} %shard_map.29), calls=%async_computation | async-start | bytes 3538944 | tf_op jit(solution)/shard_map/all_to_all | solution.py:51
  13.0 2.7 %collective-permute-start = (bf16[400,768]{1,0:T(8,128)(2,1)S(1)}, bf16[400,768]{1,0:T(8,128)(2,1)S(1)}, u32[]{:S(2)}, u32[]{:S(2)}) collective-permute-start(bf16[400,768]{1,0:T(8,128)(2,1)S(1)} %copy-done.2), channel_id=1, source_target_pairs={{0,4},{1,5},{2,6},{3,7},{4,0},{5,1},{6,2},{7,3},{8,12},{9,13},{10,... | collective-permute-start | bytes 1843208 | tf_op jit(solution)/shard_map/ppermute | solution.py:47
  15.7 37.9 %all-to-all-done.got_ref = bf16[8,144,768]{2,1,0:T(8,128)(2,1)S(1)} async-done(((bf16[8,144,768]{2,1,0:T(8,128)(2,1)}), bf16[8,144,768]{2,1,0:T(8,128)(2,1)S(1)}, u32[]{:S(2)}, u32[]{:S(2)}) %all-to-all-start) | async-done | bytes 1769504 | tf_op jit(solution)/shard_map/all_to_all | solution.py:51
  53.7 1.2 copy-done
  54.9 2.9 %shard_map.30 = (bf16[1040,768]{1,0:T(8,128)(2,1)}, bf16[272,768]{1,0:T(8,128)(2,1)}) custom-call(bf16[8,144,768]{2,1,0:T(8,128)(2,1)} %copy-done), custom_call_target="tpu_custom_call" | custom-call | bytes 6291456 | tf_op jit(solution)/shard_map/pallas_call | solution.py:290
  57.8 0.7 slice.104
  58.6 0.6 pad_maximum_fusion.2.refs_1_.refs_3_
  59.2 9.5 %shard_map.31 = (f32[1024,768]{1,0:T(8,128)}, f32[1024,128]{1,0:T(8,128)}) custom-call(bf16[1040,768]{1,0:T(8,128)(2,1)} %get-tuple-element.17.refs_0_.refs_2_, f32[2,1024]{1,0:T(2,128)} %pad_maximum_fusion.2.refs_1_.refs_3_, bf16[1040,768]{1,0:T(8,128)(2,1)} %get-tuple-element.17.refs_0_.refs_2_, f32[2,1024]{1,0:T(2,128)} %pad_maximum_fusion.2.refs_1_.refs_3_), custom_call_target="tpu_custom_call" | custom-call | flops 3221225472 | bytes 9437184 | tf_op jit(solution)/shard_map/pallas_call | solution.py:236
  68.8 0.8 copy-done.3
  69.6 3.1 %shard_map.32 = bf16[8,96,768]{2,1,0:T(8,128)(2,1)} custom-call(bf16[400,768]{1,0:T(8,128)(2,1)} %copy-done.3, f32[1024,128]{1,0:T(8,128)} %get-tuple-element.18.after_ref.refs_5_), custom_call_target="tpu_custom_call" | custom-call | flops 452984832 | bytes 2359296 | tf_op jit(solution)/shard_map/pallas_call | solution.py:306
  72.7 3.7 %all-to-all-start.1 = ((bf16[8,96,768]{2,1,0:T(8,128)(2,1)}), bf16[8,96,768]{2,1,0:T(8,128)(2,1)S(1)}, u32[]{:S(2)}, u32[]{:S(2)}) async-start(bf16[8,96,768]{2,1,0:T(8,128)(2,1)} %shard_map.32), calls=%async_computation.1 | async-start | bytes 2359296 | tf_op jit(solution)/shard_map/all_to_all | solution.py:51
  76.4 0.1 collective-permute-start.2
  76.5 0.1 collective-permute-start.4
  76.6 21.2 %collective-permute-done.2.refs_2_ = bf16[272,768]{1,0:T(8,128)(2,1)S(1)} collective-permute-done((bf16[272,768]{1,0:T(8,128)(2,1)S(1)}, bf16[272,768]{1,0:T(8,128)(2,1)S(1)}, u32[]{:S(2)}, u32[]{:S(2)}) %collective-permute-start.2) | collective-permute-done | bytes 417824 | tf_op jit(solution)/shard_map/ppermute | solution.py:47
  97.9 0.7 reshape.86.refs_7_
  98.6 0.1 slice_maximum_fusion
  98.7 0.7 reshape.84.refs_3_
  99.4 0.3 collective-permute-done.3.refs_4_
  99.7 0.1 pad_maximum_fusion.1
  99.8 0.7 reshape.85.refs_5_
  100.5 0.7 reshape.82.refs_3_
  101.2 0.7 slice.155
  101.9 0.8 all-to-all-done.1
  102.8 0.7 pad_maximum_fusion.3.refs_3_
  103.5 10.3 %shard_map.33 = (f32[1024,768]{1,0:T(8,128)}, f32[1024,128]{1,0:T(8,128)}) custom-call(bf16[1040,768]{1,0:T(8,128)(2,1)} %get-tuple-element.17.refs_0_.refs_2_, f32[2,1024]{1,0:T(2,128)} %pad_maximum_fusion.2.refs_1_.refs_3_, bf16[1040,768]{1,0:T(8,128)(2,1)} %collective-permute-done.4.refs_2_, f32[2,1024]{1,0:T(2,128)} %pad_maximum_fusion.3.refs_3_, ...), custom_call_target="tpu_custom_call" | custom-call | flops 3221225472 | bytes 9437184 | tf_op jit(solution)/shard_map/pallas_call | solution.py:236
  113.8 11.5 %shard_map.34 = (f32[1024,768]{1,0:T(8,128)}, f32[1024,128]{1,0:T(8,128)}) custom-call(bf16[1040,768]{1,0:T(8,128)(2,1)} %get-tuple-element.17.refs_0_.refs_2_, f32[2,1024]{1,0:T(2,128)} %pad_maximum_fusion.2.refs_1_.refs_3_, bf16[272,768]{1,0:T(8,128)(2,1)} %copy-done.4, f32[2,256]{1,0:T(2,128)} %reshape.84.refs_3_, bf16[272,768]{1,0:T(8,128)(2,1)} %copy-done.5, ...), custom_call_target="tpu_custom_call" | custom-call | flops 4026531840 | bytes 9437184 | tf_op jit(solution)/shard_map/pallas_call | solution.py:236
  125.3 1.0 copy-done.6
  126.4 8.9 %shard_map.35 = bf16[1024,768]{1,0:T(8,128)(2,1)} custom-call(bf16[1040,768]{1,0:T(8,128)(2,1)} %get-tuple-element.17.refs_0_.refs_2_, f32[2,1024]{1,0:T(2,128)} %pad_maximum_fusion.2.refs_1_.refs_3_, bf16[768,768]{1,0:T(8,128)(2,1)} %copy-done.6, f32[2,768]{1,0:T(2,128)} %reshape.82.refs_3_, f32[1024,768]{1,0:T(8,128)} %get-tuple-element.23.refs_4_, ...), custom_call_target="tpu_custom_call" | custom-call | flops 2415919104 | bytes 9437184 | tf_op jit(solution)/shard_map/pallas_call | solution.py:236
  135.2 26.2 %all_to_all.15 = bf16[8,128,768]{2,1,0:T(8,128)(2,1)} all-to-all(bf16[8,128,768]{2,1,0:T(8,128)(2,1)} %bitcast.16), channel_id=1, replica_groups={{0,1,2,3,16,17,18,19},{4,5,6,7,20,21,22,23},{8,9,10,11,24,25,26,27},{12..., dimensions={0} | all-to-all | bytes 3145728 | tf_op jit(solution)/shard_map/all_to_all | solution.py:51
  161.4 3.6 %shard_map.36 = bf16[512,768]{1,0:T(8,128)(2,1)} custom-call(s32[8,512]{1,0:T(8,128)} %get-tuple-element.15.place_ref, bf16[1024,768]{1,0:T(8,128)(2,1)} %bitcast.17), custom_call_target="tpu_custom_call" | custom-call | flops 805306368 | bytes 2359296 | tf_op jit(solution)/shard_map/pallas_call | solution.py:335
  (34 shorter events, 0.3 us)
Async XLA Ops:
  6.7 6.3 %copy-start.2 = (bf16[400,768]{1,0:T(8,128)(2,1)S(1)}, bf16[400,768]{1,0:T(8,128)(2,1)}, u32[]{:S(2)}) copy-start(bf16[400,768]{1,0:T(8,128)(2,1)} %get-tuple-element.16.after_ref) | copy-start | bytes 1843204
  6.7 46.9 %all-to-all-start = ((bf16[8,144,768]{2,1,0:T(8,128)(2,1)}), bf16[8,144,768]{2,1,0:T(8,128)(2,1)S(1)}, u32[]{:S(2)}, u32[]{:S(2)}) async-start(bf16[8,144,768]{2,1,0:T(8,128)(2,1)} %shard_map.29), calls=%async_computation | async-start | bytes 3538944 | tf_op jit(solution)/shard_map/all_to_all | solution.py:51
  13.0 55.7 %collective-permute-start = (bf16[400,768]{1,0:T(8,128)(2,1)S(1)}, bf16[400,768]{1,0:T(8,128)(2,1)S(1)}, u32[]{:S(2)}, u32[]{:S(2)}) collective-permute-start(bf16[400,768]{1,0:T(8,128)(2,1)S(1)} %copy-done.2), channel_id=1, source_target_pairs={{0,4},{1,5},{2,6},{3,7},{4,0},{5,1},{6,2},{7,3},{8,12},{9,13},{10,... | collective-permute-start | bytes 1843208 | tf_op jit(solution)/shard_map/ppermute | solution.py:47
  53.7 1.2 copy-start
  68.8 0.8 copy-start.3
  72.7 3.7 %copy-start.7 = (bf16[272,768]{1,0:T(8,128)(2,1)S(1)}, bf16[272,768]{1,0:T(8,128)(2,1)}, u32[]{:S(2)}) copy-start(bf16[272,768]{1,0:T(8,128)(2,1)} %get-tuple-element.19) | copy-start | bytes 1253380
  72.7 30.1 %all-to-all-start.1 = ((bf16[8,96,768]{2,1,0:T(8,128)(2,1)}), bf16[8,96,768]{2,1,0:T(8,128)(2,1)S(1)}, u32[]{:S(2)}, u32[]{:S(2)}) async-start(bf16[8,96,768]{2,1,0:T(8,128)(2,1)} %shard_map.32), calls=%async_computation.1 | async-start | bytes 2359296 | tf_op jit(solution)/shard_map/all_to_all | solution.py:51
  76.4 21.4 %collective-permute-start.2 = (bf16[272,768]{1,0:T(8,128)(2,1)S(1)}, bf16[272,768]{1,0:T(8,128)(2,1)S(1)}, u32[]{:S(2)}, u32[]{:S(2)}) collective-permute-start(bf16[272,768]{1,0:T(8,128)(2,1)S(1)} %copy-done.7), channel_id=1, source_target_pairs={{0,4},{1,5},{2,6},{3,7},{4,0},{5,1},{6,2},{7,3},{8,12},{9,13},{10,... | collective-permute-start | bytes 1253384 | tf_op jit(solution)/shard_map/ppermute | solution.py:47
  76.5 24.7 %collective-permute-start.4 = (bf16[1040,768]{1,0:T(8,128)(2,1)}, bf16[1040,768]{1,0:T(8,128)(2,1)}, u32[]{:S(2)}, u32[]{:S(2)}) collective-permute-start(bf16[1040,768]{1,0:T(8,128)(2,1)} %get-tuple-element.17.refs_0_.refs_2_), channel_id=1, source_target_pairs={{0,8},{1,9},{2,10},{3,11},{4,12},{5,13},{6,14},{7,15},{8,0},{9,1},... | collective-permute-start | bytes 4792328 | tf_op jit(solution)/shard_map/ppermute | solution.py:47
  97.8 16.0 %copy-start.4 = (bf16[272,768]{1,0:T(8,128)(2,1)}, bf16[272,768]{1,0:T(8,128)(2,1)S(1)}, u32[]{:S(2)}) copy-start(bf16[272,768]{1,0:T(8,128)(2,1)S(1)} %collective-permute-done.2.refs_2_) | copy-start | bytes 1253380
  97.8 1.8 %collective-permute-start.3 = (bf16[272,768]{1,0:T(8,128)(2,1)S(1)}, bf16[272,768]{1,0:T(8,128)(2,1)S(1)}, u32[]{:S(2)}, u32[]{:S(2)}) collective-permute-start(bf16[272,768]{1,0:T(8,128)(2,1)S(1)} %collective-permute-done.2.refs_2_), channel_id=1, source_target_pairs={{0,8},{1,9},{2,10},{3,11},{4,12},{5,13},{6,14},{7,15},{8,0},{9,1},... | collective-permute-start | bytes 1253384 | tf_op jit(solution)/shard_map/ppermute | solution.py:47
  99.7 14.1 %copy-start.5 = (bf16[272,768]{1,0:T(8,128)(2,1)}, bf16[272,768]{1,0:T(8,128)(2,1)S(1)}, u32[]{:S(2)}) copy-start(bf16[272,768]{1,0:T(8,128)(2,1)S(1)} %collective-permute-done.3.refs_4_) | copy-start | bytes 1253380
  102.8 11.0 %copy-start.1 = (bf16[8,96,768]{2,1,0:T(8,128)(2,1)}, bf16[8,96,768]{2,1,0:T(8,128)(2,1)S(1)}, u32[]{:S(2)}) copy-start(bf16[8,96,768]{2,1,0:T(8,128)(2,1)S(1)} %all-to-all-done.1) | copy-start | bytes 3538948
  102.8 22.5 %collective-permute-start.1 = (bf16[768,768]{1,0:T(8,128)(2,1)S(1)}, bf16[768,768]{1,0:T(8,128)(2,1)S(1)}, u32[]{:S(2)}, u32[]{:S(2)}) collective-permute-start(bf16[768,768]{1,0:T(8,128)(2,1)S(1)} %bitcast.18), channel_id=1, source_target_pairs={{0,8},{1,9},{2,10},{3,11},{4,12},{5,13},{6,14},{7,15},{8,0},{9,1},... | collective-permute-start | bytes 3538952 | tf_op jit(solution)/shard_map/ppermute | solution.py:47
  125.3 1.0 copy-start.6

commit v3 on v2

v3 whole, which is shorter than its diff:
```python
import functools
import math

import jax
import jax.numpy as jnp
from jax import lax
from jax.experimental import pallas as pl
from jax.experimental.pallas import tpu as pltpu
from jax.sharding import PartitionSpec as P

BPD = 2
CAP = 512
TILE = 16
FACTS = 4
LANES = 128

sharpness = 32.0
epsilon = 1e-06

AXES = ("hx", "hy")
VMEM = pl.BlockSpec(memory_space=pltpu.VMEM)
ANY = pl.BlockSpec(memory_space=pl.ANY)
F32, BF16, I32 = jnp.float32, jnp.bfloat16, jnp.int32


class Plan:
    def __init__(self, nx, ny, files, width, slots):
        self.nx, self.ny, self.files, self.width, self.slots = nx, ny, files, width, slots
        self.devices = nx * ny
        self.cells = self.devices // 4
        self.total = self.cells * slots
        self.known = min(slots, LANES)
        self.core_bit, self.half_bit = ny, ny // 2
        self.groups = [
            [(2 * u + core) * ny + half * (ny // 2) + v for u in range(nx // 2) for v in range(ny // 2)]
            for core in range(2)
            for half in range(2)
        ]


def swapped(value, bit, plan):
    return lax.ppermute(value, AXES, [(i, i ^ bit) for i in range(plan.devices)])


def exchange(value, plan):
    shape = (plan.cells, plan.slots, plan.width)
    return lax.all_to_all(
        value.reshape(shape), AXES, split_axis=0, concat_axis=0, tiled=True, axis_index_groups=plan.groups
    ).reshape(plan.total, plan.width)


def call(kernel, out_shape, args, flops, moved, exps=0, after=(), scratch=()):
    return pl.pallas_call(
        kernel,
        out_shape=out_shape,
        in_specs=[VMEM] * len(args) + [ANY] * len(after),
        out_specs=jax.tree.map(lambda _: VMEM, out_shape),
        scratch_shapes=list(scratch),
        compiler_params=pltpu.CompilerParams(vmem_limit_bytes=56 * 1024 * 1024),
        cost_estimate=pl.CostEstimate(flops=flops, bytes_accessed=moved, transcendentals=exps),
    )(*args, *after)


def iota(shape, dim):
    return lax.broadcasted_iota(I32, shape, dim)


def column(row):
    return jnp.broadcast_to(row, (LANES, row.shape[1])).T


def rows_dot(left, right):
    return lax.dot_general(left, right, (((1,), (1,)), ((), ())), preferred_element_type=F32)


def as_bf16(mask):
    return mask.astype(F32).astype(BF16)


def pack_kernel(plan, bucket_ref, rows_ref, *refs):
    out_ref, place_ref = refs[-2:]
    nx, ny, files, slots, known = plan.nx, plan.ny, plan.files, plan.slots, plan.known
    bucket = bucket_ref[...]
    low_b = ny.bit_length() - 1
    a = bucket >> (low_b + 1)
    b = (bucket >> 1) & (ny - 1)
    c = bucket & 1
    cell = (a & (nx // 2 - 1)) * (ny // 2) + (b & (ny // 2 - 1))
    tag = (a >> (nx.bit_length() - 2)) * 4 + (b >> (low_b - 1)) * 2 + c + 1
    order = cell * files + iota((1, files), 1)
    before = column(order)[:, :1] < order
    same = column(cell)[:, :1] == cell
    index = jnp.sum((before & same).astype(I32), axis=0, keepdims=True)
    over = jnp.max(index, axis=1, keepdims=True) >= slots - 1
    slot = jnp.where(index < slots - 1, cell * slots + index, plan.total)
    place_ref[...] = jnp.broadcast_to(slot, place_ref.shape)

    rows = rows_ref[...]
    wide = rows.astype(F32)
    square = jnp.sum(wide * wide, axis=1, keepdims=True)
    square = jnp.broadcast_to(square, (files, LANES)).T[0:1, :]
    inv = 1.0 / jnp.sqrt(square * (1.0 / plan.width) + epsilon)
    high = inv.astype(BF16).astype(F32)
    middle = (inv - high).astype(BF16).astype(F32)
    low = inv - high - middle
    which = iota((TILE, files), 0)
    facts = jnp.where(
        which == 0,
        tag.astype(F32),
        jnp.where(which == 1, high, jnp.where(which == 2, middle, jnp.where(which == 3, low, 0.0))),
    ).astype(BF16)
    last = iota((TILE, known), 0) == TILE - 1
    flag = jnp.broadcast_to(over.astype(F32), (TILE, LANES))
    for block in range(plan.cells):
        match = as_bf16(iota((slots, files), 0) + block * slots == slot)
        packed = jnp.dot(match, rows, preferred_element_type=F32)
        here = block * slots
        out_ref[here : here + slots, :] = packed.astype(BF16)
        line = rows_dot(facts, match)
        tail = slice(here + slots - TILE, here + slots)
        for fact in range(FACTS):
            lanes = slice(fact * LANES, fact * LANES + known)
            out_ref[tail, lanes] = jnp.where(
                last, line[fact : fact + 1, :known], packed[slots - TILE :, lanes]
            ).astype(BF16)
        lanes = slice(FACTS * LANES, (FACTS + 1) * LANES)
        out_ref[tail, lanes] = jnp.where(
            iota((TILE, LANES), 0) == TILE - 1, flag, packed[slots - TILE :, lanes]
        ).astype(BF16)


def facts_of(plan, ref):
    slots, known = plan.slots, plan.known
    tags, invs = [], []
    for source in range(plan.cells):
        end = (source + 1) * slots
        lines = ref[end - TILE : end, 0 : FACTS * LANES].astype(F32)[TILE - 1 : TILE, :]
        tag, high, middle, low = (
            lines[:, fact * LANES : fact * LANES + known] for fact in range(FACTS)
        )
        tags.append(tag)
        invs.append(high + middle + low)
        if known < slots:
            empty = jnp.zeros((1, slots - known), F32)
            tags.append(empty)
            invs.append(empty)
    return jnp.concatenate(tags, axis=1), jnp.concatenate(invs, axis=1)


def attend_kernel(plan, sets, first, last, *refs):
    refs = list(refs)
    query_ref = refs.pop(0)
    keys = [(refs.pop(0), own) for own in sets]
    if not first:
        old_ref, old_sum_ref = refs.pop(0), refs.pop(0)
    if last:
        out_ref, column_ref = refs
    else:
        out_ref, sum_ref, column_ref = refs
    total, width = plan.total, plan.width
    tag, inv = facts_of(plan, query_ref)
    place = jnp.maximum(tag.astype(I32) - 1, 0)
    bits = (2 << place) | (2 << (place ^ 1)) | (2 << (place ^ 2)) | (2 << (place ^ 4))
    column_ref[0] = column(inv * (sharpness / width * math.log2(math.e)))
    column_ref[1] = column(bits.astype(F32))
    key_facts = []
    for key_ref, own in keys:
        key_tag, key_inv = facts_of(plan, key_ref)
        key_facts.append((1 << key_tag.astype(I32), key_inv))
    chunk = total // 2
    for step in range(2):
        here = slice(step * chunk, (step + 1) * chunk)
        query = query_ref[here, :]
        query_inv = column_ref[0, here, :][:, 0:1]
        query_bits = column_ref[1, here, :][:, 0:1].astype(I32)
        if first:
            numerator = jnp.zeros((chunk, width), F32)
            denominator = jnp.ones((chunk, LANES), F32)
        else:
            numerator, denominator = old_ref[here, :], old_sum_ref[here, :]
        for (key_ref, own), (key_bit, key_inv) in zip(keys, key_facts):
            score = rows_dot(query, key_ref[...]) * query_inv * key_inv
            live = (query_bits & key_bit) != 0
            if own:
                live = live & (iota((chunk, total), 0) + step * chunk != iota((chunk, total), 1))
            kernel = jnp.where(live, jnp.exp2(score), 0.0)
            denominator = denominator + jnp.sum(kernel, axis=1, keepdims=True)
            numerator = numerator + jnp.dot(
                kernel.astype(BF16), key_ref[...], preferred_element_type=F32
            )
        if last:
            out_ref[here, :] = (numerator / denominator[:, 0:1]).astype(BF16)
        else:
            out_ref[here, :] = numerator
            sum_ref[here, :] = denominator


def attend(plan, query, key_sets, old=(), last=False):
    total, width = plan.total, plan.width
    count = len(key_sets) * total
    if last:
        out_shape = jax.ShapeDtypeStruct((total, width), BF16)
    else:
        out_shape = (
            jax.ShapeDtypeStruct((total, width), F32),
            jax.ShapeDtypeStruct((total, LANES), F32),
        )
    return call(
        functools.partial(attend_kernel, plan, [own for _, own in key_sets], not old, last),
        out_shape,
        [query, *(rows for rows, _ in key_sets), *old],
        4 * total * count * width,
        12 * total * width,
        total * count,
        scratch=[pltpu.VMEM((2, total, LANES), F32)],
    )


def unpack_kernel(plan, place_ref, home_ref, out_ref):
    slot = column(place_ref[0:1, :])[:, 0:1]
    match = as_bf16(iota((plan.files, plan.total), 1) == slot)
    out_ref[...] = jnp.dot(match, home_ref[...], preferred_element_type=F32).astype(BF16)


def smooth(plan, embeddings, bucket):
    files, width, total = plan.files, plan.width, plan.total
    bucket = bucket.reshape(1, files)

    def pack(which, rows, after=()):
        return call(
            functools.partial(pack_kernel, plan),
            (
                jax.ShapeDtypeStruct((total, width), BF16),
                jax.ShapeDtypeStruct((8, files), I32),
            ),
            [which, rows],
            2 * total * files * width,
            6 * files * width,
            after=after,
        )

    other_bucket = swapped(bucket, plan.half_bit, plan)
    other_rows = swapped(embeddings, plan.half_bit, plan)
    payload, place = pack(bucket, embeddings, (other_bucket,))
    own = exchange(payload, plan)
    mate = swapped(own, plan.core_bit, plan)
    relayed, _ = pack(other_bucket, other_rows, (own,))
    half = exchange(relayed, plan)
    sums = attend(plan, own, [(own, True), (mate, False)])
    mate_half = swapped(half, plan.core_bit, plan)
    sums = attend(plan, own, [(half, False)], sums)
    smoothed = attend(plan, own, [(mate_half, False)], sums, last=True)
    flags = [
        rows.reshape(plan.cells, plan.slots, width)[:, -1, FACTS * LANES]
        for rows in (own, mate, half, mate_half)
    ]
    return exchange(smoothed, plan), place, jnp.max(jnp.concatenate(flags)) > 0


def unpack(plan, home, place):
    return call(
        functools.partial(unpack_kernel, plan),
        jax.ShapeDtypeStruct((plan.files, plan.width), BF16),
        [place, home],
        2 * plan.total * plan.files * plan.width,
        6 * plan.files * plan.width,
    )


def body(embeddings, bucket):
    nx, ny = lax.axis_size("hx"), lax.axis_size("hy")
    most = 4 * BPD * CAP // (nx * ny)
    short, full = (
        Plan(nx, ny, *embeddings.shape, slots)
        for slots in (max(2 * TILE, most * 7 // 8 // TILE * TILE), most + TILE)
    )
    home, place, over = smooth(short, embeddings, bucket)

    def again(home, place):
        home, place, _ = smooth(full, embeddings, bucket)
        return unpack(full, home, place)

    return lax.cond(over, again, functools.partial(unpack, short), home, place)


def solution(mesh):
    return jax.shard_map(
        body,
        mesh=mesh,
        in_specs=(P(("hx", "hy"), None), P(("hx", "hy"))),
        out_specs=P(("hx", "hy"), None),
        check_vma=False,
    )
```

time: 166 us -> 136 us (0.82)
  blocking collectives: 26.2 us -> 0 us
  Pallas kernels: 56.5 us -> 35.7 us
  waiting for transfers between devices: 60.3 us -> 67.7 us
  starting transfers between devices: 12.9 us -> 19.8 us
  other arithmetic: 1.47 us -> 5.41 us
  local copies, waits for them, and re-layouts: 7.47 us -> 3.71 us
  between operations: 0.16 us -> 2.68 us
    all_to_all x1 -> x0, blocking collectives: 26.2 us -> none  [exchange(): lax.all_to_all(value, AXES, split_axis=0, concat_axis=0, tiled=True, axis...]
    pallas_call x9 -> x6, Pallas kernels: 56.5 us -> 35.7 us  [call(): pl.pallas_call(kernel, out_shape=out_shape, in_specs=[VMEM] * len(args) +...]
    ppermute x5 -> x4, waiting for transfers between devices: 21.5 us -> 34.8 us  [swapped(): lax.ppermute(value, AXES, [(i, i ^ bit) for i in range(plan.devices)])]
    all_to_all x2 -> x3, waiting for transfers between devices: 38.8 us -> 32.9 us  [exchange(): lax.all_to_all(value.reshape(shape), AXES, split_axis=0, concat_axis=0, t...]
    reduce_max x0 -> x4, other arithmetic: none -> 5.41 us  [smooth(): jnp.max(jnp.concatenate(flags)) > 0]
    ppermute x5 -> x4, starting transfers between devices: 2.88 us -> 6.77 us  [swapped(): lax.ppermute(value, AXES, [(i, i ^ bit) for i in range(plan.devices)])]
    all_to_all x2 -> x3, starting transfers between devices: 10 us -> 13 us  [exchange(): lax.all_to_all(value.reshape(shape), AXES, split_axis=0, concat_axis=0, t...]
    reshape x8 -> x0, local copies, waits for them, and re-layouts: 2.86 us -> none  [the longest x4 2.69 us: flat(): return facts.reshape(2, -1)]
  transfers between devices with their start and end apart: 7 -> 7, of which waited for: 4 -> 5; matrix products, arithmetic and copies ran while one was open for 4% -> 4% of each run, Pallas kernels for 21% -> 14%
where the time goes in v3:
time: 136 us; the launch traced here: 135 us
  waiting for transfers between devices  67.7 us (50%)
  Pallas kernels  35.7 us (26%)
  starting transfers between devices  19.8 us (15%)
  other arithmetic  5.41 us (4%)
  local copies, waits for them, and re-layouts  3.71 us (3%)
  between operations  2.68 us (2%)
    pallas_call x6, Pallas kernels, call(): pl.pallas_call(kernel, out_shape=out_shape, in_specs=[VMEM] * len(args) +...  35.7 us
    ppermute x4, waiting for transfers between devices, swapped(): lax.ppermute(value, AXES, [(i, i ^ bit) for i in range(plan.devices)])  34.8 us
    all_to_all x3, waiting for transfers between devices, exchange(): lax.all_to_all(value.reshape(shape), AXES, split_axis=0, concat_axis=0, t...  32.9 us
    all_to_all x3, starting transfers between devices, exchange(): lax.all_to_all(value.reshape(shape), AXES, split_axis=0, concat_axis=0, t...  13 us
    ppermute x4, starting transfers between devices, swapped(): lax.ppermute(value, AXES, [(i, i ^ bit) for i in range(plan.devices)])  6.77 us
    reduce_max x4, other arithmetic, smooth(): jnp.max(jnp.concatenate(flags)) > 0  5.41 us
    unnamed x20, local copies, waits for them, and re-layouts  3.71 us
  transfers between devices with their start and end apart: 7, of which 5 were waited for; matrix products, arithmetic and copies ran while one was open for 4% of the time, Pallas kernels for 14%

profile of v3, /device:TPU:0, one launch (start us, length us, event | category | flops | bytes accessed | tf_op | source)
XLA Modules:
  0.0 135.3 jit_solution(12114514807956494274)
XLA Ops:
  0.0 4.0 %collective-permute-start.4 = (s32[1,512]{1,0:T(1,128)}, s32[1,512]{1,0:T(1,128)S(1)}, u32[]{:S(2)}, u32[]{:S(2)}) collective-permute-start(s32[1,512]{1,0:T(1,128)} %bitcast.41), channel_id=1, source_target_pairs={{0,4},{1,5},{2,6},{3,7},{4,0},{5,1},{6,2},{7,3},{8,12},{9,13},{10,... | collective-permute-start | bytes 6152 | tf_op jit(solution)/shard_map/ppermute | solution.py:42
  4.0 1.8 %collective-permute-done.4.refs_0_.bucket_ref = s32[1,512]{1,0:T(1,128)S(1)} collective-permute-done((s32[1,512]{1,0:T(1,128)}, s32[1,512]{1,0:T(1,128)S(1)}, u32[]{:S(2)}, u32[]{:S(2)}) %collective-permute-start.4) | collective-permute-done | bytes 2080 | tf_op jit(solution)/shard_map/ppermute | solution.py:42
  5.8 0.6 copy-done.12
  6.4 4.1 %shard_map.30 = (bf16[896,768]{1,0:T(8,128)(2,1)}, s32[8,512]{1,0:T(8,128)}) custom-call(s32[1,512]{1,0:T(1,128)} %bitcast.42, bf16[512,768]{1,0:T(8,128)(2,1)} %rows_ref.1, s32[1,512]{1,0:T(1,128)} %copy-done.12), custom_call_target="tpu_custom_call" | custom-call | flops 704643072 | bytes 2359296 | tf_op jit(solution)/shard_map/pallas_call | solution.py:53
  10.5 5.2 %all-to-all-start.3 = ((bf16[8,112,768]{2,1,0:T(8,128)(2,1)}), bf16[8,112,768]{2,1,0:T(8,128)(2,1)S(1)}, u32[]{:S(2)}, u32[]{:S(2)}) async-start(bf16[8,112,768]{2,1,0:T(8,128)(2,1)} %bitcast.38), calls=%async_computation.3 | async-start | bytes 2752512 | tf_op jit(solution)/shard_map/all_to_all | solution.py:47
  15.7 2.7 %collective-permute-start.6 = (bf16[512,768]{1,0:T(8,128)(2,1)S(1)}, bf16[512,768]{1,0:T(8,128)(2,1)S(1)}, u32[]{:S(2)}, u32[]{:S(2)}) collective-permute-start(bf16[512,768]{1,0:T(8,128)(2,1)S(1)} %copy-done.8), channel_id=1, source_target_pairs={{0,4},{1,5},{2,6},{3,7},{4,0},{5,1},{6,2},{7,3},{8,12},{9,13},{10,... | collective-permute-start | bytes 2359304 | tf_op jit(solution)/shard_map/ppermute | solution.py:42
  18.4 33.1 %collective-permute-done.6.rows_ref = bf16[512,768]{1,0:T(8,128)(2,1)S(1)} collective-permute-done((bf16[512,768]{1,0:T(8,128)(2,1)S(1)}, bf16[512,768]{1,0:T(8,128)(2,1)S(1)}, u32[]{:S(2)}, u32[]{:S(2)}) %collective-permute-start.6) | collective-permute-done | bytes 786464 | tf_op jit(solution)/shard_map/ppermute | solution.py:42
  51.4 0.3 all-to-all-done.3
  51.7 0.6 copy-done.9
  52.3 0.5 copy-done.3
  52.8 4.1 %shard_map.31 = (bf16[896,768]{1,0:T(8,128)(2,1)}, s32[8,512]{1,0:T(8,128)}) custom-call(s32[1,512]{1,0:T(1,128)} %copy-done.12, bf16[512,768]{1,0:T(8,128)(2,1)} %copy-done.9, bf16[896,768]{1,0:T(8,128)(2,1)} %bitcast.28), custom_call_target="tpu_custom_call" | custom-call | flops 704643072 | bytes 2359296 | tf_op jit(solution)/shard_map/pallas_call | solution.py:53
  56.9 4.1 %all-to-all-start.4 = ((bf16[8,112,768]{2,1,0:T(8,128)(2,1)}), bf16[8,112,768]{2,1,0:T(8,128)(2,1)S(1)}, u32[]{:S(2)}, u32[]{:S(2)}) async-start(bf16[8,112,768]{2,1,0:T(8,128)(2,1)} %bitcast.39), calls=%async_computation.4 | async-start | bytes 2752512 | tf_op jit(solution)/shard_map/all_to_all | solution.py:47
  61.0 0.0 copy-done.4
  61.0 0.1 collective-permute-start.5
  61.1 18.5 %all-to-all-done.4 = bf16[8,112,768]{2,1,0:T(8,128)(2,1)S(1)} async-done(((bf16[8,112,768]{2,1,0:T(8,128)(2,1)}), bf16[8,112,768]{2,1,0:T(8,128)(2,1)S(1)}, u32[]{:S(2)}, u32[]{:S(2)}) %all-to-all-start.4) | async-done | bytes 1376288 | tf_op jit(solution)/shard_map/all_to_all | solution.py:47
  79.6 0.0 collective-permute-start.7
  79.6 0.0 collective-permute-done.5.refs_2_
  79.6 11.2 %shard_map.32 = (f32[896,768]{1,0:T(8,128)}, f32[896,128]{1,0:T(8,128)}) custom-call(bf16[896,768]{1,0:T(8,128)(2,1)} %bitcast.29, bf16[896,768]{1,0:T(8,128)(2,1)} %bitcast.30, bf16[896,768]{1,0:T(8,128)(2,1)} %collective-permute-done.5.refs_2_), custom_call_target="tpu_custom_call" | custom-call | flops 4932501504 | bytes 8257536 | tf_op jit(solution)/shard_map/pallas_call | solution.py:53
  90.8 7.6 %shard_map.33 = (f32[896,768]{1,0:T(8,128)}, f32[896,128]{1,0:T(8,128)}) custom-call(bf16[896,768]{1,0:T(8,128)(2,1)} %bitcast.31, bf16[896,768]{1,0:T(8,128)(2,1)} %bitcast.35, f32[896,768]{1,0:T(8,128)} %get-tuple-element.37.refs_2_, f32[896,128]{1,0:T(8,128)} %get-tuple-element.38.refs_3_), custom_call_target="tpu_custom_call" | custom-call | flops 2466250752 | bytes 8257536 | tf_op jit(solution)/shard_map/pallas_call | solution.py:53
  98.4 0.0 collective-permute-done.7.refs_1_
  98.4 1.1 copy-done.6
  99.5 7.4 %shard_map.34 = bf16[896,768]{1,0:T(8,128)(2,1)} custom-call(bf16[896,768]{1,0:T(8,128)(2,1)} %bitcast.32, bf16[896,768]{1,0:T(8,128)(2,1)} %copy-done.6, f32[896,768]{1,0:T(8,128)} %get-tuple-element.39.refs_2_, f32[896,128]{1,0:T(8,128)} %get-tuple-element.40.refs_3_), custom_call_target="tpu_custom_call" | custom-call | flops 2466250752 | bytes 8257536 | tf_op jit(solution)/shard_map/pallas_call | solution.py:53
  106.9 3.7 %all-to-all-start.5 = ((bf16[8,112,768]{2,1,0:T(8,128)(2,1)}), bf16[8,112,768]{2,1,0:T(8,128)(2,1)S(1)}, u32[]{:S(2)}, u32[]{:S(2)}) async-start(bf16[8,112,768]{2,1,0:T(8,128)(2,1)} %bitcast.37), calls=%async_computation.5 | async-start | bytes 2752512 | tf_op jit(solution)/shard_map/all_to_all | solution.py:47
  110.6 1.3 slice_reduce_fusion.3
  112.0 1.4 %slice_reduce_fusion.2 = bf16[]{:T(256)} fusion(bf16[8,112,768]{2,1,0:T(8,128)(2,1)} %bitcast.11), kind=kLoop, calls=%fused_computation.2 | loop fusion | flops 7 | bytes 18 | tf_op jit(solution)/shard_map/reduce_max | solution.py:257
  114.7 1.3 slice_reduce_fusion.1
  116.7 1.3 slice_reduce_fusion
  118.7 14.2 %all-to-all-done.5 = bf16[8,112,768]{2,1,0:T(8,128)(2,1)S(1)} async-done(((bf16[8,112,768]{2,1,0:T(8,128)(2,1)}), bf16[8,112,768]{2,1,0:T(8,128)(2,1)S(1)}, u32[]{:S(2)}, u32[]{:S(2)}) %all-to-all-start.5) | async-done | bytes 1376288 | tf_op jit(solution)/shard_map/all_to_all | solution.py:47
  132.8 1.6 %conditional.1 = (bf16[512,768]{1,0:T(8,128)(2,1)S(1)}) conditional(s32[]{:T(128)} %convert_element_type.3, (bf16[8,112,768]{2,1,0:T(8,128)(2,1)S(1)}, s32[8,512]{1,0:T(8,128)S(1)}) %tuple.20, (s32[512]{0:T(512)S(1)}, bf16[512,768]{1,0:T(8,128)(2,1)S(1)}) %tuple.18), branch_computations={%region_4.5_spmd, %region_5.6_spmd} | conditional | flops 19025362944 | bytes 101859728 | solution.py:283
  132.8 1.3 branch_0_fun.1
  134.4 0.0 copy-start.14
  134.4 0.9 copy-done.14
  (13 shorter events, 0.0 us)
Async XLA Ops:
  0.0 5.8 %collective-permute-start.4 = (s32[1,512]{1,0:T(1,128)}, s32[1,512]{1,0:T(1,128)S(1)}, u32[]{:S(2)}, u32[]{:S(2)}) collective-permute-start(s32[1,512]{1,0:T(1,128)} %bitcast.41), channel_id=1, source_target_pairs={{0,4},{1,5},{2,6},{3,7},{4,0},{5,1},{6,2},{7,3},{8,12},{9,13},{10,... | collective-permute-start | bytes 6152 | tf_op jit(solution)/shard_map/ppermute | solution.py:42
  5.8 0.6 copy-start.12
  10.5 5.2 %copy-start.8 = (bf16[512,768]{1,0:T(8,128)(2,1)S(1)}, bf16[512,768]{1,0:T(8,128)(2,1)}, u32[]{:S(2)}) copy-start(bf16[512,768]{1,0:T(8,128)(2,1)} %rows_ref.1) | copy-start | bytes 2359300
  10.5 41.2 %all-to-all-start.3 = ((bf16[8,112,768]{2,1,0:T(8,128)(2,1)}), bf16[8,112,768]{2,1,0:T(8,128)(2,1)S(1)}, u32[]{:S(2)}, u32[]{:S(2)}) async-start(bf16[8,112,768]{2,1,0:T(8,128)(2,1)} %bitcast.38), calls=%async_computation.3 | async-start | bytes 2752512 | tf_op jit(solution)/shard_map/all_to_all | solution.py:47
  15.7 35.7 %collective-permute-start.6 = (bf16[512,768]{1,0:T(8,128)(2,1)S(1)}, bf16[512,768]{1,0:T(8,128)(2,1)S(1)}, u32[]{:S(2)}, u32[]{:S(2)}) collective-permute-start(bf16[512,768]{1,0:T(8,128)(2,1)S(1)} %copy-done.8), channel_id=1, source_target_pairs={{0,4},{1,5},{2,6},{3,7},{4,0},{5,1},{6,2},{7,3},{8,12},{9,13},{10,... | collective-permute-start | bytes 2359304 | tf_op jit(solution)/shard_map/ppermute | solution.py:42
  51.4 0.9 copy-start.9
  51.7 1.1 copy-start.3
  56.9 4.1 %copy-start.4 = (bf16[8,112,768]{2,1,0:T(8,128)(2,1)S(1)}, bf16[8,112,768]{2,1,0:T(8,128)(2,1)}, u32[]{:S(2)}) copy-start(bf16[8,112,768]{2,1,0:T(8,128)(2,1)} %copy-done.3) | copy-start | bytes 4128772
  56.9 22.6 %all-to-all-start.4 = ((bf16[8,112,768]{2,1,0:T(8,128)(2,1)}), bf16[8,112,768]{2,1,0:T(8,128)(2,1)S(1)}, u32[]{:S(2)}, u32[]{:S(2)}) async-start(bf16[8,112,768]{2,1,0:T(8,128)(2,1)} %bitcast.39), calls=%async_computation.4 | async-start | bytes 2752512 | tf_op jit(solution)/shard_map/all_to_all | solution.py:47
  61.0 18.5 %collective-permute-start.5 = (bf16[896,768]{1,0:T(8,128)(2,1)S(1)}, bf16[896,768]{1,0:T(8,128)(2,1)}, u32[]{:S(2)}, u32[]{:S(2)}) collective-permute-start(bf16[896,768]{1,0:T(8,128)(2,1)S(1)} %bitcast.33), channel_id=1, source_target_pairs={{0,8},{1,9},{2,10},{3,11},{4,12},{5,13},{6,14},{7,15},{8,0},{9,1},... | collective-permute-start | bytes 4128776 | tf_op jit(solution)/shard_map/ppermute | solution.py:42
  79.6 11.2 %copy-start.5 = (bf16[8,112,768]{2,1,0:T(8,128)(2,1)}, bf16[8,112,768]{2,1,0:T(8,128)(2,1)S(1)}, u32[]{:S(2)}) copy-start(bf16[8,112,768]{2,1,0:T(8,128)(2,1)S(1)} %all-to-all-done.4) | copy-start | bytes 4128772
  79.6 18.8 %collective-permute-start.7 = (bf16[896,768]{1,0:T(8,128)(2,1)S(1)}, bf16[896,768]{1,0:T(8,128)(2,1)S(1)}, u32[]{:S(2)}, u32[]{:S(2)}) collective-permute-start(bf16[896,768]{1,0:T(8,128)(2,1)S(1)} %bitcast.34), channel_id=1, source_target_pairs={{0,8},{1,9},{2,10},{3,11},{4,12},{5,13},{6,14},{7,15},{8,0},{9,1},... | collective-permute-start | bytes 4128776 | tf_op jit(solution)/shard_map/ppermute | solution.py:42
  98.4 1.1 copy-start.6
  106.9 25.9 %copy-start.11 = (s32[512]{0:T(512)S(1)}, s32[512]{0:T(512)}, u32[]{:S(2)}) copy-start(s32[512]{0:T(512)} %param.5) | copy-start | bytes 6148
  106.9 25.9 %copy-start.15 = (s32[8,512]{1,0:T(8,128)S(1)}, s32[8,512]{1,0:T(8,128)}, u32[]{:S(2)}) copy-start(s32[8,512]{1,0:T(8,128)} %get-tuple-element.41) | copy-start | bytes 49156
  106.9 25.9 %all-to-all-start.5 = ((bf16[8,112,768]{2,1,0:T(8,128)(2,1)}), bf16[8,112,768]{2,1,0:T(8,128)(2,1)S(1)}, u32[]{:S(2)}, u32[]{:S(2)}) async-start(bf16[8,112,768]{2,1,0:T(8,128)(2,1)} %bitcast.37), calls=%async_computation.5 | async-start | bytes 2752512 | tf_op jit(solution)/shard_map/all_to_all | solution.py:47
  134.4 0.9 copy-start.14

commit v4 on v3

--- a/solution.py
+++ b/solution.py
@@ -49,14 +49,14 @@
     ).reshape(plan.total, plan.width)
 
 
-def call(kernel, out_shape, args, flops, moved, exps=0, after=(), scratch=()):
+def call(kernel, out_shape, args, flops, moved, exps=0, after=(), scratch=(), limit=12):
     return pl.pallas_call(
         kernel,
         out_shape=out_shape,
         in_specs=[VMEM] * len(args) + [ANY] * len(after),
         out_specs=jax.tree.map(lambda _: VMEM, out_shape),
         scratch_shapes=list(scratch),
-        compiler_params=pltpu.CompilerParams(vmem_limit_bytes=56 * 1024 * 1024),
+        compiler_params=pltpu.CompilerParams(vmem_limit_bytes=limit * 1024 * 1024),
         cost_estimate=pl.CostEstimate(flops=flops, bytes_accessed=moved, transcendentals=exps),
     )(*args, *after)
 
@@ -131,10 +131,11 @@
 
 def facts_of(plan, ref):
     slots, known = plan.slots, plan.known
-    tags, invs = [], []
+    tags, invs, over = [], [], jnp.zeros((1, LANES), F32)
     for source in range(plan.cells):
         end = (source + 1) * slots
-        lines = ref[end - TILE : end, 0 : FACTS * LANES].astype(F32)[TILE - 1 : TILE, :]
+        lines = ref[end - TILE : end, 0 : (FACTS + 1) * LANES].astype(F32)[TILE - 1 : TILE, :]
+        over = jnp.maximum(over, lines[:, FACTS * LANES :])
         tag, high, middle, low = (
             lines[:, fact * LANES : fact * LANES + known] for fact in range(FACTS)
         )
@@ -144,7 +145,7 @@
             empty = jnp.zeros((1, slots - known), F32)
             tags.append(empty)
             invs.append(empty)
-    return jnp.concatenate(tags, axis=1), jnp.concatenate(invs, axis=1)
+    return jnp.concatenate(tags, axis=1), jnp.concatenate(invs, axis=1), over
 
 
 def attend_kernel(plan, sets, first, last, *refs):
@@ -152,21 +153,26 @@
     query_ref = refs.pop(0)
     keys = [(refs.pop(0), own) for own in sets]
     if not first:
-        old_ref, old_sum_ref = refs.pop(0), refs.pop(0)
+        old_over_ref, old_ref, old_sum_ref = refs[:3]
+        del refs[:3]
     if last:
-        out_ref, column_ref = refs
+        over_ref, out_ref, column_ref = refs
     else:
-        out_ref, sum_ref, column_ref = refs
+        over_ref, out_ref, sum_ref, column_ref = refs
     total, width = plan.total, plan.width
-    tag, inv = facts_of(plan, query_ref)
+    tag, inv, over = facts_of(plan, query_ref)
+    if not first:
+        over = jnp.maximum(over, old_over_ref[0:1, :])
     place = jnp.maximum(tag.astype(I32) - 1, 0)
     bits = (2 << place) | (2 << (place ^ 1)) | (2 << (place ^ 2)) | (2 << (place ^ 4))
     column_ref[0] = column(inv * (sharpness / width * math.log2(math.e)))
     column_ref[1] = column(bits.astype(F32))
     key_facts = []
     for key_ref, own in keys:
-        key_tag, key_inv = facts_of(plan, key_ref)
+        key_tag, key_inv, key_over = facts_of(plan, key_ref)
         key_facts.append((1 << key_tag.astype(I32), key_inv))
+        over = jnp.maximum(over, key_over)
+    over_ref[...] = jnp.broadcast_to(over, over_ref.shape)
     chunk = total // 2
     for step in range(2):
         here = slice(step * chunk, (step + 1) * chunk)
@@ -195,13 +201,15 @@
             sum_ref[here, :] = denominator
 
 
-def attend(plan, query, key_sets, old=(), last=False):
+def attend(plan, query, key_sets, old=(), last=False, weight=1):
     total, width = plan.total, plan.width
     count = len(key_sets) * total
+    flag = jax.ShapeDtypeStruct((8, LANES), F32)
     if last:
-        out_shape = jax.ShapeDtypeStruct((total, width), BF16)
+        out_shape = (flag, jax.ShapeDtypeStruct((total, width), BF16))
     else:
         out_shape = (
+            flag,
             jax.ShapeDtypeStruct((total, width), F32),
             jax.ShapeDtypeStruct((total, LANES), F32),
         )
@@ -209,10 +217,11 @@
         functools.partial(attend_kernel, plan, [own for _, own in key_sets], not old, last),
         out_shape,
         [query, *(rows for rows, _ in key_sets), *old],
-        4 * total * count * width,
+        weight * 4 * total * count * width,
         12 * total * width,
         total * count,
         scratch=[pltpu.VMEM((2, total, LANES), F32)],
+        limit=18,
     )
 
 
@@ -241,20 +250,16 @@
 
     other_bucket = swapped(bucket, plan.half_bit, plan)
     other_rows = swapped(embeddings, plan.half_bit, plan)
-    payload, place = pack(bucket, embeddings, (other_bucket,))
+    payload, place = pack(bucket, embeddings)
     own = exchange(payload, plan)
     mate = swapped(own, plan.core_bit, plan)
     relayed, _ = pack(other_bucket, other_rows, (own,))
     half = exchange(relayed, plan)
     sums = attend(plan, own, [(own, True), (mate, False)])
     mate_half = swapped(half, plan.core_bit, plan)
-    sums = attend(plan, own, [(half, False)], sums)
-    smoothed = attend(plan, own, [(mate_half, False)], sums, last=True)
-    flags = [
-        rows.reshape(plan.cells, plan.slots, width)[:, -1, FACTS * LANES]
-        for rows in (own, mate, half, mate_half)
-    ]
-    return exchange(smoothed, plan), place, jnp.max(jnp.concatenate(flags)) > 0
+    sums = attend(plan, own, [(half, False)], sums, weight=40)
+    over, smoothed = attend(plan, own, [(mate_half, False)], sums, last=True)
+    return exchange(smoothed, plan), place, over[0, 0] > 0
 
 
 def unpack(plan, home, place):

time: 136 us -> 113 us (0.83)
  Pallas kernels: 35.7 us -> 23.7 us
  other arithmetic: 5.41 us -> 0 us
  starting transfers between devices: 19.8 us -> 16.8 us
  between operations: 2.68 us -> 0.73 us
    pallas_call x6, Pallas kernels: 35.7 us -> 23.7 us  [call(): pl.pallas_call(kernel, out_shape=out_shape, in_specs=[VMEM] * len(args) +...]
    reduce_max x4 -> x0, other arithmetic: 5.41 us -> none  [smooth(): jnp.max(jnp.concatenate(flags)) > 0]
    ppermute x4, starting transfers between devices: 6.77 us -> 3.05 us  [swapped(): lax.ppermute(value, AXES, [(i, i ^ bit) for i in range(plan.devices)])]
    all_to_all x3, waiting for transfers between devices: 32.9 us -> 29.4 us  [exchange(): lax.all_to_all(value.reshape(shape), AXES, split_axis=0, concat_axis=0, t...]
    ppermute x4, waiting for transfers between devices: 34.8 us -> 37.1 us  [swapped(): lax.ppermute(value, AXES, [(i, i ^ bit) for i in range(plan.devices)])]
    unnamed x20 -> x12, local copies, waits for them, and re-layouts: 3.71 us -> 4.37 us
  transfers between devices with their start and end apart: 7 -> 7, of which waited for: 5 -> 5; matrix products, arithmetic and copies ran while one was open for 4% -> 0% of each run, Pallas kernels for 14% -> 9%
where the time goes in v4:
time: 113 us
  waiting for transfers between devices  66.5 us (59%)
  Pallas kernels  23.7 us (21%)
  starting transfers between devices  16.8 us (15%)
  local copies, waits for them, and re-layouts  4.89 us (4%)
    ppermute x4, waiting for transfers between devices, swapped(): lax.ppermute(value, AXES, [(i, i ^ bit) for i in range(plan.devices)])  37.1 us
    all_to_all x3, waiting for transfers between devices, exchange(): lax.all_to_all(value.reshape(shape), AXES, split_axis=0, concat_axis=0, t...  29.4 us
    pallas_call x6, Pallas kernels, call(): pl.pallas_call(kernel, out_shape=out_shape, in_specs=[VMEM] * len(args) +...  23.7 us
    all_to_all x3, starting transfers between devices, exchange(): lax.all_to_all(value.reshape(shape), AXES, split_axis=0, concat_axis=0, t...  13.8 us
    unnamed x12, local copies, waits for them, and re-layouts  4.37 us
    ppermute x4, starting transfers between devices, swapped(): lax.ppermute(value, AXES, [(i, i ^ bit) for i in range(plan.devices)])  3.05 us
  transfers between devices with their start and end apart: 7, of which 5 were waited for; matrix products, arithmetic and copies ran while one was open for 0% of the time, Pallas kernels for 9%

profile of v4, /device:TPU:0, one launch (start us, length us, event | category | flops | bytes accessed | tf_op | source)
XLA Modules:
  0.0 112.7 jit_solution(3157428773080559882)
XLA Ops:
  0.0 4.2 %shard_map.30 = (bf16[896,768]{1,0:T(8,128)(2,1)}, s32[8,512]{1,0:T(8,128)S(1)}) custom-call(s32[1,512]{1,0:T(1,128)} %bitcast.33, bf16[512,768]{1,0:T(8,128)(2,1)} %rows_ref.1), custom_call_target="tpu_custom_call" | custom-call | flops 704643072 | bytes 2359296 | tf_op jit(solution)/shard_map/pallas_call | solution.py:53
  4.2 0.0 copy-start.5
  4.2 0.0 copy-start.7
  4.2 6.3 %all-to-all-start.3 = ((bf16[8,112,768]{2,1,0:T(8,128)(2,1)}), bf16[8,112,768]{2,1,0:T(8,128)(2,1)S(1)}, u32[]{:S(2)}, u32[]{:S(2)}) async-start(bf16[8,112,768]{2,1,0:T(8,128)(2,1)} %bitcast.9), calls=%async_computation.3 | async-start | bytes 2752512 | tf_op jit(solution)/shard_map/all_to_all | solution.py:47
  10.5 0.0 copy-done.5
  10.5 2.7 %collective-permute-start.5 = (bf16[512,768]{1,0:T(8,128)(2,1)S(1)}, bf16[512,768]{1,0:T(8,128)(2,1)S(1)}, u32[]{:S(2)}, u32[]{:S(2)}) collective-permute-start(bf16[512,768]{1,0:T(8,128)(2,1)S(1)} %copy-done.5), channel_id=1, source_target_pairs={{0,4},{1,5},{2,6},{3,7},{4,0},{5,1},{6,2},{7,3},{8,12},{9,13},{10,... | collective-permute-start | bytes 2359304 | tf_op jit(solution)/shard_map/ppermute | solution.py:42
  13.1 0.0 copy-done.7
  13.1 0.3 collective-permute-start.4
  13.5 34.0 %collective-permute-done.4.bucket_ref = s32[1,512]{1,0:T(1,128)S(1)} collective-permute-done((s32[1,512]{1,0:T(1,128)S(1)}, s32[1,512]{1,0:T(1,128)S(1)}, u32[]{:S(2)}, u32[]{:S(2)}) %collective-permute-start.4) | collective-permute-done | bytes 2080 | tf_op jit(solution)/shard_map/ppermute | solution.py:42
  47.4 0.0 collective-permute-done.5.rows_ref
  47.4 0.2 all-to-all-done.3
  47.6 1.9 %shard_map.31 = (bf16[896,768]{1,0:T(8,128)(2,1)S(1)}, s32[8,512]{1,0:T(8,128)}) custom-call(s32[1,512]{1,0:T(1,128)S(1)} %collective-permute-done.4.bucket_ref, bf16[512,768]{1,0:T(8,128)(2,1)S(1)} %collective-permute-done.5.rows_ref, bf16[896,768]{1,0:T(8,128)(2,1)S(1)} %bitcast.23), custom_call_target="tpu_custom_call" | custom-call | flops 704643072 | bytes 2359296 | tf_op jit(solution)/shard_map/pallas_call | solution.py:53
  49.5 0.0 copy-start
  49.5 1.1 copy-done
  50.6 3.8 %all-to-all-start.4 = ((bf16[8,112,768]{2,1,0:T(8,128)(2,1)}), bf16[8,112,768]{2,1,0:T(8,128)(2,1)S(1)}, u32[]{:S(2)}, u32[]{:S(2)}) async-start(bf16[8,112,768]{2,1,0:T(8,128)(2,1)} %bitcast.31), calls=%async_computation.4 | async-start | bytes 2752512 | tf_op jit(solution)/shard_map/all_to_all | solution.py:47
  54.4 0.1 collective-permute-start.7
  54.5 3.1 %collective-permute-done.7.refs_2_ = bf16[896,768]{1,0:T(8,128)(2,1)S(1)} collective-permute-done((bf16[896,768]{1,0:T(8,128)(2,1)S(1)}, bf16[896,768]{1,0:T(8,128)(2,1)S(1)}, u32[]{:S(2)}, u32[]{:S(2)}) %collective-permute-start.7) | collective-permute-done | bytes 1376288 | tf_op jit(solution)/shard_map/ppermute | solution.py:42
  57.6 7.1 %shard_map.32 = (f32[8,128]{1,0:T(8,128)S(1)}, f32[896,768]{1,0:T(8,128)S(1)}, f32[896,128]{1,0:T(8,128)S(1)}) custom-call(bf16[896,768]{1,0:T(8,128)(2,1)S(1)} %bitcast.25, bf16[896,768]{1,0:T(8,128)(2,1)S(1)} %bitcast.26, bf16[896,768]{1,0:T(8,128)(2,1)S(1)} %collective-permute-done.7.refs_2_), custom_call_target="tpu_custom_call" | custom-call | flops 4932501504 | bytes 8257536 | tf_op jit(solution)/shard_map/pallas_call | solution.py:53
  64.7 0.0 copy-start.1
  64.7 1.5 %copy-done.1 = f32[896,768]{1,0:T(8,128)} copy-done((f32[896,768]{1,0:T(8,128)}, f32[896,768]{1,0:T(8,128)S(1)}, u32[]{:S(2)}) %copy-start.1) | copy-done | bytes 2752536
  66.2 6.7 %all-to-all-done.4 = bf16[8,112,768]{2,1,0:T(8,128)(2,1)S(1)} async-done(((bf16[8,112,768]{2,1,0:T(8,128)(2,1)}), bf16[8,112,768]{2,1,0:T(8,128)(2,1)S(1)}, u32[]{:S(2)}, u32[]{:S(2)}) %all-to-all-start.4) | async-done | bytes 1376288 | tf_op jit(solution)/shard_map/all_to_all | solution.py:47
  73.0 0.0 collective-permute-start.6
  73.0 1.8 %copy-done.2 = f32[896,768]{1,0:T(8,128)S(1)} copy-done((f32[896,768]{1,0:T(8,128)S(1)}, f32[896,768]{1,0:T(8,128)}, u32[]{:S(2)}) %copy-start.2) | copy-done | bytes 2752536
  74.7 3.4 %shard_map.33 = (f32[8,128]{1,0:T(8,128)S(1)}, f32[896,768]{1,0:T(8,128)S(1)}, f32[896,128]{1,0:T(8,128)S(1)}) custom-call(bf16[896,768]{1,0:T(8,128)(2,1)S(1)} %bitcast.27, bf16[896,768]{1,0:T(8,128)(2,1)S(1)} %bitcast.30, f32[8,128]{1,0:T(8,128)S(1)} %get-tuple-element.44.refs_2_, f32[896,768]{1,0:T(8,128)S(1)} %copy-done.2, ...), custom_call_target="tpu_custom_call" | custom-call | flops 98650030080 | bytes 8257536 | tf_op jit(solution)/shard_map/pallas_call | solution.py:53
  78.1 0.0 collective-permute-done.6.refs_1_
  78.2 5.0 %shard_map.34 = (f32[8,128]{1,0:T(8,128)S(1)}, bf16[896,768]{1,0:T(8,128)(2,1)}) custom-call(bf16[896,768]{1,0:T(8,128)(2,1)S(1)} %bitcast.28, bf16[896,768]{1,0:T(8,128)(2,1)S(1)} %collective-permute-done.6.refs_1_, f32[8,128]{1,0:T(8,128)S(1)} %get-tuple-element.47.refs_2_, f32[896,768]{1,0:T(8,128)S(1)} %get-tuple-element.48.refs_3_, ...), custom_call_target="tpu_custom_call" | custom-call | flops 2466250752 | bytes 8257536 | tf_op jit(solution)/shard_map/pallas_call | solution.py:53
  83.1 3.7 %all-to-all-start.5 = ((bf16[8,112,768]{2,1,0:T(8,128)(2,1)}), bf16[8,112,768]{2,1,0:T(8,128)(2,1)S(1)}, u32[]{:S(2)}, u32[]{:S(2)}) async-start(bf16[8,112,768]{2,1,0:T(8,128)(2,1)} %bitcast.14), calls=%async_computation.5 | async-start | bytes 2752512 | tf_op jit(solution)/shard_map/all_to_all | solution.py:47
  86.9 0.5 slice.3
  88.0 22.5 %all-to-all-done.5 = bf16[8,112,768]{2,1,0:T(8,128)(2,1)S(1)} async-done(((bf16[8,112,768]{2,1,0:T(8,128)(2,1)}), bf16[8,112,768]{2,1,0:T(8,128)(2,1)S(1)}, u32[]{:S(2)}, u32[]{:S(2)}) %all-to-all-start.5) | async-done | bytes 1376288 | tf_op jit(solution)/shard_map/all_to_all | solution.py:47
  110.5 0.0 copy-done.6
  110.5 2.2 %conditional.1 = (bf16[512,768]{1,0:T(8,128)(2,1)}) conditional(s32[]{:T(128)} %bitcast.13, (bf16[8,112,768]{2,1,0:T(8,128)(2,1)S(1)}, s32[8,512]{1,0:T(8,128)S(1)}) %tuple.11, (s32[512]{0:T(512)S(1)}, bf16[512,768]{1,0:T(8,128)(2,1)S(1)}) %tuple.18), branch_computations={%region_0.0_spmd, %region_1.0_spmd} | conditional | flops 178023038976 | bytes 98705696 | solution.py:288
  110.5 2.2 %branch_0_fun.1 = bf16[512,768]{1,0:T(8,128)(2,1)} custom-call(s32[8,512]{1,0:T(8,128)S(1)} %get-tuple-element.17.place_ref, bf16[896,768]{1,0:T(8,128)(2,1)S(1)} %bitcast.32), custom_call_target="tpu_custom_call" | custom-call | flops 704643072 | bytes 2359296 | tf_op jit(solution)/shard_map/cond/branch_0_fun/pallas_call | solution.py:53
  (2 shorter events, 0.0 us)
Async XLA Ops:
  4.2 6.3 %copy-start.5 = (bf16[512,768]{1,0:T(8,128)(2,1)S(1)}, bf16[512,768]{1,0:T(8,128)(2,1)}, u32[]{:S(2)}) copy-start(bf16[512,768]{1,0:T(8,128)(2,1)} %rows_ref.1) | copy-start | bytes 2359300
  4.2 9.0 %copy-start.7 = (s32[512]{0:T(512)S(1)}, s32[512]{0:T(512)}, u32[]{:S(2)}) copy-start(s32[512]{0:T(512)} %param.5) | copy-start | bytes 6148
  4.2 43.5 %all-to-all-start.3 = ((bf16[8,112,768]{2,1,0:T(8,128)(2,1)}), bf16[8,112,768]{2,1,0:T(8,128)(2,1)S(1)}, u32[]{:S(2)}, u32[]{:S(2)}) async-start(bf16[8,112,768]{2,1,0:T(8,128)(2,1)} %bitcast.9), calls=%async_computation.3 | async-start | bytes 2752512 | tf_op jit(solution)/shard_map/all_to_all | solution.py:47
  10.5 37.0 %collective-permute-start.5 = (bf16[512,768]{1,0:T(8,128)(2,1)S(1)}, bf16[512,768]{1,0:T(8,128)(2,1)S(1)}, u32[]{:S(2)}, u32[]{:S(2)}) collective-permute-start(bf16[512,768]{1,0:T(8,128)(2,1)S(1)} %copy-done.5), channel_id=1, source_target_pairs={{0,4},{1,5},{2,6},{3,7},{4,0},{5,1},{6,2},{7,3},{8,12},{9,13},{10,... | collective-permute-start | bytes 2359304 | tf_op jit(solution)/shard_map/ppermute | solution.py:42
  13.1 34.3 %collective-permute-start.4 = (s32[1,512]{1,0:T(1,128)S(1)}, s32[1,512]{1,0:T(1,128)S(1)}, u32[]{:S(2)}, u32[]{:S(2)}) collective-permute-start(s32[1,512]{1,0:T(1,128)S(1)} %bitcast.34), channel_id=1, source_target_pairs={{0,4},{1,5},{2,6},{3,7},{4,0},{5,1},{6,2},{7,3},{8,12},{9,13},{10,... | collective-permute-start | bytes 6152 | tf_op jit(solution)/shard_map/ppermute | solution.py:42
  49.5 1.1 copy-start
  50.6 22.3 %all-to-all-start.4 = ((bf16[8,112,768]{2,1,0:T(8,128)(2,1)}), bf16[8,112,768]{2,1,0:T(8,128)(2,1)S(1)}, u32[]{:S(2)}, u32[]{:S(2)}) async-start(bf16[8,112,768]{2,1,0:T(8,128)(2,1)} %bitcast.31), calls=%async_computation.4 | async-start | bytes 2752512 | tf_op jit(solution)/shard_map/all_to_all | solution.py:47
  54.4 3.2 %collective-permute-start.7 = (bf16[896,768]{1,0:T(8,128)(2,1)S(1)}, bf16[896,768]{1,0:T(8,128)(2,1)S(1)}, u32[]{:S(2)}, u32[]{:S(2)}) collective-permute-start(bf16[896,768]{1,0:T(8,128)(2,1)S(1)} %bitcast.24), channel_id=1, source_target_pairs={{0,8},{1,9},{2,10},{3,11},{4,12},{5,13},{6,14},{7,15},{8,0},{9,1},... | collective-permute-start | bytes 4128776 | tf_op jit(solution)/shard_map/ppermute | solution.py:42
  64.7 1.5 %copy-start.1 = (f32[896,768]{1,0:T(8,128)}, f32[896,768]{1,0:T(8,128)S(1)}, u32[]{:S(2)}) copy-start(f32[896,768]{1,0:T(8,128)S(1)} %get-tuple-element.45.refs_3_) | copy-start | bytes 8257540
  73.0 5.2 %collective-permute-start.6 = (bf16[896,768]{1,0:T(8,128)(2,1)S(1)}, bf16[896,768]{1,0:T(8,128)(2,1)S(1)}, u32[]{:S(2)}, u32[]{:S(2)}) collective-permute-start(bf16[896,768]{1,0:T(8,128)(2,1)S(1)} %bitcast.29), channel_id=1, source_target_pairs={{0,8},{1,9},{2,10},{3,11},{4,12},{5,13},{6,14},{7,15},{8,0},{9,1},... | collective-permute-start | bytes 4128776 | tf_op jit(solution)/shard_map/ppermute | solution.py:42
  73.0 1.8 %copy-start.2 = (f32[896,768]{1,0:T(8,128)S(1)}, f32[896,768]{1,0:T(8,128)}, u32[]{:S(2)}) copy-start(f32[896,768]{1,0:T(8,128)} %copy-done.1) | copy-start | bytes 8257540
  83.1 27.4 %copy-start.6 = (bf16[512,768]{1,0:T(8,128)(2,1)S(1)}, bf16[512,768]{1,0:T(8,128)(2,1)}, u32[]{:S(2)}) copy-start(bf16[512,768]{1,0:T(8,128)(2,1)} %rows_ref.1) | copy-start | bytes 2359300
  83.1 27.4 %all-to-all-start.5 = ((bf16[8,112,768]{2,1,0:T(8,128)(2,1)}), bf16[8,112,768]{2,1,0:T(8,128)(2,1)S(1)}, u32[]{:S(2)}, u32[]{:S(2)}) async-start(bf16[8,112,768]{2,1,0:T(8,128)(2,1)} %bitcast.14), calls=%async_computation.5 | async-start | bytes 2752512 | tf_op jit(solution)/shard_map/all_to_all | solution.py:47

commit v5 on v4

--- a/solution.py
+++ b/solution.py
@@ -20,6 +20,7 @@
 AXES = ("hx", "hy")
 VMEM = pl.BlockSpec(memory_space=pltpu.VMEM)
 ANY = pl.BlockSpec(memory_space=pl.ANY)
+SMEM = pl.BlockSpec(memory_space=pltpu.SMEM)
 F32, BF16, I32 = jnp.float32, jnp.bfloat16, jnp.int32
 
 
@@ -30,9 +31,13 @@
         self.cells = self.devices // 4
         self.total = self.cells * slots
         self.known = min(slots, LANES)
-        self.core_bit, self.half_bit = ny, ny // 2
+        self.core_bit, self.half_bit = ny, ny // 2 + ny // 4
         self.groups = [
-            [(2 * u + core) * ny + half * (ny // 2) + v for u in range(nx // 2) for v in range(ny // 2)]
+            [
+                (2 * u + core) * ny + half * (ny // 2) + (v ^ half * (ny // 4))
+                for u in range(nx // 2)
+                for v in range(ny // 2)
+            ]
             for core in range(2)
             for half in range(2)
         ]
@@ -49,12 +54,12 @@
     ).reshape(plan.total, plan.width)
 
 
-def call(kernel, out_shape, args, flops, moved, exps=0, after=(), scratch=(), limit=12):
+def call(kernel, out_shape, args, flops, moved, exps=0, after=(), scratch=(), limit=12, out_specs=None):
     return pl.pallas_call(
         kernel,
         out_shape=out_shape,
         in_specs=[VMEM] * len(args) + [ANY] * len(after),
-        out_specs=jax.tree.map(lambda _: VMEM, out_shape),
+        out_specs=out_specs or jax.tree.map(lambda _: VMEM, out_shape),
         scratch_shapes=list(scratch),
         compiler_params=pltpu.CompilerParams(vmem_limit_bytes=limit * 1024 * 1024),
         cost_estimate=pl.CostEstimate(flops=flops, bytes_accessed=moved, transcendentals=exps),
@@ -109,24 +114,22 @@
         tag.astype(F32),
         jnp.where(which == 1, high, jnp.where(which == 2, middle, jnp.where(which == 3, low, 0.0))),
     ).astype(BF16)
-    last = iota((TILE, known), 0) == TILE - 1
+    match = as_bf16(iota((plan.total, files), 0) == slot)
+    out_ref[...] = jnp.dot(match, rows, preferred_element_type=F32).astype(BF16)
+    last = iota((TILE, LANES), 0) == TILE - 1
     flag = jnp.broadcast_to(over.astype(F32), (TILE, LANES))
     for block in range(plan.cells):
-        match = as_bf16(iota((slots, files), 0) + block * slots == slot)
-        packed = jnp.dot(match, rows, preferred_element_type=F32)
-        here = block * slots
-        out_ref[here : here + slots, :] = packed.astype(BF16)
-        line = rows_dot(facts, match)
-        tail = slice(here + slots - TILE, here + slots)
+        here, end = block * slots, (block + 1) * slots
+        line = rows_dot(facts, match[here:end, :])
+        tail = slice(end - TILE, end)
+        old = out_ref[tail, 0 : (FACTS + 1) * LANES].astype(F32)
         for fact in range(FACTS):
             lanes = slice(fact * LANES, fact * LANES + known)
             out_ref[tail, lanes] = jnp.where(
-                last, line[fact : fact + 1, :known], packed[slots - TILE :, lanes]
+                last[:, :known], line[fact : fact + 1, :known], old[:, lanes]
             ).astype(BF16)
         lanes = slice(FACTS * LANES, (FACTS + 1) * LANES)
-        out_ref[tail, lanes] = jnp.where(
-            iota((TILE, LANES), 0) == TILE - 1, flag, packed[slots - TILE :, lanes]
-        ).astype(BF16)
+        out_ref[tail, lanes] = jnp.where(last, flag, old[:, lanes]).astype(BF16)
 
 
 def facts_of(plan, ref):
@@ -148,23 +151,20 @@
     return jnp.concatenate(tags, axis=1), jnp.concatenate(invs, axis=1), over
 
 
-def attend_kernel(plan, sets, first, last, *refs):
+def attend_kernel(plan, sets, olds, *refs):
     refs = list(refs)
     query_ref = refs.pop(0)
     keys = [(refs.pop(0), own) for own in sets]
-    if not first:
-        old_over_ref, old_ref, old_sum_ref = refs[:3]
-        del refs[:3]
-    if last:
-        over_ref, out_ref, column_ref = refs
-    else:
-        over_ref, out_ref, sum_ref, column_ref = refs
+    old_refs = refs[: 2 * olds]
+    over_ref, out_ref, column_ref = refs[2 * olds :]
     total, width = plan.total, plan.width
+    chunk = total // 2
     tag, inv, over = facts_of(plan, query_ref)
-    if not first:
+    for old_over_ref in old_refs[0::2]:
         over = jnp.maximum(over, old_over_ref[0:1, :])
     place = jnp.maximum(tag.astype(I32) - 1, 0)
     bits = (2 << place) | (2 << (place ^ 1)) | (2 << (place ^ 2)) | (2 << (place ^ 4))
+    bits = jnp.where(tag > 0.0, bits, 0)
     column_ref[0] = column(inv * (sharpness / width * math.log2(math.e)))
     column_ref[1] = column(bits.astype(F32))
     key_facts = []
@@ -172,18 +172,16 @@
         key_tag, key_inv, key_over = facts_of(plan, key_ref)
         key_facts.append((1 << key_tag.astype(I32), key_inv))
         over = jnp.maximum(over, key_over)
-    over_ref[...] = jnp.broadcast_to(over, over_ref.shape)
-    chunk = total // 2
+    if olds:
+        over_ref[0] = jnp.max(over).astype(I32)
+    else:
+        over_ref[...] = jnp.broadcast_to(over, over_ref.shape)
     for step in range(2):
         here = slice(step * chunk, (step + 1) * chunk)
         query = query_ref[here, :]
         query_inv = column_ref[0, here, :][:, 0:1]
         query_bits = column_ref[1, here, :][:, 0:1].astype(I32)
-        if first:
-            numerator = jnp.zeros((chunk, width), F32)
-            denominator = jnp.ones((chunk, LANES), F32)
-        else:
-            numerator, denominator = old_ref[here, :], old_sum_ref[here, :]
+        numerator, denominator = 0.0, 0.0
         for (key_ref, own), (key_bit, key_inv) in zip(keys, key_facts):
             score = rows_dot(query, key_ref[...]) * query_inv * key_inv
             live = (query_bits & key_bit) != 0
@@ -194,34 +192,34 @@
             numerator = numerator + jnp.dot(
                 kernel.astype(BF16), key_ref[...], preferred_element_type=F32
             )
-        if last:
-            out_ref[here, :] = (numerator / denominator[:, 0:1]).astype(BF16)
+        for old_ref in old_refs[1::2]:
+            numerator = numerator + old_ref[here, 0:width]
+            denominator = denominator + old_ref[here, width:][:, 0:1]
+        if olds:
+            out_ref[here, :] = (numerator / (1.0 + denominator)).astype(BF16)
         else:
-            out_ref[here, :] = numerator
-            sum_ref[here, :] = denominator
-
-
-def attend(plan, query, key_sets, old=(), last=False, weight=1):
+            out_ref[here, 0:width] = numerator
+            out_ref[here, width:] = jnp.broadcast_to(denominator, (chunk, LANES))
+
+
+def attend(plan, query, key_sets, olds=(), weight=1):
     total, width = plan.total, plan.width
     count = len(key_sets) * total
-    flag = jax.ShapeDtypeStruct((8, LANES), F32)
-    if last:
-        out_shape = (flag, jax.ShapeDtypeStruct((total, width), BF16))
-    else:
-        out_shape = (
-            flag,
-            jax.ShapeDtypeStruct((total, width), F32),
-            jax.ShapeDtypeStruct((total, LANES), F32),
-        )
     return call(
-        functools.partial(attend_kernel, plan, [own for _, own in key_sets], not old, last),
-        out_shape,
-        [query, *(rows for rows, _ in key_sets), *old],
+        functools.partial(attend_kernel, plan, [own for _, own in key_sets], len(olds)),
+        (
+            jax.ShapeDtypeStruct((1,), I32) if olds else jax.ShapeDtypeStruct((8, LANES), F32),
+            jax.ShapeDtypeStruct((total, width), BF16)
+            if olds
+            else jax.ShapeDtypeStruct((total, width + LANES), F32),
+        ),
+        [query, *(rows for rows, _ in key_sets), *(part for old in olds for part in old)],
         weight * 4 * total * count * width,
         12 * total * width,
         total * count,
         scratch=[pltpu.VMEM((2, total, LANES), F32)],
-        limit=18,
+        limit=26,
+        out_specs=(SMEM if olds else VMEM, VMEM),
     )
 
 
@@ -251,18 +249,21 @@
     other_bucket = swapped(bucket, plan.half_bit, plan)
     other_rows = swapped(embeddings, plan.half_bit, plan)
     payload, place = pack(bucket, embeddings)
-    own = exchange(payload, plan)
+    own = lax.cond(
+        lax.axis_index(AXES) != plan.devices, lambda payload: exchange(payload, plan), lambda payload: payload, payload
+    )
     mate = swapped(own, plan.core_bit, plan)
     relayed, _ = pack(other_bucket, other_rows, (own,))
     half = exchange(relayed, plan)
-    sums = attend(plan, own, [(own, True), (mate, False)])
+    near = attend(plan, own, [(own, True), (mate, False)])
     mate_half = swapped(half, plan.core_bit, plan)
-    sums = attend(plan, own, [(half, False)], sums, weight=40)
-    over, smoothed = attend(plan, own, [(mate_half, False)], sums, last=True)
-    return exchange(smoothed, plan), place, over[0, 0] > 0
-
-
-def unpack(plan, home, place):
+    far = attend(plan, own, [(half, False)], weight=40)
+    over, smoothed = attend(plan, own, [(mate_half, False)], [near, far])
+    return smoothed, place, over[0] > 0
+
+
+def unpack(plan, smoothed, place):
+    home = exchange(smoothed, plan)
     return call(
         functools.partial(unpack_kernel, plan),
         jax.ShapeDtypeStruct((plan.files, plan.width), BF16),
@@ -279,13 +280,13 @@
         Plan(nx, ny, *embeddings.shape, slots)
         for slots in (max(2 * TILE, most * 7 // 8 // TILE * TILE), most + TILE)
     )
-    home, place, over = smooth(short, embeddings, bucket)
-
-    def again(home, place):
-        home, place, _ = smooth(full, embeddings, bucket)
-        return unpack(full, home, place)
-
-    return lax.cond(over, again, functools.partial(unpack, short), home, place)
+    smoothed, place, over = smooth(short, embeddings, bucket)
+
+    def again(smoothed, place):
+        smoothed, place, _ = smooth(full, embeddings, bucket)
+        return unpack(full, smoothed, place)
+
+    return lax.cond(over, again, functools.partial(unpack, short), smoothed, place)
 
 
 def solution(mesh):

time: 113 us -> 102 us (0.903)
  waiting for transfers between devices: 66.5 us -> 12.2 us
  blocking collectives: 0 us -> 53.7 us
  starting transfers between devices: 16.8 us -> 9.62 us
  local copies, waits for them, and re-layouts: 4.89 us -> 0.1 us
  Pallas kernels: 23.7 us -> 25.4 us
    all_to_all x0 -> x2, blocking collectives: none -> 53.7 us  [exchange(): lax.all_to_all(value.reshape(shape), AXES, split_axis=0, concat_axis=0, t...]
    ppermute x4, waiting for transfers between devices: 37.1 us -> 3.12 us  [swapped(): lax.ppermute(value, AXES, [(i, i ^ bit) for i in range(plan.devices)])]
    all_to_all x3 -> x1, waiting for transfers between devices: 29.4 us -> 9.05 us  [exchange(): lax.all_to_all(value.reshape(shape), AXES, split_axis=0, concat_axis=0, t...]
    all_to_all x3 -> x1, starting transfers between devices: 13.8 us -> 4.46 us  [exchange(): lax.all_to_all(value.reshape(shape), AXES, split_axis=0, concat_axis=0, t...]
    unnamed x12 -> x6, local copies, waits for them, and re-layouts: 4.37 us -> 0.01 us
    ppermute x4, starting transfers between devices: 3.05 us -> 5.16 us  [swapped(): lax.ppermute(value, AXES, [(i, i ^ bit) for i in range(plan.devices)])]
    pallas_call x6, Pallas kernels: 23.7 us -> 25.4 us  [call(): pl.pallas_call(kernel, out_shape=out_shape, in_specs=[VMEM] * len(args) +...]
  transfers between devices with their start and end apart: 7 -> 5, of which waited for: 5 -> 2; matrix products, arithmetic and copies ran while one was open for 0% -> 0% of each run, Pallas kernels for 9% -> 17%
where the time goes in v5:
time: 102 us
  blocking collectives  53.7 us (53%)
  Pallas kernels  25.4 us (25%)
  waiting for transfers between devices  12.2 us (12%)
  starting transfers between devices  9.62 us (9%)
    all_to_all x2, blocking collectives, exchange(): lax.all_to_all(value.reshape(shape), AXES, split_axis=0, concat_axis=0, t...  53.7 us
    pallas_call x6, Pallas kernels, call(): pl.pallas_call(kernel, out_shape=out_shape, in_specs=[VMEM] * len(args) +...  25.4 us
    all_to_all x1, waiting for transfers between devices, exchange(): lax.all_to_all(value.reshape(shape), AXES, split_axis=0, concat_axis=0, t...  9.05 us
    ppermute x4, starting transfers between devices, swapped(): lax.ppermute(value, AXES, [(i, i ^ bit) for i in range(plan.devices)])  5.16 us
    all_to_all x1, starting transfers between devices, exchange(): lax.all_to_all(value.reshape(shape), AXES, split_axis=0, concat_axis=0, t...  4.46 us
    ppermute x4, waiting for transfers between devices, swapped(): lax.ppermute(value, AXES, [(i, i ^ bit) for i in range(plan.devices)])  3.12 us
  transfers between devices with their start and end apart: 5, of which 2 were waited for; matrix products, arithmetic and copies ran while one was open for 0% of the time, Pallas kernels for 17%

profile of v5, /device:TPU:0, one launch (start us, length us, event | category | flops | bytes accessed | tf_op | source)
XLA Modules:
  0.0 101.9 jit_solution(8242139712810355102)
XLA Ops:
  0.0 5.0 %collective-permute-start.5 = (bf16[512,768]{1,0:T(8,128)(2,1)}, bf16[512,768]{1,0:T(8,128)(2,1)S(1)}, u32[]{:S(2)}, u32[]{:S(2)}) collective-permute-start(bf16[512,768]{1,0:T(8,128)(2,1)} %rows_ref.1), channel_id=1, source_target_pairs={{0,6},{1,7},{2,4},{3,5},{4,2},{5,3},{6,0},{7,1},{8,14},{9,15},{10,... | collective-permute-start | bytes 2359304 | tf_op jit(solution)/shard_map/ppermute | solution.py:47
  5.0 0.0 collective-permute-start.4
  5.1 2.8 %shard_map.30 = (bf16[896,768]{1,0:T(8,128)(2,1)S(1)}, s32[8,512]{1,0:T(8,128)S(1)}) custom-call(s32[1,512]{1,0:T(1,128)} %bitcast.24, bf16[512,768]{1,0:T(8,128)(2,1)} %rows_ref.1), custom_call_target="tpu_custom_call" | custom-call | flops 704643072 | bytes 2359296 | tf_op jit(solution)/shard_map/pallas_call | solution.py:58
  7.9 31.7 %conditional.3 = (bf16[896,768]{1,0:T(8,128)(2,1)S(1)}) conditional(s32[]{:T(128)} %convert_element_type.12, bf16[896,768]{1,0:T(8,128)(2,1)S(1)} %get-tuple-element.47, bf16[896,768]{1,0:T(8,128)(2,1)S(1)} %get-tuple-element.47), branch_computations={%region_0.0_spmd, %region_1.0_spmd} | conditional | bytes 5505032 | solution.py:252
  7.9 0.1 copy.11
  8.0 31.6 %all_to_all.25 = bf16[8,112,768]{2,1,0:T(8,128)(2,1)S(1)} all-to-all(bf16[8,112,768]{2,1,0:T(8,128)(2,1)S(1)} %copy.11), channel_id=1, replica_groups={{0,1,2,3,16,17,18,19},{6,7,4,5,22,23,20,21},{8,9,10,11,24,25,26,27},{14..., dimensions={0} | all-to-all | bytes 2752512 | tf_op jit(solution)/shard_map/cond/branch_1_fun/all_to_all | solution.py:52
  39.6 0.0 copy-start.2
  39.6 0.0 collective-permute-done.4.bucket_ref
  39.6 0.0 collective-permute-done.5.rows_ref
  39.6 2.7 %shard_map.31 = (bf16[896,768]{1,0:T(8,128)(2,1)}, s32[8,512]{1,0:T(8,128)}) custom-call(s32[1,512]{1,0:T(1,128)S(1)} %collective-permute-done.4.bucket_ref, bf16[512,768]{1,0:T(8,128)(2,1)S(1)} %collective-permute-done.5.rows_ref, bf16[896,768]{1,0:T(8,128)(2,1)S(1)} %get-tuple-element.60.refs_0_.refs_1_), custom_call_target="tpu_custom_call" | custom-call | flops 704643072 | bytes 2359296 | tf_op jit(solution)/shard_map/pallas_call | solution.py:58
  42.3 4.5 %all-to-all-start.5 = ((bf16[8,112,768]{2,1,0:T(8,128)(2,1)}), bf16[8,112,768]{2,1,0:T(8,128)(2,1)}, u32[]{:S(2)}, u32[]{:S(2)}) async-start(bf16[8,112,768]{2,1,0:T(8,128)(2,1)} %bitcast.12), calls=%async_computation.5 | async-start | bytes 2752512 | tf_op jit(solution)/shard_map/all_to_all | solution.py:52
  46.7 0.0 copy-done.2
  46.8 0.1 collective-permute-start.7
  46.8 3.1 %collective-permute-done.7.refs_2_ = bf16[896,768]{1,0:T(8,128)(2,1)S(1)} collective-permute-done((bf16[896,768]{1,0:T(8,128)(2,1)S(1)}, bf16[896,768]{1,0:T(8,128)(2,1)S(1)}, u32[]{:S(2)}, u32[]{:S(2)}) %collective-permute-start.7) | collective-permute-done | bytes 1376288 | tf_op jit(solution)/shard_map/ppermute | solution.py:47
  50.0 8.8 %shard_map.32 = (f32[8,128]{1,0:T(8,128)S(1)}, f32[896,896]{1,0:T(8,128)S(1)}) custom-call(bf16[896,768]{1,0:T(8,128)(2,1)} %copy-done.2, bf16[896,768]{1,0:T(8,128)(2,1)} %copy-done.2, bf16[896,768]{1,0:T(8,128)(2,1)S(1)} %collective-permute-done.7.refs_2_), custom_call_target="tpu_custom_call" | custom-call | flops 4932501504 | bytes 8257536 | tf_op jit(solution)/shard_map/pallas_call | solution.py:58
  58.8 9.0 %all-to-all-done.5 = bf16[8,112,768]{2,1,0:T(8,128)(2,1)} async-done(((bf16[8,112,768]{2,1,0:T(8,128)(2,1)}), bf16[8,112,768]{2,1,0:T(8,128)(2,1)}, u32[]{:S(2)}, u32[]{:S(2)}) %all-to-all-start.5) | async-done | bytes 1376288 | tf_op jit(solution)/shard_map/all_to_all | solution.py:52
  67.8 0.0 copy-start.3
  67.8 0.0 collective-permute-start.6
  67.8 5.3 %shard_map.33 = (f32[8,128]{1,0:T(8,128)S(1)}, f32[896,896]{1,0:T(8,128)S(1)}) custom-call(bf16[896,768]{1,0:T(8,128)(2,1)} %copy-done.2, bf16[896,768]{1,0:T(8,128)(2,1)} %bitcast.13.refs_1_), custom_call_target="tpu_custom_call" | custom-call | flops 98650030080 | bytes 8257536 | tf_op jit(solution)/shard_map/pallas_call | solution.py:58
  73.1 0.0 collective-permute-done.6.refs_1_
  73.1 0.0 copy-done.3
  73.1 0.0 copy-start.4
  73.1 3.8 %shard_map.34 = (s32[1]{0:T(128)}, bf16[896,768]{1,0:T(8,128)(2,1)S(1)}) custom-call(bf16[896,768]{1,0:T(8,128)(2,1)S(1)} %copy-done.3, bf16[896,768]{1,0:T(8,128)(2,1)S(1)} %collective-permute-done.6.refs_1_, f32[8,128]{1,0:T(8,128)S(1)} %get-tuple-element.49.refs_2_, f32[896,896]{1,0:T(8,128)S(1)} %get-tuple-element.50.refs_3_, ...), custom_call_target="tpu_custom_call" | custom-call | flops 2466250752 | bytes 8257536 | tf_op jit(solution)/shard_map/pallas_call | solution.py:58
  77.5 0.0 copy-done.4
  77.5 24.3 %conditional.4 = (bf16[512,768]{1,0:T(8,128)(2,1)}) conditional(s32[]{:T(128)} %bitcast.14, (bf16[896,768]{1,0:T(8,128)(2,1)S(1)}, s32[8,512]{1,0:T(8,128)S(1)}) %tuple.23, (s32[512]{0:T(512)S(1)}, bf16[512,768]{1,0:T(8,128)(2,1)}) %tuple.33), branch_computations={%region_2.0_spmd, %region_3.0_spmd} | conditional | flops 178023038976 | bytes 105193824 | solution.py:289
  77.6 22.1 %all_to_all.26 = bf16[8,112,768]{2,1,0:T(8,128)(2,1)S(1)} all-to-all(bf16[8,112,768]{2,1,0:T(8,128)(2,1)S(1)} %bitcast.22), channel_id=1, replica_groups={{0,1,2,3,16,17,18,19},{6,7,4,5,22,23,20,21},{8,9,10,11,24,25,26,27},{14..., dimensions={0} | all-to-all | bytes 2752512 | tf_op jit(solution)/shard_map/cond/branch_0_fun/all_to_all | solution.py:52
  99.7 2.1 %branch_0_fun.1 = bf16[512,768]{1,0:T(8,128)(2,1)} custom-call(s32[8,512]{1,0:T(8,128)S(1)} %get-tuple-element.26.place_ref, bf16[896,768]{1,0:T(8,128)(2,1)S(1)} %bitcast.17), custom_call_target="tpu_custom_call" | custom-call | flops 704643072 | bytes 2359296 | tf_op jit(solution)/shard_map/cond/branch_0_fun/pallas_call | solution.py:58
Async XLA Ops:
  0.0 39.6 %collective-permute-start.5 = (bf16[512,768]{1,0:T(8,128)(2,1)}, bf16[512,768]{1,0:T(8,128)(2,1)S(1)}, u32[]{:S(2)}, u32[]{:S(2)}) collective-permute-start(bf16[512,768]{1,0:T(8,128)(2,1)} %rows_ref.1), channel_id=1, source_target_pairs={{0,6},{1,7},{2,4},{3,5},{4,2},{5,3},{6,0},{7,1},{8,14},{9,15},{10,... | collective-permute-start | bytes 2359304 | tf_op jit(solution)/shard_map/ppermute | solution.py:47
  5.0 34.5 %collective-permute-start.4 = (s32[1,512]{1,0:T(1,128)}, s32[1,512]{1,0:T(1,128)S(1)}, u32[]{:S(2)}, u32[]{:S(2)}) collective-permute-start(s32[1,512]{1,0:T(1,128)} %bitcast.23), channel_id=1, source_target_pairs={{0,6},{1,7},{2,4},{3,5},{4,2},{5,3},{6,0},{7,1},{8,14},{9,15},{10,... | collective-permute-start | bytes 6152 | tf_op jit(solution)/shard_map/ppermute | solution.py:47
  39.6 7.2 %copy-start.2 = (bf16[896,768]{1,0:T(8,128)(2,1)}, bf16[896,768]{1,0:T(8,128)(2,1)S(1)}, u32[]{:S(2)}) copy-start(bf16[896,768]{1,0:T(8,128)(2,1)S(1)} %get-tuple-element.60.refs_0_.refs_1_) | copy-start | bytes 4128772
  42.3 25.5 %all-to-all-start.5 = ((bf16[8,112,768]{2,1,0:T(8,128)(2,1)}), bf16[8,112,768]{2,1,0:T(8,128)(2,1)}, u32[]{:S(2)}, u32[]{:S(2)}) async-start(bf16[8,112,768]{2,1,0:T(8,128)(2,1)} %bitcast.12), calls=%async_computation.5 | async-start | bytes 2752512 | tf_op jit(solution)/shard_map/all_to_all | solution.py:52
  46.8 3.2 %collective-permute-start.7 = (bf16[896,768]{1,0:T(8,128)(2,1)S(1)}, bf16[896,768]{1,0:T(8,128)(2,1)S(1)}, u32[]{:S(2)}, u32[]{:S(2)}) collective-permute-start(bf16[896,768]{1,0:T(8,128)(2,1)S(1)} %get-tuple-element.60.refs_0_.refs_1_), channel_id=1, source_target_pairs={{0,8},{1,9},{2,10},{3,11},{4,12},{5,13},{6,14},{7,15},{8,0},{9,1},... | collective-permute-start | bytes 4128776 | tf_op jit(solution)/shard_map/ppermute | solution.py:47
  67.8 5.3 %copy-start.3 = (bf16[896,768]{1,0:T(8,128)(2,1)S(1)}, bf16[896,768]{1,0:T(8,128)(2,1)}, u32[]{:S(2)}) copy-start(bf16[896,768]{1,0:T(8,128)(2,1)} %copy-done.2) | copy-start | bytes 4128772
  67.8 5.3 %collective-permute-start.6 = (bf16[896,768]{1,0:T(8,128)(2,1)}, bf16[896,768]{1,0:T(8,128)(2,1)S(1)}, u32[]{:S(2)}, u32[]{:S(2)}) collective-permute-start(bf16[896,768]{1,0:T(8,128)(2,1)} %bitcast.13.refs_1_), channel_id=1, source_target_pairs={{0,8},{1,9},{2,10},{3,11},{4,12},{5,13},{6,14},{7,15},{8,0},{9,1},... | collective-permute-start | bytes 4128776 | tf_op jit(solution)/shard_map/ppermute | solution.py:47
  73.1 4.5 %copy-start.4 = (s32[512]{0:T(512)S(1)}, s32[512]{0:T(512)}, u32[]{:S(2)}) copy-start(s32[512]{0:T(512)} %param.9) | copy-start | bytes 6148

commit v6 on v5

--- a/solution.py
+++ b/solution.py
@@ -33,14 +33,20 @@
         self.known = min(slots, LANES)
         self.core_bit, self.half_bit = ny, ny // 2 + ny // 4
         self.groups = [
-            [
-                (2 * u + core) * ny + half * (ny // 2) + (v ^ half * (ny // 4))
-                for u in range(nx // 2)
-                for v in range(ny // 2)
-            ]
+            turned(
+                [
+                    (2 * u + core) * ny + half * (ny // 2) + (v ^ half * (ny // 4))
+                    for u in range(nx // 2)
+                    for v in range(ny // 2)
+                ]
+            )
             for core in range(2)
             for half in range(2)
         ]
+
+
+def turned(members):
+    return [members[-1 - i // 2 if i % 2 else i // 2] for i in range(len(members))]
 
 
 def swapped(value, bit, plan):
@@ -82,9 +88,8 @@
     return mask.astype(F32).astype(BF16)
 
 
-def pack_kernel(plan, bucket_ref, rows_ref, *refs):
-    out_ref, place_ref = refs[-2:]
-    nx, ny, files, slots, known = plan.nx, plan.ny, plan.files, plan.slots, plan.known
+def place_kernel(plan, bucket_ref, rows_ref, place_ref):
+    nx, ny, files, slots = plan.nx, plan.ny, plan.files, plan.slots
     bucket = bucket_ref[...]
     low_b = ny.bit_length() - 1
     a = bucket >> (low_b + 1)
@@ -96,28 +101,34 @@
     before = column(order)[:, :1] < order
     same = column(cell)[:, :1] == cell
     index = jnp.sum((before & same).astype(I32), axis=0, keepdims=True)
-    over = jnp.max(index, axis=1, keepdims=True) >= slots - 1
+    over = (jnp.max(index, axis=1, keepdims=True) >= slots - 1).astype(F32)
     slot = jnp.where(index < slots - 1, cell * slots + index, plan.total)
-    place_ref[...] = jnp.broadcast_to(slot, place_ref.shape)
-
-    rows = rows_ref[...]
-    wide = rows.astype(F32)
+    wide = rows_ref[...].astype(F32)
     square = jnp.sum(wide * wide, axis=1, keepdims=True)
     square = jnp.broadcast_to(square, (files, LANES)).T[0:1, :]
     inv = 1.0 / jnp.sqrt(square * (1.0 / plan.width) + epsilon)
     high = inv.astype(BF16).astype(F32)
     middle = (inv - high).astype(BF16).astype(F32)
     low = inv - high - middle
-    which = iota((TILE, files), 0)
-    facts = jnp.where(
-        which == 0,
-        tag.astype(F32),
-        jnp.where(which == 1, high, jnp.where(which == 2, middle, jnp.where(which == 3, low, 0.0))),
-    ).astype(BF16)
+    line = iota((8, files), 0)
+    place = jnp.zeros((8, files), F32)
+    for index, value in enumerate((tag.astype(F32), high, middle, low, over, slot.astype(F32))):
+        place = jnp.where(line == index, value, place)
+    place_ref[...] = place
+
+
+def pack_kernel(plan, place_ref, rows_ref, *refs):
+    out_ref = refs[-1]
+    files, slots, known = plan.files, plan.slots, plan.known
+    place = place_ref[...]
+    facts = jnp.concatenate([place, jnp.zeros((TILE - 8, files), F32)], axis=0)
+    facts = jnp.where(iota((TILE, files), 0) < FACTS, facts, 0.0).astype(BF16)
+    over, slot = place[4:5, 0:LANES], place[5:6, :].astype(I32)
+    rows = rows_ref[...]
     match = as_bf16(iota((plan.total, files), 0) == slot)
     out_ref[...] = jnp.dot(match, rows, preferred_element_type=F32).astype(BF16)
     last = iota((TILE, LANES), 0) == TILE - 1
-    flag = jnp.broadcast_to(over.astype(F32), (TILE, LANES))
+    flag = jnp.broadcast_to(over, (TILE, LANES))
     for block in range(plan.cells):
         here, end = block * slots, (block + 1) * slots
         line = rows_dot(facts, match[here:end, :])
@@ -224,7 +235,7 @@
 
 
 def unpack_kernel(plan, place_ref, home_ref, out_ref):
-    slot = column(place_ref[0:1, :])[:, 0:1]
+    slot = column(place_ref[5:6, :])[:, 0:1].astype(I32)
     match = as_bf16(iota((plan.files, plan.total), 1) == slot)
     out_ref[...] = jnp.dot(match, home_ref[...], preferred_element_type=F32).astype(BF16)
 
@@ -233,27 +244,31 @@
     files, width, total = plan.files, plan.width, plan.total
     bucket = bucket.reshape(1, files)
 
-    def pack(which, rows, after=()):
+    def pack(place, rows, after=()):
         return call(
             functools.partial(pack_kernel, plan),
-            (
-                jax.ShapeDtypeStruct((total, width), BF16),
-                jax.ShapeDtypeStruct((8, files), I32),
-            ),
-            [which, rows],
+            jax.ShapeDtypeStruct((total, width), BF16),
+            [place, rows],
             2 * total * files * width,
             6 * files * width,
             after=after,
         )
 
-    other_bucket = swapped(bucket, plan.half_bit, plan)
     other_rows = swapped(embeddings, plan.half_bit, plan)
-    payload, place = pack(bucket, embeddings)
+    place = call(
+        functools.partial(place_kernel, plan),
+        jax.ShapeDtypeStruct((8, files), F32),
+        [bucket, embeddings],
+        4 * files * files,
+        2 * files * width,
+    )
+    other_place = swapped(place, plan.half_bit, plan)
+    payload = pack(place, embeddings)
     own = lax.cond(
         lax.axis_index(AXES) != plan.devices, lambda payload: exchange(payload, plan), lambda payload: payload, payload
     )
     mate = swapped(own, plan.core_bit, plan)
-    relayed, _ = pack(other_bucket, other_rows, (own,))
+    relayed = pack(other_place, other_rows, (own,))
     half = exchange(relayed, plan)
     near = attend(plan, own, [(own, True), (mate, False)])
     mate_half = swapped(half, plan.core_bit, plan)

time: 102 us -> 99.5 us (0.975)
  waiting for transfers between devices: 12.2 us -> 8.14 us
  Pallas kernels: 25.4 us -> 26.5 us
    all_to_all x1, waiting for transfers between devices: 9.05 us -> 5.01 us  [exchange(): lax.all_to_all(value.reshape(shape), AXES, split_axis=0, concat_axis=0, t...]
    pallas_call x6 -> x7, Pallas kernels: 25.4 us -> 26.5 us  [call(): pl.pallas_call(kernel, out_shape=out_shape, in_specs=[VMEM] * len(args) +...]
  transfers between devices with their start and end apart: 5 -> 5, of which waited for: 2 -> 2; matrix products, arithmetic and copies ran while one was open for 0% -> 0% of each run, Pallas kernels for 17% -> 18%
where the time goes in v6:
time: 99.5 us; the launch traced here: 99.1 us
  blocking collectives  54 us (54%)
  Pallas kernels  26.5 us (27%)
  starting transfers between devices  9.66 us (10%)
  waiting for transfers between devices  8.14 us (8%)
    all_to_all x2, blocking collectives, exchange(): lax.all_to_all(value.reshape(shape), AXES, split_axis=0, concat_axis=0, t...  54 us
    pallas_call x7, Pallas kernels, call(): pl.pallas_call(kernel, out_shape=out_shape, in_specs=[VMEM] * len(args) +...  26.5 us
    ppermute x4, starting transfers between devices, swapped(): lax.ppermute(value, AXES, [(i, i ^ bit) for i in range(plan.devices)])  5.19 us
    all_to_all x1, waiting for transfers between devices, exchange(): lax.all_to_all(value.reshape(shape), AXES, split_axis=0, concat_axis=0, t...  5.01 us
    all_to_all x1, starting transfers between devices, exchange(): lax.all_to_all(value.reshape(shape), AXES, split_axis=0, concat_axis=0, t...  4.46 us
    ppermute x4, waiting for transfers between devices, swapped(): lax.ppermute(value, AXES, [(i, i ^ bit) for i in range(plan.devices)])  3.12 us
  transfers between devices with their start and end apart: 5, of which 2 were waited for; matrix products, arithmetic and copies ran while one was open for 0% of the time, Pallas kernels for 18%

profile of v6, /device:TPU:0, one launch (start us, length us, event | category | flops | bytes accessed | tf_op | source)
XLA Modules:
  0.0 99.1 jit_solution(14767200804008156093)
XLA Ops:
  0.0 5.0 %collective-permute-start.5 = (bf16[512,768]{1,0:T(8,128)(2,1)}, bf16[512,768]{1,0:T(8,128)(2,1)S(1)}, u32[]{:S(2)}, u32[]{:S(2)}) collective-permute-start(bf16[512,768]{1,0:T(8,128)(2,1)} %rows_ref.3), channel_id=1, source_target_pairs={{0,6},{1,7},{2,4},{3,5},{4,2},{5,3},{6,0},{7,1},{8,14},{9,15},{10,... | collective-permute-start | bytes 2359304 | tf_op jit(solution)/shard_map/ppermute | solution.py:53
  5.0 1.9 %shard_map.30.place_ref = f32[8,512]{1,0:T(8,128)S(1)} custom-call(s32[1,512]{1,0:T(1,128)} %bitcast.23, bf16[512,768]{1,0:T(8,128)(2,1)} %rows_ref.3), custom_call_target="tpu_custom_call" | custom-call | flops 1048576 | bytes 786432 | tf_op jit(solution)/shard_map/pallas_call | solution.py:64
  7.0 0.1 collective-permute-start.4
  7.1 2.3 %shard_map.31 = bf16[896,768]{1,0:T(8,128)(2,1)S(1)} custom-call(f32[8,512]{1,0:T(8,128)S(1)} %shard_map.30.place_ref, bf16[512,768]{1,0:T(8,128)(2,1)} %rows_ref.3), custom_call_target="tpu_custom_call" | custom-call | flops 704643072 | bytes 2359296 | tf_op jit(solution)/shard_map/pallas_call | solution.py:64
  9.3 30.1 %conditional.3 = (bf16[896,768]{1,0:T(8,128)(2,1)S(1)}) conditional(s32[]{:T(128)} %convert_element_type.12, bf16[896,768]{1,0:T(8,128)(2,1)S(1)} %shard_map.31, bf16[896,768]{1,0:T(8,128)(2,1)S(1)} %shard_map.31), branch_computations={%region_0.0_spmd, %region_1.0_spmd} | conditional | bytes 5505032 | solution.py:267
  9.4 0.1 copy.11
  9.4 30.0 %all_to_all.25 = bf16[8,112,768]{2,1,0:T(8,128)(2,1)S(1)} all-to-all(bf16[8,112,768]{2,1,0:T(8,128)(2,1)S(1)} %copy.11), channel_id=1, replica_groups={{0,19,1,18,2,17,3,16},{6,21,7,20,4,23,5,22},{8,27,9,26,10,25,11,24},{14..., dimensions={0} | all-to-all | bytes 2752512 | tf_op jit(solution)/shard_map/cond/branch_1_fun/all_to_all | solution.py:58
  39.4 0.0 copy-start.2
  39.5 0.0 collective-permute-done.4.place_ref
  39.5 0.0 collective-permute-done.5.rows_ref
  39.5 2.2 %shard_map.32 = bf16[896,768]{1,0:T(8,128)(2,1)} custom-call(f32[8,512]{1,0:T(8,128)S(1)} %collective-permute-done.4.place_ref, bf16[512,768]{1,0:T(8,128)(2,1)S(1)} %collective-permute-done.5.rows_ref, bf16[896,768]{1,0:T(8,128)(2,1)S(1)} %get-tuple-element.51.refs_0_.refs_1_), custom_call_target="tpu_custom_call" | custom-call | flops 704643072 | bytes 2359296 | tf_op jit(solution)/shard_map/pallas_call | solution.py:64
  41.7 4.5 %all-to-all-start.5 = ((bf16[8,112,768]{2,1,0:T(8,128)(2,1)}), bf16[8,112,768]{2,1,0:T(8,128)(2,1)}, u32[]{:S(2)}, u32[]{:S(2)}) async-start(bf16[8,112,768]{2,1,0:T(8,128)(2,1)} %bitcast.12), calls=%async_computation.5 | async-start | bytes 2752512 | tf_op jit(solution)/shard_map/all_to_all | solution.py:58
  46.1 0.0 copy-done.2
  46.2 0.1 collective-permute-start.7
  46.2 3.1 %collective-permute-done.7.refs_2_ = bf16[896,768]{1,0:T(8,128)(2,1)S(1)} collective-permute-done((bf16[896,768]{1,0:T(8,128)(2,1)S(1)}, bf16[896,768]{1,0:T(8,128)(2,1)S(1)}, u32[]{:S(2)}, u32[]{:S(2)}) %collective-permute-start.7) | collective-permute-done | bytes 1376288 | tf_op jit(solution)/shard_map/ppermute | solution.py:53
  49.3 8.9 %shard_map.33 = (f32[8,128]{1,0:T(8,128)S(1)}, f32[896,896]{1,0:T(8,128)S(1)}) custom-call(bf16[896,768]{1,0:T(8,128)(2,1)} %copy-done.2, bf16[896,768]{1,0:T(8,128)(2,1)} %copy-done.2, bf16[896,768]{1,0:T(8,128)(2,1)S(1)} %collective-permute-done.7.refs_2_), custom_call_target="tpu_custom_call" | custom-call | flops 4932501504 | bytes 8257536 | tf_op jit(solution)/shard_map/pallas_call | solution.py:64
  58.2 5.0 %all-to-all-done.5 = bf16[8,112,768]{2,1,0:T(8,128)(2,1)} async-done(((bf16[8,112,768]{2,1,0:T(8,128)(2,1)}), bf16[8,112,768]{2,1,0:T(8,128)(2,1)}, u32[]{:S(2)}, u32[]{:S(2)}) %all-to-all-start.5) | async-done | bytes 1376288 | tf_op jit(solution)/shard_map/all_to_all | solution.py:58
  63.2 0.0 copy-start.3
  63.2 0.0 collective-permute-start.6
  63.2 5.3 %shard_map.34 = (f32[8,128]{1,0:T(8,128)S(1)}, f32[896,896]{1,0:T(8,128)S(1)}) custom-call(bf16[896,768]{1,0:T(8,128)(2,1)} %copy-done.2, bf16[896,768]{1,0:T(8,128)(2,1)} %bitcast.13.refs_1_), custom_call_target="tpu_custom_call" | custom-call | flops 98650030080 | bytes 8257536 | tf_op jit(solution)/shard_map/pallas_call | solution.py:64
  68.5 0.0 collective-permute-done.6.refs_1_
  68.5 0.0 copy-done.3
  68.5 0.0 copy-start.4
  68.5 3.8 %shard_map.35 = (s32[1]{0:T(128)}, bf16[896,768]{1,0:T(8,128)(2,1)S(1)}) custom-call(bf16[896,768]{1,0:T(8,128)(2,1)S(1)} %copy-done.3, bf16[896,768]{1,0:T(8,128)(2,1)S(1)} %collective-permute-done.6.refs_1_, f32[8,128]{1,0:T(8,128)S(1)} %get-tuple-element.41.refs_2_, f32[896,896]{1,0:T(8,128)S(1)} %get-tuple-element.42.refs_3_, ...), custom_call_target="tpu_custom_call" | custom-call | flops 2466250752 | bytes 8257536 | tf_op jit(solution)/shard_map/pallas_call | solution.py:64
  73.0 0.0 copy-done.4
  73.0 26.2 %conditional.4 = (bf16[512,768]{1,0:T(8,128)(2,1)}) conditional(s32[]{:T(128)} %bitcast.14, (bf16[896,768]{1,0:T(8,128)(2,1)S(1)}, f32[8,512]{1,0:T(8,128)S(1)}) %tuple.23, (s32[512]{0:T(512)S(1)}, bf16[512,768]{1,0:T(8,128)(2,1)}) %tuple.33), branch_computations={%region_2.0_spmd, %region_3.0_spmd} | conditional | flops 178024087552 | bytes 106037600 | solution.py:304
  73.0 24.0 %all_to_all.26 = bf16[8,112,768]{2,1,0:T(8,128)(2,1)S(1)} all-to-all(bf16[8,112,768]{2,1,0:T(8,128)(2,1)S(1)} %bitcast.22), channel_id=1, replica_groups={{0,19,1,18,2,17,3,16},{6,21,7,20,4,23,5,22},{8,27,9,26,10,25,11,24},{14..., dimensions={0} | all-to-all | bytes 2752512 | tf_op jit(solution)/shard_map/cond/branch_0_fun/all_to_all | solution.py:58
  97.0 2.2 %branch_0_fun.1 = bf16[512,768]{1,0:T(8,128)(2,1)} custom-call(f32[8,512]{1,0:T(8,128)S(1)} %get-tuple-element.26.place_ref, bf16[896,768]{1,0:T(8,128)(2,1)S(1)} %bitcast.17), custom_call_target="tpu_custom_call" | custom-call | flops 704643072 | bytes 2359296 | tf_op jit(solution)/shard_map/cond/branch_0_fun/pallas_call | solution.py:64
Async XLA Ops:
  0.0 39.5 %collective-permute-start.5 = (bf16[512,768]{1,0:T(8,128)(2,1)}, bf16[512,768]{1,0:T(8,128)(2,1)S(1)}, u32[]{:S(2)}, u32[]{:S(2)}) collective-permute-start(bf16[512,768]{1,0:T(8,128)(2,1)} %rows_ref.3), channel_id=1, source_target_pairs={{0,6},{1,7},{2,4},{3,5},{4,2},{5,3},{6,0},{7,1},{8,14},{9,15},{10,... | collective-permute-start | bytes 2359304 | tf_op jit(solution)/shard_map/ppermute | solution.py:53
  7.0 32.5 %collective-permute-start.4 = (f32[8,512]{1,0:T(8,128)S(1)}, f32[8,512]{1,0:T(8,128)S(1)}, u32[]{:S(2)}, u32[]{:S(2)}) collective-permute-start(f32[8,512]{1,0:T(8,128)S(1)} %shard_map.30.place_ref), channel_id=1, source_target_pairs={{0,6},{1,7},{2,4},{3,5},{4,2},{5,3},{6,0},{7,1},{8,14},{9,15},{10,... | collective-permute-start | bytes 49160 | tf_op jit(solution)/shard_map/ppermute | solution.py:53
  39.4 6.7 %copy-start.2 = (bf16[896,768]{1,0:T(8,128)(2,1)}, bf16[896,768]{1,0:T(8,128)(2,1)S(1)}, u32[]{:S(2)}) copy-start(bf16[896,768]{1,0:T(8,128)(2,1)S(1)} %get-tuple-element.51.refs_0_.refs_1_) | copy-start | bytes 4128772
  41.7 21.6 %all-to-all-start.5 = ((bf16[8,112,768]{2,1,0:T(8,128)(2,1)}), bf16[8,112,768]{2,1,0:T(8,128)(2,1)}, u32[]{:S(2)}, u32[]{:S(2)}) async-start(bf16[8,112,768]{2,1,0:T(8,128)(2,1)} %bitcast.12), calls=%async_computation.5 | async-start | bytes 2752512 | tf_op jit(solution)/shard_map/all_to_all | solution.py:58
  46.2 3.2 %collective-permute-start.7 = (bf16[896,768]{1,0:T(8,128)(2,1)S(1)}, bf16[896,768]{1,0:T(8,128)(2,1)S(1)}, u32[]{:S(2)}, u32[]{:S(2)}) collective-permute-start(bf16[896,768]{1,0:T(8,128)(2,1)S(1)} %get-tuple-element.51.refs_0_.refs_1_), channel_id=1, source_target_pairs={{0,8},{1,9},{2,10},{3,11},{4,12},{5,13},{6,14},{7,15},{8,0},{9,1},... | collective-permute-start | bytes 4128776 | tf_op jit(solution)/shard_map/ppermute | solution.py:53
  63.2 5.3 %copy-start.3 = (bf16[896,768]{1,0:T(8,128)(2,1)S(1)}, bf16[896,768]{1,0:T(8,128)(2,1)}, u32[]{:S(2)}) copy-start(bf16[896,768]{1,0:T(8,128)(2,1)} %copy-done.2) | copy-start | bytes 4128772
  63.2 5.3 %collective-permute-start.6 = (bf16[896,768]{1,0:T(8,128)(2,1)}, bf16[896,768]{1,0:T(8,128)(2,1)S(1)}, u32[]{:S(2)}, u32[]{:S(2)}) collective-permute-start(bf16[896,768]{1,0:T(8,128)(2,1)} %bitcast.13.refs_1_), channel_id=1, source_target_pairs={{0,8},{1,9},{2,10},{3,11},{4,12},{5,13},{6,14},{7,15},{8,0},{9,1},... | collective-permute-start | bytes 4128776 | tf_op jit(solution)/shard_map/ppermute | solution.py:53
  68.5 4.5 %copy-start.4 = (s32[512]{0:T(512)S(1)}, s32[512]{0:T(512)}, u32[]{:S(2)}) copy-start(s32[512]{0:T(512)} %param.9) | copy-start | bytes 6148

commit v7 on v6

--- a/solution.py
+++ b/solution.py
@@ -117,30 +117,42 @@
     place_ref[...] = place
 
 
-def pack_kernel(plan, place_ref, rows_ref, *refs):
-    out_ref = refs[-1]
+def pack_kernel(plan, place_ref, rows_ref, out_ref, info_ref):
     files, slots, known = plan.files, plan.slots, plan.known
     place = place_ref[...]
     facts = jnp.concatenate([place, jnp.zeros((TILE - 8, files), F32)], axis=0)
     facts = jnp.where(iota((TILE, files), 0) < FACTS, facts, 0.0).astype(BF16)
     over, slot = place[4:5, 0:LANES], place[5:6, :].astype(I32)
-    rows = rows_ref[...]
     match = as_bf16(iota((plan.total, files), 0) == slot)
-    out_ref[...] = jnp.dot(match, rows, preferred_element_type=F32).astype(BF16)
-    last = iota((TILE, LANES), 0) == TILE - 1
-    flag = jnp.broadcast_to(over, (TILE, LANES))
+    out_ref[...] = jnp.dot(match, rows_ref[...], preferred_element_type=F32).astype(BF16)
+    info_ref[...] = jnp.zeros(info_ref.shape, F32)
+    info_ref[0:8, 0:files] = place
     for block in range(plan.cells):
-        here, end = block * slots, (block + 1) * slots
-        line = rows_dot(facts, match[here:end, :])
+        line = rows_dot(facts, match[block * slots : (block + 1) * slots, :])
+        row = slice(8 + block, 9 + block)
+        for fact in range(FACTS):
+            info_ref[row, fact * LANES : fact * LANES + known] = line[fact : fact + 1, :known]
+        info_ref[row, FACTS * LANES : (FACTS + 1) * LANES] = over
+    add_facts(plan, info_ref, out_ref)
+
+
+def add_facts(plan, info_ref, out_ref):
+    size = (FACTS + 1) * LANES
+    last = iota((TILE, size), 0) == TILE - 1
+    for block in range(plan.cells):
+        end = (block + 1) * plan.slots
         tail = slice(end - TILE, end)
-        old = out_ref[tail, 0 : (FACTS + 1) * LANES].astype(F32)
-        for fact in range(FACTS):
-            lanes = slice(fact * LANES, fact * LANES + known)
-            out_ref[tail, lanes] = jnp.where(
-                last[:, :known], line[fact : fact + 1, :known], old[:, lanes]
-            ).astype(BF16)
-        lanes = slice(FACTS * LANES, (FACTS + 1) * LANES)
-        out_ref[tail, lanes] = jnp.where(last, flag, old[:, lanes]).astype(BF16)
+        out_ref[tail, 0:size] = jnp.where(
+            last, info_ref[8 + block : 9 + block, 0:size], out_ref[tail, 0:size].astype(F32)
+        ).astype(BF16)
+
+
+def relay_kernel(plan, info_ref, rows_ref, after_ref, out_ref):
+    del after_ref
+    slot = info_ref[5:6, 0 : plan.files].astype(I32)
+    match = as_bf16(iota((plan.total, plan.files), 0) == slot)
+    out_ref[...] = jnp.dot(match, rows_ref[...], preferred_element_type=F32).astype(BF16)
+    add_facts(plan, info_ref, out_ref)
 
 
 def facts_of(plan, ref):
@@ -244,16 +256,6 @@
     files, width, total = plan.files, plan.width, plan.total
     bucket = bucket.reshape(1, files)
 
-    def pack(place, rows, after=()):
-        return call(
-            functools.partial(pack_kernel, plan),
-            jax.ShapeDtypeStruct((total, width), BF16),
-            [place, rows],
-            2 * total * files * width,
-            6 * files * width,
-            after=after,
-        )
-
     other_rows = swapped(embeddings, plan.half_bit, plan)
     place = call(
         functools.partial(place_kernel, plan),
@@ -262,13 +264,29 @@
         4 * files * files,
         2 * files * width,
     )
-    other_place = swapped(place, plan.half_bit, plan)
-    payload = pack(place, embeddings)
+    payload, info = call(
+        functools.partial(pack_kernel, plan),
+        (
+            jax.ShapeDtypeStruct((total, width), BF16),
+            jax.ShapeDtypeStruct((8 + plan.cells, width), F32),
+        ),
+        [place, embeddings],
+        2 * total * files * width,
+        6 * files * width,
+    )
+    other_info = swapped(info, plan.half_bit, plan)
     own = lax.cond(
         lax.axis_index(AXES) != plan.devices, lambda payload: exchange(payload, plan), lambda payload: payload, payload
     )
     mate = swapped(own, plan.core_bit, plan)
-    relayed = pack(other_place, other_rows, (own,))
+    relayed = call(
+        functools.partial(relay_kernel, plan),
+        jax.ShapeDtypeStruct((total, width), BF16),
+        [other_info, other_rows],
+        2 * total * files * width,
+        6 * files * width,
+        after=(own,),
+    )
     half = exchange(relayed, plan)
     near = attend(plan, own, [(own, True), (mate, False)])
     mate_half = swapped(half, plan.core_bit, plan)

time: 99.5 us -> 99.3 us (level)
  no operation moved by 1% of the time
where the time goes in v7:
time: 99.3 us; the launch traced here: 98.9 us
  blocking collectives  54 us (54%)
  Pallas kernels  26.2 us (26%)
  starting transfers between devices  9.67 us (10%)
  waiting for transfers between devices  8.19 us (8%)
    all_to_all x2, blocking collectives, exchange(): lax.all_to_all(value.reshape(shape), AXES, split_axis=0, concat_axis=0, t...  54 us
    pallas_call x7, Pallas kernels, call(): pl.pallas_call(kernel, out_shape=out_shape, in_specs=[VMEM] * len(args) +...  26.2 us
    ppermute x4, starting transfers between devices, swapped(): lax.ppermute(value, AXES, [(i, i ^ bit) for i in range(plan.devices)])  5.19 us
    all_to_all x1, waiting for transfers between devices, exchange(): lax.all_to_all(value.reshape(shape), AXES, split_axis=0, concat_axis=0, t...  5.07 us
    all_to_all x1, starting transfers between devices, exchange(): lax.all_to_all(value.reshape(shape), AXES, split_axis=0, concat_axis=0, t...  4.47 us
    ppermute x4, waiting for transfers between devices, swapped(): lax.ppermute(value, AXES, [(i, i ^ bit) for i in range(plan.devices)])  3.12 us
  transfers between devices with their start and end apart: 5, of which 2 were waited for; matrix products, arithmetic and copies ran while one was open for 0% of the time, Pallas kernels for 18%

profile of v7, /device:TPU:0, one launch (start us, length us, event | category | flops | bytes accessed | tf_op | source)
XLA Modules:
  0.0 98.9 jit_solution(3019979390731875273)
XLA Ops:
  0.0 5.0 %collective-permute-start.5 = (bf16[512,768]{1,0:T(8,128)(2,1)}, bf16[512,768]{1,0:T(8,128)(2,1)S(1)}, u32[]{:S(2)}, u32[]{:S(2)}) collective-permute-start(bf16[512,768]{1,0:T(8,128)(2,1)} %rows_ref.3), channel_id=1, source_target_pairs={{0,6},{1,7},{2,4},{3,5},{4,2},{5,3},{6,0},{7,1},{8,14},{9,15},{10,... | collective-permute-start | bytes 2359304 | tf_op jit(solution)/shard_map/ppermute | solution.py:53
  5.0 1.9 %shard_map.30.place_ref = f32[8,512]{1,0:T(8,128)S(1)} custom-call(s32[1,512]{1,0:T(1,128)} %bitcast.23, bf16[512,768]{1,0:T(8,128)(2,1)} %rows_ref.3), custom_call_target="tpu_custom_call" | custom-call | flops 1048576 | bytes 786432 | tf_op jit(solution)/shard_map/pallas_call | solution.py:64
  7.0 2.3 %shard_map.31 = (bf16[896,768]{1,0:T(8,128)(2,1)S(1)}, f32[16,768]{1,0:T(8,128)S(1)}) custom-call(f32[8,512]{1,0:T(8,128)S(1)} %shard_map.30.place_ref, bf16[512,768]{1,0:T(8,128)(2,1)} %rows_ref.3), custom_call_target="tpu_custom_call" | custom-call | flops 704643072 | bytes 2359296 | tf_op jit(solution)/shard_map/pallas_call | solution.py:64
  9.3 0.1 collective-permute-start.4
  9.3 30.8 %conditional.3 = (bf16[896,768]{1,0:T(8,128)(2,1)S(1)}) conditional(s32[]{:T(128)} %convert_element_type.12, bf16[896,768]{1,0:T(8,128)(2,1)S(1)} %get-tuple-element.45, bf16[896,768]{1,0:T(8,128)(2,1)S(1)} %get-tuple-element.45), branch_computations={%region_0.0_spmd, %region_1.0_spmd} | conditional | bytes 5505032 | solution.py:278
  9.4 0.1 copy.11
  9.5 30.7 %all_to_all.25 = bf16[8,112,768]{2,1,0:T(8,128)(2,1)S(1)} all-to-all(bf16[8,112,768]{2,1,0:T(8,128)(2,1)S(1)} %copy.11), channel_id=1, replica_groups={{0,19,1,18,2,17,3,16},{6,21,7,20,4,23,5,22},{8,27,9,26,10,25,11,24},{14..., dimensions={0} | all-to-all | bytes 2752512 | tf_op jit(solution)/shard_map/cond/branch_1_fun/all_to_all | solution.py:58
  40.2 0.0 copy-start.4
  40.2 0.0 collective-permute-done.4.info_ref
  40.2 0.0 collective-permute-done.5.rows_ref
  40.2 2.0 %shard_map.32 = bf16[896,768]{1,0:T(8,128)(2,1)} custom-call(f32[16,768]{1,0:T(8,128)S(1)} %collective-permute-done.4.info_ref, bf16[512,768]{1,0:T(8,128)(2,1)S(1)} %collective-permute-done.5.rows_ref, bf16[896,768]{1,0:T(8,128)(2,1)S(1)} %get-tuple-element.57.after_ref.refs_0_.refs_1_), custom_call_target="tpu_custom_call" | custom-call | flops 704643072 | bytes 2359296 | tf_op jit(solution)/shard_map/pallas_call | solution.py:64
  42.1 4.5 %all-to-all-start.5 = ((bf16[8,112,768]{2,1,0:T(8,128)(2,1)}), bf16[8,112,768]{2,1,0:T(8,128)(2,1)}, u32[]{:S(2)}, u32[]{:S(2)}) async-start(bf16[8,112,768]{2,1,0:T(8,128)(2,1)} %bitcast.12), calls=%async_computation.5 | async-start | bytes 2752512 | tf_op jit(solution)/shard_map/all_to_all | solution.py:58
  46.6 0.0 copy-done.4
  46.6 0.1 collective-permute-start.7
  46.7 3.1 %collective-permute-done.7.refs_2_ = bf16[896,768]{1,0:T(8,128)(2,1)S(1)} collective-permute-done((bf16[896,768]{1,0:T(8,128)(2,1)S(1)}, bf16[896,768]{1,0:T(8,128)(2,1)S(1)}, u32[]{:S(2)}, u32[]{:S(2)}) %collective-permute-start.7) | collective-permute-done | bytes 1376288 | tf_op jit(solution)/shard_map/ppermute | solution.py:53
  49.8 8.8 %shard_map.33 = (f32[8,128]{1,0:T(8,128)S(1)}, f32[896,896]{1,0:T(8,128)S(1)}) custom-call(bf16[896,768]{1,0:T(8,128)(2,1)} %copy-done.4, bf16[896,768]{1,0:T(8,128)(2,1)} %copy-done.4, bf16[896,768]{1,0:T(8,128)(2,1)S(1)} %collective-permute-done.7.refs_2_), custom_call_target="tpu_custom_call" | custom-call | flops 4932501504 | bytes 8257536 | tf_op jit(solution)/shard_map/pallas_call | solution.py:64
  58.6 5.1 %all-to-all-done.5 = bf16[8,112,768]{2,1,0:T(8,128)(2,1)} async-done(((bf16[8,112,768]{2,1,0:T(8,128)(2,1)}), bf16[8,112,768]{2,1,0:T(8,128)(2,1)}, u32[]{:S(2)}, u32[]{:S(2)}) %all-to-all-start.5) | async-done | bytes 1376288 | tf_op jit(solution)/shard_map/all_to_all | solution.py:58
  63.7 0.0 copy-start.5
  63.7 0.0 collective-permute-start.6
  63.7 5.3 %shard_map.34 = (f32[8,128]{1,0:T(8,128)S(1)}, f32[896,896]{1,0:T(8,128)S(1)}) custom-call(bf16[896,768]{1,0:T(8,128)(2,1)} %copy-done.4, bf16[896,768]{1,0:T(8,128)(2,1)} %bitcast.13.refs_1_), custom_call_target="tpu_custom_call" | custom-call | flops 98650030080 | bytes 8257536 | tf_op jit(solution)/shard_map/pallas_call | solution.py:64
  68.9 0.0 collective-permute-done.6.refs_1_
  69.0 0.0 copy-done.5
  69.0 0.0 copy-start.6
  69.0 3.8 %shard_map.35 = (s32[1]{0:T(128)}, bf16[896,768]{1,0:T(8,128)(2,1)S(1)}) custom-call(bf16[896,768]{1,0:T(8,128)(2,1)S(1)} %copy-done.5, bf16[896,768]{1,0:T(8,128)(2,1)S(1)} %collective-permute-done.6.refs_1_, f32[8,128]{1,0:T(8,128)S(1)} %get-tuple-element.47.refs_2_, f32[896,896]{1,0:T(8,128)S(1)} %get-tuple-element.48.refs_3_, ...), custom_call_target="tpu_custom_call" | custom-call | flops 2466250752 | bytes 8257536 | tf_op jit(solution)/shard_map/pallas_call | solution.py:64
  73.4 0.0 copy-done.6
  73.4 25.5 %conditional.4 = (bf16[512,768]{1,0:T(8,128)(2,1)}) conditional(s32[]{:T(128)} %bitcast.14, (bf16[896,768]{1,0:T(8,128)(2,1)S(1)}, f32[8,512]{1,0:T(8,128)S(1)}) %tuple.23, (s32[512]{0:T(512)S(1)}, bf16[512,768]{1,0:T(8,128)(2,1)}) %tuple.33), branch_computations={%region_2.0_spmd, %region_3.0_spmd} | conditional | flops 178024087552 | bytes 106299800 | solution.py:322
  73.4 23.3 %all_to_all.26 = bf16[8,112,768]{2,1,0:T(8,128)(2,1)S(1)} all-to-all(bf16[8,112,768]{2,1,0:T(8,128)(2,1)S(1)} %bitcast.22), channel_id=1, replica_groups={{0,19,1,18,2,17,3,16},{6,21,7,20,4,23,5,22},{8,27,9,26,10,25,11,24},{14..., dimensions={0} | all-to-all | bytes 2752512 | tf_op jit(solution)/shard_map/cond/branch_0_fun/all_to_all | solution.py:58
  96.7 2.2 %branch_0_fun.1 = bf16[512,768]{1,0:T(8,128)(2,1)} custom-call(f32[8,512]{1,0:T(8,128)S(1)} %get-tuple-element.26.place_ref, bf16[896,768]{1,0:T(8,128)(2,1)S(1)} %bitcast.17), custom_call_target="tpu_custom_call" | custom-call | flops 704643072 | bytes 2359296 | tf_op jit(solution)/shard_map/cond/branch_0_fun/pallas_call | solution.py:64
Async XLA Ops:
  0.0 40.2 %collective-permute-start.5 = (bf16[512,768]{1,0:T(8,128)(2,1)}, bf16[512,768]{1,0:T(8,128)(2,1)S(1)}, u32[]{:S(2)}, u32[]{:S(2)}) collective-permute-start(bf16[512,768]{1,0:T(8,128)(2,1)} %rows_ref.3), channel_id=1, source_target_pairs={{0,6},{1,7},{2,4},{3,5},{4,2},{5,3},{6,0},{7,1},{8,14},{9,15},{10,... | collective-permute-start | bytes 2359304 | tf_op jit(solution)/shard_map/ppermute | solution.py:53
  9.3 30.9 %collective-permute-start.4 = (f32[16,768]{1,0:T(8,128)S(1)}, f32[16,768]{1,0:T(8,128)S(1)}, u32[]{:S(2)}, u32[]{:S(2)}) collective-permute-start(f32[16,768]{1,0:T(8,128)S(1)} %get-tuple-element.46), channel_id=1, source_target_pairs={{0,6},{1,7},{2,4},{3,5},{4,2},{5,3},{6,0},{7,1},{8,14},{9,15},{10,... | collective-permute-start | bytes 147464 | tf_op jit(solution)/shard_map/ppermute | solution.py:53
  40.2 6.5 %copy-start.4 = (bf16[896,768]{1,0:T(8,128)(2,1)}, bf16[896,768]{1,0:T(8,128)(2,1)S(1)}, u32[]{:S(2)}) copy-start(bf16[896,768]{1,0:T(8,128)(2,1)S(1)} %get-tuple-element.57.after_ref.refs_0_.refs_1_) | copy-start | bytes 4128772
  42.1 21.5 %all-to-all-start.5 = ((bf16[8,112,768]{2,1,0:T(8,128)(2,1)}), bf16[8,112,768]{2,1,0:T(8,128)(2,1)}, u32[]{:S(2)}, u32[]{:S(2)}) async-start(bf16[8,112,768]{2,1,0:T(8,128)(2,1)} %bitcast.12), calls=%async_computation.5 | async-start | bytes 2752512 | tf_op jit(solution)/shard_map/all_to_all | solution.py:58
  46.6 3.2 %collective-permute-start.7 = (bf16[896,768]{1,0:T(8,128)(2,1)S(1)}, bf16[896,768]{1,0:T(8,128)(2,1)S(1)}, u32[]{:S(2)}, u32[]{:S(2)}) collective-permute-start(bf16[896,768]{1,0:T(8,128)(2,1)S(1)} %get-tuple-element.57.after_ref.refs_0_.refs_1_), channel_id=1, source_target_pairs={{0,8},{1,9},{2,10},{3,11},{4,12},{5,13},{6,14},{7,15},{8,0},{9,1},... | collective-permute-start | bytes 4128776 | tf_op jit(solution)/shard_map/ppermute | solution.py:53
  63.7 5.3 %copy-start.5 = (bf16[896,768]{1,0:T(8,128)(2,1)S(1)}, bf16[896,768]{1,0:T(8,128)(2,1)}, u32[]{:S(2)}) copy-start(bf16[896,768]{1,0:T(8,128)(2,1)} %copy-done.4) | copy-start | bytes 4128772
  63.7 5.3 %collective-permute-start.6 = (bf16[896,768]{1,0:T(8,128)(2,1)}, bf16[896,768]{1,0:T(8,128)(2,1)S(1)}, u32[]{:S(2)}, u32[]{:S(2)}) collective-permute-start(bf16[896,768]{1,0:T(8,128)(2,1)} %bitcast.13.refs_1_), channel_id=1, source_target_pairs={{0,8},{1,9},{2,10},{3,11},{4,12},{5,13},{6,14},{7,15},{8,0},{9,1},... | collective-permute-start | bytes 4128776 | tf_op jit(solution)/shard_map/ppermute | solution.py:53
  69.0 4.5 %copy-start.6 = (s32[512]{0:T(512)S(1)}, s32[512]{0:T(512)}, u32[]{:S(2)}) copy-start(s32[512]{0:T(512)} %param.9) | copy-start | bytes 6148

commit v8 on v7

--- a/solution.py
+++ b/solution.py
@@ -181,7 +181,8 @@
     old_refs = refs[: 2 * olds]
     over_ref, out_ref, column_ref = refs[2 * olds :]
     total, width = plan.total, plan.width
-    chunk = total // 2
+    steps = 1 if total <= 1024 else 2
+    chunk = total // steps
     tag, inv, over = facts_of(plan, query_ref)
     for old_over_ref in old_refs[0::2]:
         over = jnp.maximum(over, old_over_ref[0:1, :])
@@ -199,7 +200,7 @@
         over_ref[0] = jnp.max(over).astype(I32)
     else:
         over_ref[...] = jnp.broadcast_to(over, over_ref.shape)
-    for step in range(2):
+    for step in range(steps):
         here = slice(step * chunk, (step + 1) * chunk)
         query = query_ref[here, :]
         query_inv = column_ref[0, here, :][:, 0:1]

time: 99.3 us -> 99.2 us (level)
  transfers between devices with their start and end apart: 5 -> 5, of which waited for: 2 -> 2; matrix products, arithmetic and copies ran while one was open for 0% -> 0% of each run, Pallas kernels for 18% -> 19%
where the time goes in v8:
time: 99.2 us; the launch traced here: 98.8 us
  blocking collectives  54 us (54%)
  Pallas kernels  26.6 us (27%)
  starting transfers between devices  9.67 us (10%)
  waiting for transfers between devices  7.73 us (8%)
    all_to_all x2, blocking collectives, exchange(): lax.all_to_all(value.reshape(shape), AXES, split_axis=0, concat_axis=0, t...  54 us
    pallas_call x7, Pallas kernels, call(): pl.pallas_call(kernel, out_shape=out_shape, in_specs=[VMEM] * len(args) +...  26.6 us
    ppermute x4, starting transfers between devices, swapped(): lax.ppermute(value, AXES, [(i, i ^ bit) for i in range(plan.devices)])  5.19 us
    all_to_all x1, waiting for transfers between devices, exchange(): lax.all_to_all(value.reshape(shape), AXES, split_axis=0, concat_axis=0, t...  4.61 us
    all_to_all x1, starting transfers between devices, exchange(): lax.all_to_all(value.reshape(shape), AXES, split_axis=0, concat_axis=0, t...  4.47 us
    ppermute x4, waiting for transfers between devices, swapped(): lax.ppermute(value, AXES, [(i, i ^ bit) for i in range(plan.devices)])  3.12 us
  transfers between devices with their start and end apart: 5, of which 2 were waited for; matrix products, arithmetic and copies ran while one was open for 0% of the time, Pallas kernels for 19%

profile of v8, /device:TPU:0, one launch (start us, length us, event | category | flops | bytes accessed | tf_op | source)
XLA Modules:
  0.0 98.8 jit_solution(8670799049625829622)
XLA Ops:
  0.0 5.0 %collective-permute-start.5 = (bf16[512,768]{1,0:T(8,128)(2,1)}, bf16[512,768]{1,0:T(8,128)(2,1)S(1)}, u32[]{:S(2)}, u32[]{:S(2)}) collective-permute-start(bf16[512,768]{1,0:T(8,128)(2,1)} %rows_ref.3), channel_id=1, source_target_pairs={{0,6},{1,7},{2,4},{3,5},{4,2},{5,3},{6,0},{7,1},{8,14},{9,15},{10,... | collective-permute-start | bytes 2359304 | tf_op jit(solution)/shard_map/ppermute | solution.py:53
  5.0 1.9 %shard_map.30.place_ref = f32[8,512]{1,0:T(8,128)S(1)} custom-call(s32[1,512]{1,0:T(1,128)} %bitcast.23, bf16[512,768]{1,0:T(8,128)(2,1)} %rows_ref.3), custom_call_target="tpu_custom_call" | custom-call | flops 1048576 | bytes 786432 | tf_op jit(solution)/shard_map/pallas_call | solution.py:64
  7.0 2.3 %shard_map.31 = (bf16[896,768]{1,0:T(8,128)(2,1)S(1)}, f32[16,768]{1,0:T(8,128)S(1)}) custom-call(f32[8,512]{1,0:T(8,128)S(1)} %shard_map.30.place_ref, bf16[512,768]{1,0:T(8,128)(2,1)} %rows_ref.3), custom_call_target="tpu_custom_call" | custom-call | flops 704643072 | bytes 2359296 | tf_op jit(solution)/shard_map/pallas_call | solution.py:64
  9.3 0.1 collective-permute-start.4
  9.3 30.8 %conditional.3 = (bf16[896,768]{1,0:T(8,128)(2,1)S(1)}) conditional(s32[]{:T(128)} %convert_element_type.12, bf16[896,768]{1,0:T(8,128)(2,1)S(1)} %get-tuple-element.45, bf16[896,768]{1,0:T(8,128)(2,1)S(1)} %get-tuple-element.45), branch_computations={%region_0.0_spmd, %region_1.0_spmd} | conditional | bytes 5505032 | solution.py:279
  9.4 0.1 copy.11
  9.5 30.7 %all_to_all.25 = bf16[8,112,768]{2,1,0:T(8,128)(2,1)S(1)} all-to-all(bf16[8,112,768]{2,1,0:T(8,128)(2,1)S(1)} %copy.11), channel_id=1, replica_groups={{0,19,1,18,2,17,3,16},{6,21,7,20,4,23,5,22},{8,27,9,26,10,25,11,24},{14..., dimensions={0} | all-to-all | bytes 2752512 | tf_op jit(solution)/shard_map/cond/branch_1_fun/all_to_all | solution.py:58
  40.2 0.0 copy-start.4
  40.2 0.0 collective-permute-done.4.info_ref
  40.2 0.0 collective-permute-done.5.rows_ref
  40.2 2.0 %shard_map.32 = bf16[896,768]{1,0:T(8,128)(2,1)} custom-call(f32[16,768]{1,0:T(8,128)S(1)} %collective-permute-done.4.info_ref, bf16[512,768]{1,0:T(8,128)(2,1)S(1)} %collective-permute-done.5.rows_ref, bf16[896,768]{1,0:T(8,128)(2,1)S(1)} %get-tuple-element.57.after_ref.refs_0_.refs_1_), custom_call_target="tpu_custom_call" | custom-call | flops 704643072 | bytes 2359296 | tf_op jit(solution)/shard_map/pallas_call | solution.py:64
  42.1 4.5 %all-to-all-start.5 = ((bf16[8,112,768]{2,1,0:T(8,128)(2,1)}), bf16[8,112,768]{2,1,0:T(8,128)(2,1)}, u32[]{:S(2)}, u32[]{:S(2)}) async-start(bf16[8,112,768]{2,1,0:T(8,128)(2,1)} %bitcast.12), calls=%async_computation.5 | async-start | bytes 2752512 | tf_op jit(solution)/shard_map/all_to_all | solution.py:58
  46.6 0.0 copy-done.4
  46.6 0.1 collective-permute-start.7
  46.7 3.1 %collective-permute-done.7.refs_2_ = bf16[896,768]{1,0:T(8,128)(2,1)S(1)} collective-permute-done((bf16[896,768]{1,0:T(8,128)(2,1)S(1)}, bf16[896,768]{1,0:T(8,128)(2,1)S(1)}, u32[]{:S(2)}, u32[]{:S(2)}) %collective-permute-start.7) | collective-permute-done | bytes 1376288 | tf_op jit(solution)/shard_map/ppermute | solution.py:53
  49.8 9.3 %shard_map.33 = (f32[8,128]{1,0:T(8,128)S(1)}, f32[896,896]{1,0:T(8,128)S(1)}) custom-call(bf16[896,768]{1,0:T(8,128)(2,1)} %copy-done.4, bf16[896,768]{1,0:T(8,128)(2,1)} %copy-done.4, bf16[896,768]{1,0:T(8,128)(2,1)S(1)} %collective-permute-done.7.refs_2_), custom_call_target="tpu_custom_call" | custom-call | flops 4932501504 | bytes 8257536 | tf_op jit(solution)/shard_map/pallas_call | solution.py:64
  59.1 4.6 %all-to-all-done.5 = bf16[8,112,768]{2,1,0:T(8,128)(2,1)} async-done(((bf16[8,112,768]{2,1,0:T(8,128)(2,1)}), bf16[8,112,768]{2,1,0:T(8,128)(2,1)}, u32[]{:S(2)}, u32[]{:S(2)}) %all-to-all-start.5) | async-done | bytes 1376288 | tf_op jit(solution)/shard_map/all_to_all | solution.py:58
  63.7 0.0 copy-start.5
  63.7 0.0 collective-permute-start.6
  63.7 5.2 %shard_map.34 = (f32[8,128]{1,0:T(8,128)S(1)}, f32[896,896]{1,0:T(8,128)S(1)}) custom-call(bf16[896,768]{1,0:T(8,128)(2,1)} %copy-done.4, bf16[896,768]{1,0:T(8,128)(2,1)} %bitcast.13.refs_1_), custom_call_target="tpu_custom_call" | custom-call | flops 98650030080 | bytes 8257536 | tf_op jit(solution)/shard_map/pallas_call | solution.py:64
  68.9 0.0 collective-permute-done.6.refs_1_
  68.9 0.0 copy-done.5
  68.9 0.0 copy-start.6
  68.9 3.8 %shard_map.35 = (s32[1]{0:T(128)}, bf16[896,768]{1,0:T(8,128)(2,1)S(1)}) custom-call(bf16[896,768]{1,0:T(8,128)(2,1)S(1)} %copy-done.5, bf16[896,768]{1,0:T(8,128)(2,1)S(1)} %collective-permute-done.6.refs_1_, f32[8,128]{1,0:T(8,128)S(1)} %get-tuple-element.47.refs_2_, f32[896,896]{1,0:T(8,128)S(1)} %get-tuple-element.48.refs_3_, ...), custom_call_target="tpu_custom_call" | custom-call | flops 2466250752 | bytes 8257536 | tf_op jit(solution)/shard_map/pallas_call | solution.py:64
  73.4 0.0 copy-done.6
  73.4 25.5 %conditional.4 = (bf16[512,768]{1,0:T(8,128)(2,1)}) conditional(s32[]{:T(128)} %bitcast.14, (bf16[896,768]{1,0:T(8,128)(2,1)S(1)}, f32[8,512]{1,0:T(8,128)S(1)}) %tuple.23, (s32[512]{0:T(512)S(1)}, bf16[512,768]{1,0:T(8,128)(2,1)}) %tuple.33), branch_computations={%region_2.0_spmd, %region_3.0_spmd} | conditional | flops 178024087552 | bytes 106299800 | solution.py:323
  73.4 23.3 %all_to_all.26 = bf16[8,112,768]{2,1,0:T(8,128)(2,1)S(1)} all-to-all(bf16[8,112,768]{2,1,0:T(8,128)(2,1)S(1)} %bitcast.22), channel_id=1, replica_groups={{0,19,1,18,2,17,3,16},{6,21,7,20,4,23,5,22},{8,27,9,26,10,25,11,24},{14..., dimensions={0} | all-to-all | bytes 2752512 | tf_op jit(solution)/shard_map/cond/branch_0_fun/all_to_all | solution.py:58
  96.7 2.2 %branch_0_fun.1 = bf16[512,768]{1,0:T(8,128)(2,1)} custom-call(f32[8,512]{1,0:T(8,128)S(1)} %get-tuple-element.26.place_ref, bf16[896,768]{1,0:T(8,128)(2,1)S(1)} %bitcast.17), custom_call_target="tpu_custom_call" | custom-call | flops 704643072 | bytes 2359296 | tf_op jit(solution)/shard_map/cond/branch_0_fun/pallas_call | solution.py:64
Async XLA Ops:
  0.0 40.2 %collective-permute-start.5 = (bf16[512,768]{1,0:T(8,128)(2,1)}, bf16[512,768]{1,0:T(8,128)(2,1)S(1)}, u32[]{:S(2)}, u32[]{:S(2)}) collective-permute-start(bf16[512,768]{1,0:T(8,128)(2,1)} %rows_ref.3), channel_id=1, source_target_pairs={{0,6},{1,7},{2,4},{3,5},{4,2},{5,3},{6,0},{7,1},{8,14},{9,15},{10,... | collective-permute-start | bytes 2359304 | tf_op jit(solution)/shard_map/ppermute | solution.py:53
  9.3 30.9 %collective-permute-start.4 = (f32[16,768]{1,0:T(8,128)S(1)}, f32[16,768]{1,0:T(8,128)S(1)}, u32[]{:S(2)}, u32[]{:S(2)}) collective-permute-start(f32[16,768]{1,0:T(8,128)S(1)} %get-tuple-element.46), channel_id=1, source_target_pairs={{0,6},{1,7},{2,4},{3,5},{4,2},{5,3},{6,0},{7,1},{8,14},{9,15},{10,... | collective-permute-start | bytes 147464 | tf_op jit(solution)/shard_map/ppermute | solution.py:53
  40.2 6.5 %copy-start.4 = (bf16[896,768]{1,0:T(8,128)(2,1)}, bf16[896,768]{1,0:T(8,128)(2,1)S(1)}, u32[]{:S(2)}) copy-start(bf16[896,768]{1,0:T(8,128)(2,1)S(1)} %get-tuple-element.57.after_ref.refs_0_.refs_1_) | copy-start | bytes 4128772
  42.1 21.5 %all-to-all-start.5 = ((bf16[8,112,768]{2,1,0:T(8,128)(2,1)}), bf16[8,112,768]{2,1,0:T(8,128)(2,1)}, u32[]{:S(2)}, u32[]{:S(2)}) async-start(bf16[8,112,768]{2,1,0:T(8,128)(2,1)} %bitcast.12), calls=%async_computation.5 | async-start | bytes 2752512 | tf_op jit(solution)/shard_map/all_to_all | solution.py:58
  46.6 3.2 %collective-permute-start.7 = (bf16[896,768]{1,0:T(8,128)(2,1)S(1)}, bf16[896,768]{1,0:T(8,128)(2,1)S(1)}, u32[]{:S(2)}, u32[]{:S(2)}) collective-permute-start(bf16[896,768]{1,0:T(8,128)(2,1)S(1)} %get-tuple-element.57.after_ref.refs_0_.refs_1_), channel_id=1, source_target_pairs={{0,8},{1,9},{2,10},{3,11},{4,12},{5,13},{6,14},{7,15},{8,0},{9,1},... | collective-permute-start | bytes 4128776 | tf_op jit(solution)/shard_map/ppermute | solution.py:53
  63.7 5.2 %copy-start.5 = (bf16[896,768]{1,0:T(8,128)(2,1)S(1)}, bf16[896,768]{1,0:T(8,128)(2,1)}, u32[]{:S(2)}) copy-start(bf16[896,768]{1,0:T(8,128)(2,1)} %copy-done.4) | copy-start | bytes 4128772
  63.7 5.2 %collective-permute-start.6 = (bf16[896,768]{1,0:T(8,128)(2,1)}, bf16[896,768]{1,0:T(8,128)(2,1)S(1)}, u32[]{:S(2)}, u32[]{:S(2)}) collective-permute-start(bf16[896,768]{1,0:T(8,128)(2,1)} %bitcast.13.refs_1_), channel_id=1, source_target_pairs={{0,8},{1,9},{2,10},{3,11},{4,12},{5,13},{6,14},{7,15},{8,0},{9,1},... | collective-permute-start | bytes 4128776 | tf_op jit(solution)/shard_map/ppermute | solution.py:53
  68.9 4.4 %copy-start.6 = (s32[512]{0:T(512)S(1)}, s32[512]{0:T(512)}, u32[]{:S(2)}) copy-start(s32[512]{0:T(512)} %param.9) | copy-start | bytes 6148
